TPU v7x, 1024 devices: a whole 4x8x16 slice. The times are simulated.
1024 devices in a mesh: dp: 64 (over y, z_lo, core), slot: 4 (over z_hi), grp: 4 (over x).
Axes of the slice: x: 4, y: 8, z: 16 (z_hi: 4, z_lo: 4; z = z_hi * 4 + z_lo), core: 2. Of those that a mesh axis runs over, the one named last changes fastest.
Arguments:
- pooled: bfloat16 [2048, 512, 128], P(('dp', 'grp'), 'slot'), may hold values from -6 to 6
- cotangent: bfloat16 [2048, 512, 128], P(('dp', 'grp'), 'slot'), may hold values from -6 to 6
- compress_weight: bfloat16 [2, 512, 512], replicated, may hold values from -0.25 to 0.25
- fm_basis: bfloat16 [2, 512, 32], replicated, may hold values from -0.25 to 0.25
- fm_output: bfloat16 [2, 32, 128], replicated, may hold values from -0.09375 to 0.09375
- norm_gain: float32 [2, 128], replicated, may hold values from 0.5 to 1.5
- bag_ids: int32 [2048, 512, 8], P(('dp', 'grp'), 'slot'), may hold values from 0 to 4095
- bag_lengths: int32 [2048, 512], P(('dp', 'grp'), 'slot'), may hold values from 1 to 8
- slot_table: int32 [512], P('slot'), may hold values from 0 to 127, as said below
- table_home: int32 [128], replicated, may hold values from 0 to 127, as said below
Outputs:
- table_grad: float32 [128, 4096, 128], P('dp', ('slot', 'grp'))
Inputs may be any that keep to these rules, and one draw needn't show every extreme that they name: `slot_table`: within each aligned block of 128 slots, at most 4 slots use tables whose table_home lies in one aligned block of 2 positions, and in every block of slots some block of positions takes exactly 4. `table_home`: A permutation: each position holds one table.
All inputs are finite; a program needn't handle non-finite values.
Results may differ from a plain program's by a relative error of at most 0.024.
Values may be sent and summed in bfloat16 or wider, within the bound.
No kernel may reach another device: no remote copies, remote signals or barrier semaphores. Data moves between devices by JAX's collectives and lax.ppermute only.
A program may use at most 64 MiB of HBM per device.

v0:
```python
import jax
import jax.numpy as jnp
from jax import lax
from jax.sharding import PartitionSpec as P

D = 128
LAYERS = 2
ROWS = 4096
TABLE_DEV = 2


norm_eps = 1e-05


def collect(values):
    return lax.all_gather(values, "slot", axis=1, tiled=True)


def norm_rows(total_sum):
    mean_value = jnp.mean(total_sum, axis=-1, keepdims=True)
    centered = total_sum - mean_value
    variance = jnp.mean(centered * centered, axis=-1, keepdims=True)
    inv_std = lax.rsqrt(variance + norm_eps)
    return (centered * inv_std, inv_std)


def forward_rows(gathered, first_row, amount, compress, basis_map, output_map, gain_row):
    inputs = lax.dynamic_slice_in_dim(gathered, first_row, amount, 1)
    coefficient = jnp.einsum(
        "bnd,nk->bdk", gathered, basis_map, preferred_element_type=jnp.float32
    ).astype(jnp.bfloat16)
    feature = jnp.einsum(
        "bsd,bdk->bsk", inputs, coefficient, preferred_element_type=jnp.float32
    ).astype(jnp.bfloat16)
    mix_rows = lax.dynamic_slice_in_dim(compress, first_row, amount, 0)
    mixed_rows = jnp.einsum("sn,bnd->bsd", mix_rows, gathered, preferred_element_type=jnp.float32)
    total_sum = (
        inputs.astype(jnp.float32)
        + jnp.einsum("bsk,kd->bsd", feature, output_map, preferred_element_type=jnp.float32)
        + mixed_rows
    )
    normed, inv_std = norm_rows(total_sum)
    return ((normed * gain_row).astype(jnp.bfloat16), normed, inv_std, coefficient, inputs)


def backward_rows(
    upstream,
    normed,
    inv_std,
    coefficient,
    inputs,
    compress,
    basis_map,
    output_map,
    gain_row,
    own_first,
):
    scaled = upstream.astype(jnp.float32) * gain_row
    grad_sum = inv_std * (
        scaled
        - jnp.mean(scaled, axis=-1, keepdims=True)
        - normed * jnp.mean(scaled * normed, axis=-1, keepdims=True)
    )
    grad_low = grad_sum.astype(jnp.bfloat16)
    grad_feat = jnp.einsum(
        "bsd,kd->bsk", grad_low, output_map, preferred_element_type=jnp.float32
    ).astype(jnp.bfloat16)
    local_part = grad_sum + jnp.einsum(
        "bsk,bdk->bsd", grad_feat, coefficient, preferred_element_type=jnp.float32
    )
    grad_coeff = jnp.einsum("bsd,bsk->bdk", inputs, grad_feat, preferred_element_type=jnp.float32)
    basis_wide = basis_map.astype(jnp.float32)
    amount = inputs.shape[1]
    columns = lax.dynamic_slice(compress, (own_first, 0), (amount, lax.axis_size("slot") * amount))
    linear = jnp.einsum("sn,bsd->nbd", columns, grad_low, preferred_element_type=jnp.float32)
    summed = lax.psum_scatter(
        (
            linear
            + jnp.einsum(
                "nk,bdk->nbd",
                basis_wide,
                grad_coeff,
                precision=lax.Precision.HIGHEST,
                preferred_element_type=jnp.float32,
            )
        ).astype(jnp.bfloat16),
        "slot",
        scatter_dimension=0,
        tiled=True,
    ).astype(jnp.float32)
    return (local_part + jnp.transpose(summed, (1, 0, 2))).astype(jnp.bfloat16)


def add_bags(totals, grads, keys_in, lengths, block_id, block_rows):
    bag_size = keys_in.shape[-1]
    width = grads.shape[-1]
    flat_grads = grads.reshape(-1, width).astype(jnp.float32)
    flat_keys = keys_in.reshape(-1, bag_size)
    flat_lengths = lengths.reshape(-1)
    table_part = flat_keys // ROWS
    row_part = flat_keys % ROWS - block_id * block_rows
    is_live = (
        (jnp.arange(bag_size, dtype=jnp.int32)[None, :] < flat_lengths[:, None])
        & (row_part >= 0)
        & (row_part < block_rows)
    )
    target = jnp.where(is_live, table_part * block_rows + row_part, totals.shape[0])
    values = jnp.broadcast_to(flat_grads[:, None, :], (flat_grads.shape[0], bag_size, width))
    return totals.at[target.reshape(-1)].add(values.reshape(-1, width), mode="drop")


def per_device(
    pooled,
    cotangent,
    compress_weight,
    fm_basis,
    fm_output,
    norm_gain,
    bag_ids,
    bag_lengths,
    slot_table,
    table_home,
):
    slot_count = pooled.shape[1]
    sample_count = pooled.shape[0]
    own_first = lax.axis_index("slot") * slot_count
    gathered = collect(pooled)
    saved_rows = []
    for layer_id in range(LAYERS):
        result, normed, inv_std, coefficient, inputs = forward_rows(
            gathered,
            own_first,
            slot_count,
            compress_weight[layer_id],
            fm_basis[layer_id],
            fm_output[layer_id],
            norm_gain[layer_id],
        )
        if layer_id < LAYERS - 1:
            gathered = collect(result)
        saved_rows.append((normed, inv_std, coefficient, inputs))
    upstream = cotangent
    for layer_id in reversed(range(LAYERS)):
        normed, inv_std, coefficient, inputs = saved_rows[layer_id]
        upstream = backward_rows(
            upstream,
            normed,
            inv_std,
            coefficient,
            inputs,
            compress_weight[layer_id],
            fm_basis[layer_id],
            fm_output[layer_id],
            norm_gain[layer_id],
            own_first,
        )
    dp_size = lax.axis_size("dp")
    capacity = max(2, 2 * slot_count // dp_size)
    table_count = table_home.shape[0]
    bag_size = bag_ids.shape[2]
    matches = slot_table[:, None] == jnp.arange(table_count, dtype=jnp.int32)[None, :]
    position = jnp.sum(jnp.where(matches, table_home[None, :], 0), axis=1)
    owner_id = position // TABLE_DEV
    table_local = position % TABLE_DEV
    owner_hits = (owner_id[:, None] == jnp.arange(dp_size, dtype=jnp.int32)[None, :]).astype(
        jnp.int32
    )
    earlier = jnp.cumsum(owner_hits, axis=0) - owner_hits
    rank_slot = jnp.sum(earlier * owner_hits, axis=1)
    target_slot = owner_id * capacity + rank_slot
    buffer_size = dp_size * capacity
    placing = (target_slot[None, :] == jnp.arange(buffer_size, dtype=jnp.int32)[:, None]).astype(
        jnp.bfloat16
    )
    sent_grads = (
        jnp.einsum("cs,bsd->cbd", placing, upstream, preferred_element_type=jnp.float32)
        .astype(jnp.bfloat16)
        .reshape(dp_size, capacity, sample_count, D)
    )
    row_keys = bag_ids + (table_local * ROWS)[None, :, None]
    sent_keys = (
        jnp.zeros((buffer_size, sample_count, bag_size), jnp.int32)
        .at[target_slot]
        .set(jnp.transpose(row_keys, (1, 0, 2)))
        .reshape(dp_size, capacity, sample_count, bag_size)
    )
    sent_lengths = (
        jnp.zeros((buffer_size, sample_count), jnp.int32)
        .at[target_slot]
        .set(jnp.transpose(bag_lengths, (1, 0)))
        .reshape(dp_size, capacity, sample_count)
    )
    got_grads, got_keys, got_lengths = (
        lax.all_to_all(sent_grads, "dp", split_axis=0, concat_axis=0, tiled=True),
        lax.all_to_all(sent_keys, "dp", split_axis=0, concat_axis=0, tiled=True),
        lax.all_to_all(sent_lengths, "dp", split_axis=0, concat_axis=0, tiled=True),
    )
    totals = add_bags(
        jnp.zeros((TABLE_DEV * ROWS, D), jnp.float32), got_grads, got_keys, got_lengths, 0, ROWS
    )
    return lax.psum_scatter(
        totals.reshape(TABLE_DEV, ROWS, D).astype(jnp.bfloat16),
        ("slot", "grp"),
        scatter_dimension=1,
        tiled=True,
    ).astype(jnp.float32)


def solution(mesh):
    in_specs = (
        P(("dp", "grp"), "slot", None),
        P(("dp", "grp"), "slot", None),
        P(),
        P(),
        P(),
        P(),
        P(("dp", "grp"), "slot", None),
        P(("dp", "grp"), "slot"),
        P("slot"),
        P(),
    )
    out_specs = P("dp", ("slot", "grp"), None)
    return jax.shard_map(
        per_device, mesh=mesh, in_specs=in_specs, out_specs=out_specs, check_vma=False
    )
```

profile of v0, /device:TPU:1, one launch (start us, length us, event | category | flops | bytes accessed | tf_op | source)
XLA Modules:
  0.0 535.0 jit_solution(16083674662758673920)
XLA Ops:
  8.6 2.1 fusion.74
  10.7 72.7 %all-gather.3.cloned.1.call-done = bf16[8,512,128]{2,1,0:T(8,128)(2,1)} async-done(((bf16[8,128,128]{2,1,0:T(8,128)(2,1)}), bf16[8,512,128]{2,1,0:T(8,128)(2,1)}) %all-gather.3.cloned.1.call-update) | async-done | bytes 1048592 | tf_op jit(solution)/shard_map/all_gather | solution.py:16
  83.5 1.6 copy.37
  87.0 1.7 multiply_convert_fusion
  88.7 58.6 %all-gather.5.cloned.1.call-done = bf16[8,512,128]{2,1,0:T(8,128)(2,1)} async-done(((bf16[8,128,128]{2,1,0:T(8,128)(2,1)}), bf16[8,512,128]{2,1,0:T(8,128)(2,1)}) %all-gather.5.cloned.1.call-update) | async-done | bytes 1048592 | tf_op jit(solution)/shard_map/all_gather | solution.py:16
  147.3 1.5 convolution_convert_fusion.1
  148.8 1.5 convolution_add_fusion.2
  150.4 1.7 fusion.78
  158.6 2.1 fusion.4
  160.8 55.7 %reduce-scatter.4.cloned.1.call-done = bf16[128,8,128]{2,0,1:T(8,128)(2,1)} async-done(((bf16[512,8,128]{2,0,1:T(8,128)(2,1)}), bf16[128,8,128]{2,0,1:T(8,128)(2,1)}) %reduce-scatter.4.cloned.1.call-update) | async-done | bytes 262160 | tf_op jit(solution)/shard_map/reduce_scatter | solution.py:76
  216.5 2.4 fusion.73
  221.1 2.1 fusion.3
  225.5 9.4 %all-to-all-start = ((s32[64,4,8]{2,1,0:T(4,128)}), s32[64,4,8]{2,1,0:T(4,128)S(1)}, u32[]{:S(2)}, u32[]{:S(2)}) async-start(s32[64,4,8]{2,1,0:T(4,128)} %bitcast.4), calls=%async_computation | async-start | bytes 262144 | tf_op jit(solution)/shard_map/all_to_all | solution.py:196
  235.3 4.4 scatter_fusion
  240.8 5.0 all-to-all-done
  245.7 5.8 %all-to-all-start.1 = ((s32[64,1,256]{2,1,0:T(1,128)}), s32[64,1,256]{2,1,0:T(1,128)S(1)}, u32[]{:S(2)}, u32[]{:S(2)}) async-start(s32[64,1,256]{2,1,0:T(1,128)} %reshape.368), calls=%async_computation.1 | async-start | bytes 131072 | tf_op jit(solution)/shard_map/all_to_all | solution.py:195
  252.6 14.7 %all-to-all-done.1 = s32[64,1,256]{2,1,0:T(1,128)S(1)} async-done(((s32[64,1,256]{2,1,0:T(1,128)}), s32[64,1,256]{2,1,0:T(1,128)S(1)}, u32[]{:S(2)}, u32[]{:S(2)}) %all-to-all-start.1) | async-done | bytes 65568 | tf_op jit(solution)/shard_map/all_to_all | solution.py:195
  269.7 9.5 %reduce-scatter.6.cloned.1.call-done = bf16[128,8,128]{2,0,1:T(8,128)(2,1)} async-done(((bf16[512,8,128]{2,0,1:T(8,128)(2,1)}), bf16[128,8,128]{2,0,1:T(8,128)(2,1)}) %reduce-scatter.6.cloned.1.call-update) | async-done | bytes 262160 | tf_op jit(solution)/shard_map/reduce_scatter | solution.py:76
  282.1 13.0 %all-to-all-start.2 = ((bf16[64,4,8,128]{3,2,1,0:T(8,128)(2,1)}), bf16[64,4,8,128]{3,2,1,0:T(8,128)(2,1)S(1)}, u32[]{:S(2)}, u32[]{:S(2)}) async-start(bf16[64,4,8,128]{3,2,1,0:T(8,128)(2,1)} %copy.47), calls=%async_computation.4 | async-start | bytes 1048576 | tf_op jit(solution)/shard_map/all_to_all | solution.py:194
  295.9 17.7 %all-to-all-done.2 = bf16[64,4,8,128]{3,2,1,0:T(8,128)(2,1)S(1)} async-done(((bf16[64,4,8,128]{3,2,1,0:T(8,128)(2,1)}), bf16[64,4,8,128]{3,2,1,0:T(8,128)(2,1)S(1)}, u32[]{:S(2)}, u32[]{:S(2)}) %all-to-all-start.2) | async-done | bytes 524320 | tf_op jit(solution)/shard_map/all_to_all | solution.py:194
  313.7 89.8 %scatter_custom_fusion.2 = f32[8192,128]{1,0:T(8,128)} fusion(s32[16384]{0:T(1024)S(1)} %bitcast.130, f32[2048,128]{1,0:T(8,128)S(1)} %bitcast_convert_fusion, f32[]{:T(128)} %constant.79.clone.1), kind=kCustom, calls=%fused_computation.3 | custom fusion | flops 2097152 | bytes 5242884 | tf_op jit(solution)/shard_map/scatter-add | solution.py:109
  403.5 3.7 convert_element_type.102
  407.3 119.5 %reduce-scatter.8.cloned.1.call-done = bf16[2,256,128]{2,1,0:T(8,128)(2,1)} async-done(((bf16[2,4096,128]{2,1,0:T(8,128)(2,1)}), bf16[2,256,128]{2,1,0:T(8,128)(2,1)}) %reduce-scatter.8.cloned.1.call-update) | async-done | bytes 131088 | tf_op jit(solution)/shard_map/reduce_scatter | solution.py:201
  526.8 1.6 convert_element_type.104
  (81 shorter events, 23.5 us)
Async XLA Ops:
  6.5 79.2 %copy-start.2 = (bf16[2,512,32]{1,2,0:T(8,128)(2,1)S(1)}, bf16[2,512,32]{1,2,0:T(8,128)(2,1)}, u32[]{:S(2)}) copy-start(bf16[2,512,32]{1,2,0:T(8,128)(2,1)} %param.13) | copy-start | bytes 196612
  6.5 79.5 %copy-start.5 = (bf16[2,32,128]{2,1,0:T(8,128)(2,1)S(1)}, bf16[2,32,128]{2,1,0:T(8,128)(2,1)}, u32[]{:S(2)}) copy-start(bf16[2,32,128]{2,1,0:T(8,128)(2,1)} %param.14) | copy-start | bytes 49156
  6.5 76.9 %all-gather.3.cloned.1.call-start = ((), (), s32[]{:S(2)}) async-start(), calls=%async_computation.6 | async-start | bytes 1310720 | tf_op jit(solution)/shard_map/all_gather | solution.py:16
  7.3 140.0 %all-gather.5.cloned.1.call-start = ((), (), s32[]{:S(2)}) async-start(), calls=%async_computation.7 | async-start | bytes 1310720 | tf_op jit(solution)/shard_map/all_gather | solution.py:16
  83.5 2.2 copy-start
  86.0 66.5 %copy-start.1 = (bf16[8,128,128]{2,1,0:T(8,128)(2,1)S(1)}, bf16[8,128,128]{2,1,0:T(8,128)(2,1)}, u32[]{:S(2)}) copy-start(bf16[8,128,128]{2,1,0:T(8,128)(2,1)} %param.11) | copy-start | bytes 786436
  88.7 127.8 %reduce-scatter.4.cloned.1.call-start = ((), (), s32[]{:S(2)}) async-start(), calls=%async_computation.8 | async-start | bytes 1310720 | tf_op jit(solution)/shard_map/reduce_scatter | solution.py:76
  148.8 1.6 copy-start.3
  153.8 2.2 copy-start.7
  153.8 2.2 copy-start.8
  156.0 4.7 copy-start.4
  160.7 118.5 %reduce-scatter.6.cloned.1.call-start = ((), (), s32[]{:S(2)}) async-start(), calls=%async_computation.9 | async-start | bytes 1310720 | tf_op jit(solution)/shard_map/reduce_scatter | solution.py:76
  219.5 3.7 copy-start.10
  219.5 3.7 copy-start.11
  219.5 4.2 copy-start.9
  220.4 14.5 %copy-start.6 = (s32[8,128,8]{1,2,0:T(8,128)S(1)}, s32[8,128,8]{1,2,0:T(8,128)}, u32[]{:S(2)}) copy-start(s32[8,128,8]{1,2,0:T(8,128)} %param.16) | copy-start | bytes 98308
  225.5 20.3 %all-to-all-start = ((s32[64,4,8]{2,1,0:T(4,128)}), s32[64,4,8]{2,1,0:T(4,128)S(1)}, u32[]{:S(2)}, u32[]{:S(2)}) async-start(s32[64,4,8]{2,1,0:T(4,128)} %bitcast.4), calls=%async_computation | async-start | bytes 262144 | tf_op jit(solution)/shard_map/all_to_all | solution.py:196
  245.7 21.5 %all-to-all-start.1 = ((s32[64,1,256]{2,1,0:T(1,128)}), s32[64,1,256]{2,1,0:T(1,128)S(1)}, u32[]{:S(2)}, u32[]{:S(2)}) async-start(s32[64,1,256]{2,1,0:T(1,128)} %reshape.368), calls=%async_computation.1 | async-start | bytes 131072 | tf_op jit(solution)/shard_map/all_to_all | solution.py:195
  282.1 31.5 %all-to-all-start.2 = ((bf16[64,4,8,128]{3,2,1,0:T(8,128)(2,1)}), bf16[64,4,8,128]{3,2,1,0:T(8,128)(2,1)S(1)}, u32[]{:S(2)}, u32[]{:S(2)}) async-start(bf16[64,4,8,128]{3,2,1,0:T(8,128)(2,1)} %copy.47), calls=%async_computation.4 | async-start | bytes 1048576 | tf_op jit(solution)/shard_map/all_to_all | solution.py:194
  295.1 231.7 %reduce-scatter.8.cloned.1.call-start = ((), (), s32[]{:S(2)}) async-start(), calls=%async_computation.10 | async-start | bytes 2228224 | tf_op jit(solution)/shard_map/reduce_scatter | solution.py:201
Sparse Core Ops, SparseCore 0:
  10.0 73.3 all-gather.2
  88.8 58.4 all-gather.4
  160.8 55.6 reduce-scatter.3
  223.3 55.8 reduce-scatter.5
  407.4 119.3 reduce-scatter.7
where the time goes:
time: 536 us; the launch traced here: 535 us
  waiting for transfers between devices  354 us (66%)
  other arithmetic  103 us (19%)
  starting transfers between devices  28.4 us (5%)
  matrix products  19 us (4%)
  local copies, waits for them, and re-layouts  16.4 us (3%)
  between operations  13.6 us (3%)
    all_gather x2, waiting for transfers between devices, collect(): return lax.all_gather(values, 'slot', axis=1, tiled=True)  131 us
    reduce_scatter x1, waiting for transfers between devices, per_device(): lax.psum_scatter(totals.reshape(TABLE_DEV, ROWS, D).astype(jnp.bfloat16),...  120 us
    scatter-add x1, other arithmetic, add_bags(): totals.at[target.reshape(-1)].add(values.reshape(-1, width), mode='drop')  89.8 us
    reduce_scatter x2, waiting for transfers between devices, backward_rows(): lax.psum_scatter((linear + jnp.einsum('nk,bdk->nbd', basis_wide, grad_coe...  65.3 us
    all_to_all x1, waiting for transfers between devices, per_device(): lax.all_to_all(sent_grads, 'dp', split_axis=0, concat_axis=0, tiled=True)  17.7 us
    all_to_all x1, waiting for transfers between devices, per_device(): lax.all_to_all(sent_keys, 'dp', split_axis=0, concat_axis=0, tiled=True)  14.7 us
    all_to_all x1, starting transfers between devices, per_device(): lax.all_to_all(sent_grads, 'dp', split_axis=0, concat_axis=0, tiled=True)  13 us
  transfers between devices with their start and end apart: 8, of which 8 were waited for; matrix products, arithmetic and copies ran while one was open for 3% of the time, Pallas kernels for 0%

commit v1 on v0

v1 whole, which is shorter than its diff:
```python
import jax
import jax.numpy as jnp
from jax import lax
from jax.experimental import pallas as pl
from jax.experimental.pallas import tpu as pltpu
from jax.sharding import PartitionSpec as P

D = 128
LAYERS = 2
ROWS = 4096
TABLE_DEV = 2
BAG = 8
CAPACITY = 4
N_SLOT = 4
N_GRP = 4
DP = 64
SLOT_DEV = 128
SLOTS = 512
RANK = 32
PAIR = 2
ROW_BLOCK = 256
DEAD = 64
ID_ROWS = 32
MSG_ROWS = 2 * PAIR * SLOT_DEV + 48

norm_eps = 1e-05
f32 = jnp.float32
bf16 = jnp.bfloat16


def dot(a, b, ca=1, cb=0):
    return lax.dot_general(a, b, (((ca,), (cb,)), ((), ())), preferred_element_type=f32)


def iota(shape, dim):
    return lax.broadcasted_iota(jnp.int32, shape, dim)


def layers_kernel(x_ref, compress_ref, basis_ref, output_ref, gain_ref, out_ref):
    gain = gain_ref[...]
    pair_rows = PAIR * SLOT_DEV
    current = []
    upstream = []
    for b in range(PAIR):
        rows = slice(b * SLOT_DEV, (b + 1) * SLOT_DEV)
        current.append(jnp.concatenate([x_ref[k, rows, :] for k in range(N_SLOT)], axis=0))
        rows = slice(pair_rows + b * SLOT_DEV, pair_rows + (b + 1) * SLOT_DEV)
        upstream.append(jnp.concatenate([x_ref[k, rows, :] for k in range(N_SLOT)], axis=0))
    saved = []
    for layer in range(LAYERS):
        wide = jnp.concatenate(current, axis=1)
        coefficient = dot(basis_ref[layer], wide, 0, 0).astype(bf16)
        mixed = dot(compress_ref[layer], wide)
        following = []
        entry = []
        for b in range(PAIR):
            lanes = slice(b * D, (b + 1) * D)
            coeff = coefficient[:, lanes]
            feature = dot(current[b], coeff, 1, 1).astype(bf16)
            total = current[b].astype(f32) + dot(feature, output_ref[layer]) + mixed[:, lanes]
            mean = jnp.mean(total, axis=1, keepdims=True)
            centered = total - mean
            variance = jnp.mean(centered * centered, axis=1, keepdims=True)
            inv_std = lax.rsqrt(variance + norm_eps)
            normed = centered * inv_std
            entry.append((current[b], normed, inv_std, coeff))
            following.append((normed * gain[layer : layer + 1]).astype(bf16))
        saved.append(entry)
        current = following
    for layer in reversed(range(LAYERS)):
        lows = []
        local = []
        grad_feats = []
        for b in range(PAIR):
            inputs, normed, inv_std, coeff = saved[layer][b]
            scaled = upstream[b].astype(f32) * gain[layer : layer + 1]
            grad_sum = inv_std * (
                scaled
                - jnp.mean(scaled, axis=1, keepdims=True)
                - normed * jnp.mean(scaled * normed, axis=1, keepdims=True)
            )
            low = grad_sum.astype(bf16)
            grad_feat = dot(low, output_ref[layer], 1, 1).astype(bf16)
            local.append(grad_sum + dot(grad_feat, coeff))
            lows.append(low)
            grad_feats.append(grad_feat)
        linear = dot(compress_ref[layer], jnp.concatenate(lows, axis=1), 0, 0)
        basis_twice = jnp.concatenate([basis_ref[layer], basis_ref[layer]], axis=1)
        for b in range(PAIR):
            grad_coeff = dot(grad_feats[b], saved[layer][b][0], 0, 0)
            high = grad_coeff.astype(bf16)
            rest = (grad_coeff - high.astype(f32)).astype(bf16)
            basis_part = dot(basis_twice, jnp.concatenate([high, rest], axis=0))
            upstream[b] = (local[b] + linear[:, b * D : (b + 1) * D] + basis_part).astype(bf16)
    shape = (DP * PAIR * CAPACITY, PAIR * SLOT_DEV)
    row = iota(shape, 0)
    row_key = row // (PAIR * CAPACITY) * CAPACITY + row % CAPACITY + row // CAPACITY % PAIR * 1024
    sample_key = iota((1, PAIR * SLOT_DEV), 1) // SLOT_DEV * 1024
    targets = []
    for k in range(N_SLOT):
        target = x_ref[k, 2 * pair_rows + ID_ROWS : 2 * pair_rows + ID_ROWS + 16, :]
        target = target[:1].astype(f32).astype(jnp.int32)
        targets.append(target)
        column_key = jnp.concatenate([target] * PAIR, axis=1) + sample_key
        placing = jnp.where(row_key == column_key, 1.0, 0.0).astype(bf16)
        rows = slice(k * SLOT_DEV, (k + 1) * SLOT_DEV)
        values = jnp.concatenate([u[rows] for u in upstream], axis=0)
        out_ref[:, k] = dot(placing, values).astype(bf16).reshape(DP, PAIR * CAPACITY, D)
    shape = (DP * 8, SLOTS)
    row = iota(shape, 0)
    row_key = row // 8 * CAPACITY + row % 8 * 1024
    column_key = jnp.concatenate([targets[k] + k * 1024 for k in range(N_SLOT)], axis=1)
    unpacked = []
    lane_in = iota((D, D), 0)
    lane_out = iota((D, D), 1)
    for k in range(N_SLOT):
        packed = x_ref[k, 2 * pair_rows : 2 * pair_rows + ID_ROWS, :]
        for q in range(D // ID_ROWS):
            spread = jnp.where(lane_in == q * 32 + lane_out % 32, 1.0, 0.0).astype(bf16)
            unpacked.append(dot(packed, spread).astype(bf16))
    unpacked = jnp.concatenate(unpacked, axis=0)
    rank_lane = iota((1, D), 1) // 32
    ids = jnp.zeros((DP * 8, D), f32)
    for rank in range(CAPACITY):
        placing = jnp.where(row_key + rank == column_key, 1.0, 0.0).astype(bf16)
        ids = ids + jnp.where(rank_lane == rank, dot(placing, unpacked), 0.0)
    out_ref[:, N_SLOT] = ids.astype(bf16).reshape(DP, 8, D)


def run_layers(messages, compress, basis, outputs, gain):
    return pl.pallas_call(
        layers_kernel,
        out_shape=jax.ShapeDtypeStruct((DP, N_SLOT + 1, 8, D), bf16),
        in_specs=[pl.BlockSpec(memory_space=pltpu.VMEM)] * 5,
        out_specs=pl.BlockSpec(memory_space=pltpu.VMEM),
        compiler_params=pltpu.CompilerParams(vmem_limit_bytes=48 << 20),
        cost_estimate=pl.CostEstimate(flops=2_000_000_000, bytes_accessed=4 << 20, transcendentals=4096),
        name="layers",
    )(messages, compress, basis, outputs, gain)


def bags_kernel(got_ref, out_ref, wide_ref, grads_ref, high_ref, low_ref):
    caps = N_SLOT * CAPACITY
    bags = PAIR * DP
    shape = (DP * 8, N_SLOT * bags)
    row = iota(shape, 0)
    lane = iota(shape, 1)
    pick = (row // 8 == lane % DP) & (row % 8 == lane // bags)
    ids = dot(
        got_ref[:, N_SLOT].reshape(DP * 8, D), jnp.where(pick, 1.0, 0.0).astype(bf16), 0, 0
    )
    first_sample = iota((1, bags), 1) < DP
    for k in range(N_SLOT):
        wide_ref[...] = got_ref[:, k].astype(f32).reshape(DP * 8, D)
        for rank in range(CAPACITY):
            cap = k * CAPACITY + rank
            both = ids[rank * 32 : (rank + 1) * 32, k * bags : (k + 1) * bags]
            own = jnp.where(first_sample, both[:16], both[16:])
            high, low = own[:8], own[8:]
            table = jnp.where(jnp.max(jnp.where(high >= DEAD, high - DEAD, high)[:1], axis=1, keepdims=True) >= 16, 1.0, 0.0)
            half = cap % 2
            lanes = slice(half * bags, (half + 1) * bags)
            high_ref[cap // 2, :, lanes] = high - 16.0 * table
            low_ref[cap // 2, :, lanes] = low
            values = jnp.concatenate(
                [wide_ref[pl.ds(b * CAPACITY + rank, DP, stride=8), :] for b in range(PAIR)], axis=0
            )
            rows = slice(half * bags, (half + 1) * bags)
            grads_ref[cap // 2, rows, :D] = (values * (1.0 - table)).astype(bf16)
            grads_ref[cap // 2, rows, D:] = (values * table).astype(bf16)
    rows_of = iota((ROW_BLOCK, 2 * bags), 0).astype(f32).astype(bf16)
    one = jnp.ones((), bf16)
    zero = jnp.zeros((), bf16)

    def block(index, carry):
        want = index.astype(f32)
        total = jnp.zeros((ROW_BLOCK, 2 * D), f32)
        for p in range(caps // 2):
            match = jnp.where(high_ref[p] == want, low_ref[p], -1.0)
            count = jnp.zeros((ROW_BLOCK, 2 * bags), bf16)
            for j in range(BAG):
                wanted = jnp.broadcast_to(match[j : j + 1], (16, 2 * bags)).astype(bf16)
                wanted = jnp.broadcast_to(wanted[None], (ROW_BLOCK // 16, 16, 2 * bags)).reshape(ROW_BLOCK, 2 * bags)
                count = count + jnp.where(rows_of == wanted, one, zero)
            total = total + dot(count, grads_ref[p])
        out_ref[index, 0] = total[:, :D].astype(bf16)
        out_ref[index, 1] = total[:, D:].astype(bf16)
        return carry

    lax.fori_loop(0, N_SLOT * N_GRP, block, 0)


def run_bags(got):
    pairs = N_SLOT * CAPACITY // 2
    return pl.pallas_call(
        bags_kernel,
        out_shape=jax.ShapeDtypeStruct((N_SLOT * N_GRP, TABLE_DEV, ROW_BLOCK, D), bf16),
        in_specs=[pl.BlockSpec(memory_space=pltpu.VMEM)],
        out_specs=pl.BlockSpec(memory_space=pltpu.VMEM),
        scratch_shapes=[
            pltpu.VMEM((DP * 8, D), f32),
            pltpu.VMEM((pairs, 2 * PAIR * DP, 2 * D), bf16),
            pltpu.VMEM((pairs, BAG, 2 * PAIR * DP), f32),
            pltpu.VMEM((pairs, BAG, 2 * PAIR * DP), f32),
        ],
        compiler_params=pltpu.CompilerParams(vmem_limit_bytes=48 << 20),
        cost_estimate=pl.CostEstimate(flops=20_000_000_000, bytes_accessed=4 << 20, transcendentals=0),
        name="bags",
    )(got)


def per_device(
    pooled,
    cotangent,
    compress_weight,
    fm_basis,
    fm_output,
    norm_gain,
    bag_ids,
    bag_lengths,
    slot_table,
    table_home,
):
    slot_count = pooled.shape[1]
    matches = slot_table[:, None] == jnp.arange(table_home.shape[0], dtype=jnp.int32)[None, :]
    position = jnp.sum(jnp.where(matches, table_home[None, :], 0), axis=1)
    owner = position // TABLE_DEV
    table = position % TABLE_DEV
    order = jnp.arange(slot_count, dtype=jnp.int32)
    rank = jnp.sum(
        ((owner[None, :] == owner[:, None]) & (order[None, :] < order[:, None])).astype(jnp.int32), axis=1
    )
    target = owner * CAPACITY + rank
    live = jnp.arange(BAG, dtype=jnp.int32)[None, None, :] < bag_lengths[:, :, None]
    high = jnp.where(live, bag_ids // ROW_BLOCK, DEAD) + table[None, :, None] * 16
    low = bag_ids % ROW_BLOCK
    parts = jnp.stack([high, low], axis=2).astype(bf16)
    parts = parts.reshape(N_SLOT, PAIR, 4, 32, 16).transpose(0, 3, 2, 1, 4).reshape(N_SLOT, ID_ROWS, D)
    marks = jnp.broadcast_to(target.astype(bf16)[None, None, :], (N_SLOT, 16, slot_count))
    messages = jnp.concatenate(
        [
            pooled.reshape(N_SLOT, PAIR * slot_count, D),
            cotangent.reshape(N_SLOT, PAIR * slot_count, D),
            parts,
            marks,
        ],
        axis=1,
    )
    messages = lax.all_to_all(messages, "slot", split_axis=0, concat_axis=0, tiled=True)
    sent = run_layers(messages, compress_weight, fm_basis, fm_output, norm_gain)
    got = lax.all_to_all(sent, "dp", split_axis=0, concat_axis=0, tiled=True)
    totals = run_bags(got)
    totals = totals.reshape(N_SLOT, N_GRP, TABLE_DEV, ROW_BLOCK, D).transpose(1, 0, 2, 3, 4)
    totals = lax.all_to_all(totals, "grp", split_axis=0, concat_axis=0, tiled=True)
    totals = jnp.sum(totals.astype(f32), axis=0).astype(bf16)
    totals = lax.all_to_all(totals, "slot", split_axis=0, concat_axis=0, tiled=True)
    return jnp.sum(totals.astype(f32), axis=0)


def solution(mesh):
    in_specs = (
        P(("dp", "grp"), "slot", None),
        P(("dp", "grp"), "slot", None),
        P(),
        P(),
        P(),
        P(),
        P(("dp", "grp"), "slot", None),
        P(("dp", "grp"), "slot"),
        P("slot"),
        P(),
    )
    out_specs = P("dp", ("slot", "grp"), None)
    return jax.shard_map(
        per_device, mesh=mesh, in_specs=in_specs, out_specs=out_specs, check_vma=False
    )
```

time: 536 us -> 173 us (0.32)
  waiting for transfers between devices: 354 us -> 17.3 us
  blocking collectives: 0 us -> 109 us
  other arithmetic: 103 us -> 4.96 us
  Pallas kernels: 0 us -> 20.9 us
  matrix products: 19 us -> 0 us
  local copies, waits for them, and re-layouts: 16.4 us -> 0.65 us
  between operations: 13.6 us -> 0.14 us
  starting transfers between devices: 28.4 us -> 19.3 us
    reduce_scatter x3 -> x0, waiting for transfers between devices: 185 us -> none  [the longest x1 120 us: per_device(): lax.psum_scatter(totals.reshape(TABLE_DEV, ROWS, D).astype(jnp.bfloat16),...]
    all_gather x2 -> x0, waiting for transfers between devices: 131 us -> none  [collect(): return lax.all_gather(values, 'slot', axis=1, tiled=True)]
    all_to_all x0 -> x3, blocking collectives: none -> 109 us  [the longest x1 47.7 us: per_device(): got = lax.all_to_all(sent, 'dp', split_axis=0, concat_axis=0, tiled=True)]
    scatter-add x1 -> x0, other arithmetic: 89.8 us -> none  [add_bags(): totals.at[target.reshape(-1)].add(values.reshape(-1, width), mode='drop')]
    pallas_call x0 -> x2, Pallas kernels: none -> 20.9 us  [the longest x1 16.5 us: run_bags(): pl.pallas_call(bags_kernel, out_shape=jax.ShapeDtypeStruct((N_SLOT * N_GR...]
    all_to_all x3 -> x1, waiting for transfers between devices: 37.4 us -> 17.3 us  [per_device(): lax.all_to_all(messages, 'slot', split_axis=0, concat_axis=0, tiled=True)]
    dot_general x15 -> x0, matrix products: 18.5 us -> none  [the longest x2 4.2 us: backward_rows(): jnp.einsum('nk,bdk->nbd', basis_wide, grad_coeff, precision=lax.Precision...]
    all_to_all x3 -> x1, starting transfers between devices: 28.3 us -> 19.3 us  [per_device(): lax.all_to_all(messages, 'slot', split_axis=0, concat_axis=0, tiled=True)]
  transfers between devices with their start and end apart: 8 -> 1, of which waited for: 8 -> 1; matrix products, arithmetic and copies ran while one was open for 3% -> 0% of each run, Pallas kernels for 0% -> 0%
where the time goes in v1:
time: 173 us; the launch traced here: 172 us
  blocking collectives  109 us (63%)
  Pallas kernels  20.9 us (12%)
  starting transfers between devices  19.3 us (11%)
  waiting for transfers between devices  17.3 us (10%)
  other arithmetic  4.96 us (3%)
    all_to_all x1, blocking collectives, per_device(): got = lax.all_to_all(sent, 'dp', split_axis=0, concat_axis=0, tiled=True)  47.7 us
    all_to_all x1, blocking collectives, per_device(): lax.all_to_all(totals, 'slot', split_axis=0, concat_axis=0, tiled=True)  31.8 us
    all_to_all x1, blocking collectives, per_device(): lax.all_to_all(totals, 'grp', split_axis=0, concat_axis=0, tiled=True)  29.3 us
    all_to_all x1, starting transfers between devices, per_device(): lax.all_to_all(messages, 'slot', split_axis=0, concat_axis=0, tiled=True)  19.3 us
    all_to_all x1, waiting for transfers between devices, per_device(): lax.all_to_all(messages, 'slot', split_axis=0, concat_axis=0, tiled=True)  17.3 us
    pallas_call x1, Pallas kernels, run_bags(): pl.pallas_call(bags_kernel, out_shape=jax.ShapeDtypeStruct((N_SLOT * N_GR...  16.5 us
    pallas_call x1, Pallas kernels, run_layers(): pl.pallas_call(layers_kernel, out_shape=jax.ShapeDtypeStruct((DP, N_SLOT...  4.41 us
  transfers between devices with their start and end apart: 1, of which 1 were waited for; matrix products, arithmetic and copies ran while one was open for 0% of the time, Pallas kernels for 0%

profile of v1, /device:TPU:1, one launch (start us, length us, event | category | flops | bytes accessed | tf_op | source)
XLA Modules:
  0.0 172.0 jit_solution(5675366065125080907)
XLA Ops:
  0.0 0.8 select_reduce_fusion
  0.9 0.2 convert_reduce_fusion.1
  1.1 0.8 fusion.8
  1.9 0.1 convert_element_type.20
  2.0 0.1 copy.23
  2.2 0.0 copy-start.3
  2.2 0.0 copy-start
  2.2 0.0 copy-start.1
  2.2 0.0 copy-start.2
  2.2 2.0 %pad_maximum_fusion = bf16[4,560,128]{2,1,0:T(8,128)(2,1)} fusion(bf16[4,16,128]{2,1,0:T(8,128)(2,1)S(1)} %broadcast_in_dim.21, bf16[4,32,128]{2,1,0:T(8,128)(2,1)S(1)} %copy.23, bf16[4,256,128]{2,1,0:T(8,128)(2,1)} %bitcast.20, bf16[4,256,128]{2,1,0:T(8,128)(2,1)} %bitcast.21), kind=kLoop, calls=%fused_computation.2 | loop fusion | flops 2293760 | bytes 1146880 | tf_op jit(solution)/shard_map/concatenate | solution.py:240
  4.2 19.3 %all-to-all-start = ((bf16[4,560,128]{2,1,0:T(8,128)(2,1)}), bf16[4,560,128]{2,1,0:T(8,128)(2,1)S(1)}, u32[]{:S(2)}, u32[]{:S(2)}) async-start(bf16[4,560,128]{2,1,0:T(8,128)(2,1)} %pad_maximum_fusion), calls=%async_computation | async-start | bytes 1146880 | tf_op jit(solution)/shard_map/all_to_all | solution.py:249
  23.4 0.0 copy-done.3
  23.4 0.2 copy.24.basis_ref
  23.6 17.3 %all-to-all-done.x_ref = bf16[4,560,128]{2,1,0:T(8,128)(2,1)S(1)} async-done(((bf16[4,560,128]{2,1,0:T(8,128)(2,1)}), bf16[4,560,128]{2,1,0:T(8,128)(2,1)S(1)}, u32[]{:S(2)}, u32[]{:S(2)}) %all-to-all-start) | async-done | bytes 573472 | tf_op jit(solution)/shard_map/all_to_all | solution.py:249
  40.9 0.0 copy-done
  40.9 0.0 copy-done.2
  40.9 4.4 %layers.1 = bf16[64,5,8,128]{3,2,1,0:T(8,128)(2,1)S(1)} custom-call(bf16[4,560,128]{2,1,0:T(8,128)(2,1)S(1)} %all-to-all-done.x_ref, bf16[2,512,512]{2,1,0:T(8,128)(2,1)S(1)} %copy-done, bf16[2,512,32]{2,1,0:T(8,128)(2,1)S(1)} %copy.24.basis_ref, bf16[2,32,128]{2,1,0:T(8,128)(2,1)S(1)} %copy-done.1, f32[2,128]{1,0:T(2,128)S(1)} %copy-done.2), custom_call_target="tpu_custom_call" | custom-call | flops 2000000000 | bytes 4194304 | tf_op jit(solution)/shard_map/layers/pallas_call | solution.py:131
  45.3 47.7 %all_to_all.20.got_ref = bf16[64,5,8,128]{3,2,1,0:T(8,128)(2,1)S(1)} all-to-all(bf16[64,5,8,128]{3,2,1,0:T(8,128)(2,1)S(1)} %layers.1), channel_id=1, replica_groups=mesh['dp'=64,'slot'=4,'grp'=4] {'dp'}, dimensions={0} | all-to-all | bytes 1310720 | tf_op jit(solution)/shard_map/all_to_all | solution.py:251
  93.1 16.5 %bags.1 = bf16[16,2,256,128]{3,2,1,0:T(8,128)(2,1)S(1)} custom-call(bf16[64,5,8,128]{3,2,1,0:T(8,128)(2,1)S(1)} %all_to_all.20.got_ref), custom_call_target="tpu_custom_call" | custom-call | flops 20000000000 | bytes 4194304 | tf_op jit(solution)/shard_map/bags/pallas_call | solution.py:195
  109.6 0.2 copy.27
  109.8 29.3 %all_to_all.21 = bf16[4,4,2,256,128]{4,3,2,1,0:T(8,128)(2,1)S(1)} all-to-all(bf16[4,4,2,256,128]{4,3,2,1,0:T(8,128)(2,1)S(1)} %bitcast.17), channel_id=1, replica_groups=mesh['dp'=64,'slot'=4,'grp'=4] {'grp'}, dimensions={0} | all-to-all | bytes 4194304 | tf_op jit(solution)/shard_map/all_to_all | solution.py:254
  139.1 0.4 reduce_sum.41
  139.5 31.8 %all_to_all.22 = bf16[4,2,256,128]{3,2,1,0:T(8,128)(2,1)S(1)} all-to-all(bf16[4,2,256,128]{3,2,1,0:T(8,128)(2,1)S(1)} %reduce_sum.41), channel_id=1, replica_groups=mesh['dp'=64,'slot'=4,'grp'=4] {'slot'}, dimensions={0} | all-to-all | bytes 1048576 | tf_op jit(solution)/shard_map/all_to_all | solution.py:256
  171.3 0.8 convert_reduce_fusion
  (7 shorter events, 0.1 us)
Async XLA Ops:
  2.2 21.3 %copy-start.3 = (bf16[2,512,32]{1,2,0:T(8,128)(2,1)S(1)}, bf16[2,512,32]{1,2,0:T(8,128)(2,1)}, u32[]{:S(2)}) copy-start(bf16[2,512,32]{1,2,0:T(8,128)(2,1)} %param.13) | copy-start | bytes 196612
  2.2 38.7 %copy-start = (bf16[2,512,512]{2,1,0:T(8,128)(2,1)S(1)}, bf16[2,512,512]{2,1,0:T(8,128)(2,1)}, u32[]{:S(2)}) copy-start(bf16[2,512,512]{2,1,0:T(8,128)(2,1)} %compress_ref.1) | copy-start | bytes 3145732
  2.2 38.7 %copy-start.1 = (bf16[2,32,128]{2,1,0:T(8,128)(2,1)S(1)}, bf16[2,32,128]{2,1,0:T(8,128)(2,1)}, u32[]{:S(2)}) copy-start(bf16[2,32,128]{2,1,0:T(8,128)(2,1)} %output_ref.1) | copy-start | bytes 49156
  2.2 38.7 %copy-start.2 = (f32[2,128]{1,0:T(2,128)S(1)}, f32[2,128]{1,0:T(2,128)}, u32[]{:S(2)}) copy-start(f32[2,128]{1,0:T(2,128)} %gain_ref.1) | copy-start | bytes 3076
  4.2 36.7 %all-to-all-start = ((bf16[4,560,128]{2,1,0:T(8,128)(2,1)}), bf16[4,560,128]{2,1,0:T(8,128)(2,1)S(1)}, u32[]{:S(2)}, u32[]{:S(2)}) async-start(bf16[4,560,128]{2,1,0:T(8,128)(2,1)} %pad_maximum_fusion), calls=%async_computation | async-start | bytes 1146880 | tf_op jit(solution)/shard_map/all_to_all | solution.py:249

commit v2 on v1

--- a/solution.py
+++ b/solution.py
@@ -1,3 +1,5 @@
+import functools
+
 import jax
 import jax.numpy as jnp
 from jax import lax
@@ -139,8 +141,7 @@
     )(messages, compress, basis, outputs, gain)
 
 
-def bags_kernel(got_ref, out_ref, wide_ref, grads_ref, high_ref, low_ref):
-    caps = N_SLOT * CAPACITY
+def prepare_bags(got_ref, wide_ref, grads_ref, high_ref, low_ref):
     bags = PAIR * DP
     shape = (DP * 8, N_SLOT * bags)
     row = iota(shape, 0)
@@ -157,7 +158,8 @@
             both = ids[rank * 32 : (rank + 1) * 32, k * bags : (k + 1) * bags]
             own = jnp.where(first_sample, both[:16], both[16:])
             high, low = own[:8], own[8:]
-            table = jnp.where(jnp.max(jnp.where(high >= DEAD, high - DEAD, high)[:1], axis=1, keepdims=True) >= 16, 1.0, 0.0)
+            alive = jnp.where(high >= DEAD, high - DEAD, high)[:1]
+            table = jnp.where(jnp.max(alive, axis=1, keepdims=True) >= 16, 1.0, 0.0)
             half = cap % 2
             lanes = slice(half * bags, (half + 1) * bags)
             high_ref[cap // 2, :, lanes] = high - 16.0 * table
@@ -168,45 +170,78 @@
             rows = slice(half * bags, (half + 1) * bags)
             grads_ref[cap // 2, rows, :D] = (values * (1.0 - table)).astype(bf16)
             grads_ref[cap // 2, rows, D:] = (values * table).astype(bf16)
-    rows_of = iota((ROW_BLOCK, 2 * bags), 0).astype(f32).astype(bf16)
+
+
+def add_rows(first, amount, shift, out_refs, grads_ref, high_ref, low_ref):
+    lanes = 2 * PAIR * DP
+    rows_of = (iota((amount, lanes), 0) + first).astype(f32).astype(bf16)
     one = jnp.ones((), bf16)
     zero = jnp.zeros((), bf16)
 
-    def block(index, carry):
-        want = index.astype(f32)
-        total = jnp.zeros((ROW_BLOCK, 2 * D), f32)
-        for p in range(caps // 2):
-            match = jnp.where(high_ref[p] == want, low_ref[p], -1.0)
-            count = jnp.zeros((ROW_BLOCK, 2 * bags), bf16)
-            for j in range(BAG):
-                wanted = jnp.broadcast_to(match[j : j + 1], (16, 2 * bags)).astype(bf16)
-                wanted = jnp.broadcast_to(wanted[None], (ROW_BLOCK // 16, 16, 2 * bags)).reshape(ROW_BLOCK, 2 * bags)
-                count = count + jnp.where(rows_of == wanted, one, zero)
-            total = total + dot(count, grads_ref[p])
-        out_ref[index, 0] = total[:, :D].astype(bf16)
-        out_ref[index, 1] = total[:, D:].astype(bf16)
+    def block(s, carry):
+        for r in range(N_GRP):
+            group = shift + r
+            group = jnp.where(group >= N_GRP, group - N_GRP, group)
+            want = (s * N_GRP + group).astype(f32)
+            total = jnp.zeros((amount, 2 * D), f32)
+            for p in range(N_SLOT * CAPACITY // 2):
+                match = jnp.where(high_ref[p] == want, low_ref[p], -1.0)
+                count = jnp.zeros((amount, lanes), bf16)
+                for j in range(BAG):
+                    wanted = jnp.broadcast_to(match[j : j + 1], (16, lanes)).astype(bf16)
+                    wanted = jnp.broadcast_to(wanted[None], (amount // 16, 16, lanes)).reshape(amount, lanes)
+                    count = count + jnp.where(rows_of == wanted, one, zero)
+                total = total + dot(count, grads_ref[p])
+            out_refs[r][s, 0] = total[:, :D].astype(bf16)
+            out_refs[r][s, 1] = total[:, D:].astype(bf16)
         return carry
 
-    lax.fori_loop(0, N_SLOT * N_GRP, block, 0)
-
-
-def run_bags(got):
+    lax.fori_loop(0, N_SLOT, block, 0)
+
+
+def first_bags_kernel(amount, got_ref, out_ref, grads_ref, high_ref, low_ref, wide_ref):
+    prepare_bags(got_ref, wide_ref, grads_ref, high_ref, low_ref)
+    outs = [out_ref.at[r] for r in range(N_GRP)]
+    add_rows(0, amount, jnp.int32(0), outs, grads_ref, high_ref, low_ref)
+
+
+def second_bags_kernel(first, amount, shift_ref, grads_ref, high_ref, low_ref, *out_refs):
+    add_rows(first, amount, shift_ref[0], out_refs, grads_ref, high_ref, low_ref)
+
+
+VMEM_SPEC = pl.BlockSpec(memory_space=pltpu.VMEM)
+
+
+def run_first_bags(got, amount):
     pairs = N_SLOT * CAPACITY // 2
+    lanes = 2 * PAIR * DP
     return pl.pallas_call(
-        bags_kernel,
-        out_shape=jax.ShapeDtypeStruct((N_SLOT * N_GRP, TABLE_DEV, ROW_BLOCK, D), bf16),
-        in_specs=[pl.BlockSpec(memory_space=pltpu.VMEM)],
-        out_specs=pl.BlockSpec(memory_space=pltpu.VMEM),
-        scratch_shapes=[
-            pltpu.VMEM((DP * 8, D), f32),
-            pltpu.VMEM((pairs, 2 * PAIR * DP, 2 * D), bf16),
-            pltpu.VMEM((pairs, BAG, 2 * PAIR * DP), f32),
-            pltpu.VMEM((pairs, BAG, 2 * PAIR * DP), f32),
-        ],
-        compiler_params=pltpu.CompilerParams(vmem_limit_bytes=48 << 20),
-        cost_estimate=pl.CostEstimate(flops=20_000_000_000, bytes_accessed=4 << 20, transcendentals=0),
-        name="bags",
+        functools.partial(first_bags_kernel, amount),
+        out_shape=(
+            jax.ShapeDtypeStruct((N_GRP, N_SLOT, TABLE_DEV, amount, D), bf16),
+            jax.ShapeDtypeStruct((pairs, lanes, 2 * D), bf16),
+            jax.ShapeDtypeStruct((pairs, BAG, lanes), f32),
+            jax.ShapeDtypeStruct((pairs, BAG, lanes), f32),
+        ),
+        in_specs=[VMEM_SPEC],
+        out_specs=(VMEM_SPEC,) * 4,
+        scratch_shapes=[pltpu.VMEM((DP * 8, D), f32)],
+        compiler_params=pltpu.CompilerParams(vmem_limit_bytes=32 << 20),
+        cost_estimate=pl.CostEstimate(flops=10_000_000_000, bytes_accessed=4 << 20, transcendentals=0),
+        name="first_bags",
     )(got)
+
+
+def run_second_bags(shift, grads, high, low, first, amount):
+    return pl.pallas_call(
+        functools.partial(second_bags_kernel, first, amount),
+        out_shape=(jax.ShapeDtypeStruct((N_SLOT, TABLE_DEV, amount, D), bf16),) * N_GRP,
+        in_specs=[pl.BlockSpec(memory_space=pltpu.SMEM)] + [VMEM_SPEC] * 3,
+        out_specs=(VMEM_SPEC,) * N_GRP,
+        compiler_params=pltpu.CompilerParams(vmem_limit_bytes=32 << 20),
+        cost_estimate=pl.CostEstimate(flops=10_000_000_000, bytes_accessed=4 << 20, transcendentals=0),
+        name="second_bags",
+    )(shift, grads, high, low)
 
 
 def per_device(
@@ -249,12 +284,23 @@
     messages = lax.all_to_all(messages, "slot", split_axis=0, concat_axis=0, tiled=True)
     sent = run_layers(messages, compress_weight, fm_basis, fm_output, norm_gain)
     got = lax.all_to_all(sent, "dp", split_axis=0, concat_axis=0, tiled=True)
-    totals = run_bags(got)
-    totals = totals.reshape(N_SLOT, N_GRP, TABLE_DEV, ROW_BLOCK, D).transpose(1, 0, 2, 3, 4)
-    totals = lax.all_to_all(totals, "grp", split_axis=0, concat_axis=0, tiled=True)
-    totals = jnp.sum(totals.astype(f32), axis=0).astype(bf16)
-    totals = lax.all_to_all(totals, "slot", split_axis=0, concat_axis=0, tiled=True)
-    return jnp.sum(totals.astype(f32), axis=0)
+    half = ROW_BLOCK // 2
+    first, grads, high_ids, low_ids = run_first_bags(got, half)
+    shift = lax.axis_index("grp").astype(jnp.int32).reshape(1)
+    second = run_second_bags(shift, grads, high_ids, low_ids, half, half)
+    first = lax.all_to_all(first, "grp", split_axis=0, concat_axis=0, tiled=True)
+    first = jnp.sum(first.astype(f32), axis=0).astype(bf16)
+    first, second = lax.optimization_barrier((first, second))
+    first = lax.all_to_all(first, "slot", split_axis=0, concat_axis=0, tiled=True)
+    pieces = [second[0]]
+    for step in range(1, N_GRP):
+        moves = [(i, (i + step) % N_GRP) for i in range(N_GRP)]
+        pieces.append(lax.ppermute(second[step], "grp", moves))
+    second = sum(piece.astype(f32) for piece in pieces).astype(bf16)
+    second = lax.all_to_all(second, "slot", split_axis=0, concat_axis=0, tiled=True)
+    return jnp.concatenate(
+        [jnp.sum(first.astype(f32), axis=0), jnp.sum(second.astype(f32), axis=0)], axis=1
+    )
 
 
 def solution(mesh):

time: 173 us -> 177 us (1.023); the launches traced: 172 us -> 173 us
  blocking collectives: 109 us -> 0 us
  starting transfers between devices: 19.3 us -> 73.8 us
  waiting for transfers between devices: 17.3 us -> 70.4 us
    all_to_all x3 -> x0, blocking collectives: 109 us -> none  [the longest x1 47.7 us: per_device(): got = lax.all_to_all(sent, 'dp', split_axis=0, concat_axis=0, tiled=True)]
    all_to_all x0 -> x4, starting transfers between devices: none -> 46.1 us  [the longest x1 26.9 us: per_device(): got = lax.all_to_all(sent, 'dp', split_axis=0, concat_axis=0, tiled=True)]
    all_to_all x0 -> x4, waiting for transfers between devices: none -> 43.7 us  [the longest x1 21 us: per_device(): got = lax.all_to_all(sent, 'dp', split_axis=0, concat_axis=0, tiled=True)]
    ppermute x0 -> x3, waiting for transfers between devices: none -> 9.43 us  [per_device(): pieces.append(lax.ppermute(second[step], 'grp', moves))]
    ppermute x0 -> x3, starting transfers between devices: none -> 8.4 us  [per_device(): pieces.append(lax.ppermute(second[step], 'grp', moves))]
    pallas_call x1 -> x2, Pallas kernels: 16.5 us -> 17 us  [the longest x1 9.32 us: run_first_bags(): pl.pallas_call(functools.partial(first_bags_kernel, amount), out_shape=(j...]
  transfers between devices with their start and end apart: 1 -> 8, of which waited for: 1 -> 7; matrix products, arithmetic and copies ran while one was open for 0% -> 1% of each run, Pallas kernels for 0% -> 4%
where the time goes in v2:
time: 177 us; the launch traced here: 173 us
  starting transfers between devices  73.8 us (42%)
  waiting for transfers between devices  70.4 us (40%)
  Pallas kernels  22.2 us (13%)
  other arithmetic  6.37 us (4%)
    all_to_all x1, starting transfers between devices, per_device(): got = lax.all_to_all(sent, 'dp', split_axis=0, concat_axis=0, tiled=True)  26.9 us
    all_to_all x1, waiting for transfers between devices, per_device(): got = lax.all_to_all(sent, 'dp', split_axis=0, concat_axis=0, tiled=True)  21 us
    all_to_all x1, starting transfers between devices, per_device(): lax.all_to_all(messages, 'slot', split_axis=0, concat_axis=0, tiled=True)  19.3 us
    all_to_all x1, waiting for transfers between devices, per_device(): lax.all_to_all(messages, 'slot', split_axis=0, concat_axis=0, tiled=True)  17.3 us
    all_to_all x1, waiting for transfers between devices, per_device(): lax.all_to_all(second, 'slot', split_axis=0, concat_axis=0, tiled=True)  15.8 us
    all_to_all x1, starting transfers between devices, per_device(): lax.all_to_all(second, 'slot', split_axis=0, concat_axis=0, tiled=True)  11.2 us
    ppermute x3, waiting for transfers between devices, per_device(): pieces.append(lax.ppermute(second[step], 'grp', moves))  9.43 us
    pallas_call x1, Pallas kernels, run_first_bags(): pl.pallas_call(functools.partial(first_bags_kernel, amount), out_shape=(j...  9.32 us
  transfers between devices with their start and end apart: 8, of which 7 were waited for; matrix products, arithmetic and copies ran while one was open for 1% of the time, Pallas kernels for 4%

profile of v2, /device:TPU:1, one launch (start us, length us, event | category | flops | bytes accessed | tf_op | source)
XLA Modules:
  0.0 173.4 jit_solution(11536278725428309381)
XLA Ops:
  0.0 0.8 select_reduce_fusion
  0.9 0.8 fusion.8
  2.2 2.0 %pad_maximum_fusion = bf16[4,560,128]{2,1,0:T(8,128)(2,1)} fusion(bf16[4,16,128]{2,1,0:T(8,128)(2,1)S(1)} %broadcast_in_dim.21, bf16[4,32,128]{2,1,0:T(8,128)(2,1)S(1)} %copy.18, bf16[4,256,128]{2,1,0:T(8,128)(2,1)} %bitcast.15, bf16[4,256,128]{2,1,0:T(8,128)(2,1)} %bitcast.16), kind=kLoop, calls=%fused_computation | loop fusion | flops 2293760 | bytes 1146880 | tf_op jit(solution)/shard_map/concatenate | solution.py:275
  4.2 19.3 %all-to-all-start = ((bf16[4,560,128]{2,1,0:T(8,128)(2,1)}), bf16[4,560,128]{2,1,0:T(8,128)(2,1)S(1)}, u32[]{:S(2)}, u32[]{:S(2)}) async-start(bf16[4,560,128]{2,1,0:T(8,128)(2,1)} %pad_maximum_fusion), calls=%async_computation | async-start | bytes 1146880 | tf_op jit(solution)/shard_map/all_to_all | solution.py:284
  23.6 17.3 %all-to-all-done.x_ref = bf16[4,560,128]{2,1,0:T(8,128)(2,1)S(1)} async-done(((bf16[4,560,128]{2,1,0:T(8,128)(2,1)}), bf16[4,560,128]{2,1,0:T(8,128)(2,1)S(1)}, u32[]{:S(2)}, u32[]{:S(2)}) %all-to-all-start) | async-done | bytes 573472 | tf_op jit(solution)/shard_map/all_to_all | solution.py:284
  40.9 5.3 %layers.1 = bf16[64,5,8,128]{3,2,1,0:T(8,128)(2,1)} custom-call(bf16[4,560,128]{2,1,0:T(8,128)(2,1)S(1)} %all-to-all-done.x_ref, bf16[2,512,512]{2,1,0:T(8,128)(2,1)S(1)} %copy-done, bf16[2,512,32]{2,1,0:T(8,128)(2,1)S(1)} %copy.19.basis_ref, bf16[2,32,128]{2,1,0:T(8,128)(2,1)S(1)} %copy-done.1, f32[2,128]{1,0:T(2,128)S(1)} %copy-done.2), custom_call_target="tpu_custom_call" | custom-call | flops 2000000000 | bytes 4194304 | tf_op jit(solution)/shard_map/layers/pallas_call | solution.py:133
  46.2 26.9 %all-to-all-start.1 = ((bf16[64,5,8,128]{3,2,1,0:T(8,128)(2,1)}), bf16[64,5,8,128]{3,2,1,0:T(8,128)(2,1)S(1)}, u32[]{:S(2)}, u32[]{:S(2)}) async-start(bf16[64,5,8,128]{3,2,1,0:T(8,128)(2,1)} %layers.1), calls=%async_computation.1 | async-start | bytes 1310720 | tf_op jit(solution)/shard_map/all_to_all | solution.py:286
  73.1 21.0 %all-to-all-done.1.got_ref = bf16[64,5,8,128]{3,2,1,0:T(8,128)(2,1)S(1)} async-done(((bf16[64,5,8,128]{3,2,1,0:T(8,128)(2,1)}), bf16[64,5,8,128]{3,2,1,0:T(8,128)(2,1)S(1)}, u32[]{:S(2)}, u32[]{:S(2)}) %all-to-all-start.1) | async-done | bytes 655392 | tf_op jit(solution)/shard_map/all_to_all | solution.py:286
  94.1 9.3 %first_bags.1 = (bf16[4,4,2,128,128]{4,3,2,1,0:T(8,128)(2,1)}, bf16[8,256,256]{2,1,0:T(8,128)(2,1)S(1)}, f32[8,8,256]{2,1,0:T(8,128)S(1)}, f32[8,8,256]{2,1,0:T(8,128)S(1)}) custom-call(bf16[64,5,8,128]{3,2,1,0:T(8,128)(2,1)S(1)} %all-to-all-done.1.got_ref), custom_call_target="tpu_custom_call" | custom-call | flops 10000000000 | bytes 4194304 | tf_op jit(solution)/shard_map/first_bags/pallas_call | solution.py:218
  103.4 4.0 %all-to-all-start.2 = ((bf16[4,4,2,128,128]{4,3,2,1,0:T(8,128)(2,1)}), bf16[4,4,2,128,128]{4,3,2,1,0:T(8,128)(2,1)S(1)}, u32[]{:S(2)}, u32[]{:S(2)}) async-start(bf16[4,4,2,128,128]{4,3,2,1,0:T(8,128)(2,1)} %get-tuple-element.18), calls=%async_computation.2 | async-start | bytes 2097152 | tf_op jit(solution)/shard_map/all_to_all | solution.py:291
  107.4 7.6 %second_bags.1 = (bf16[4,2,128,128]{3,2,1,0:T(8,128)(2,1)S(1)}, bf16[4,2,128,128]{3,2,1,0:T(8,128)(2,1)S(1)}, bf16[4,2,128,128]{3,2,1,0:T(8,128)(2,1)S(1)}, bf16[4,2,128,128]{3,2,1,0:T(8,128)(2,1)S(1)}) custom-call(s32[1]{0:T(128)} %bitcast.6.shift_ref, bf16[8,256,256]{2,1,0:T(8,128)(2,1)S(1)} %get-tuple-element.19.grads_ref, ...), custom_call_target="tpu_custom_call" | custom-call | flops 10000000000 | bytes 4194304 | tf_op jit(solution)/shard_map/second_bags/pallas_call | solution.py:236
  115.1 6.9 %all-to-all-done.2 = bf16[4,4,2,128,128]{4,3,2,1,0:T(8,128)(2,1)S(1)} async-done(((bf16[4,4,2,128,128]{4,3,2,1,0:T(8,128)(2,1)}), bf16[4,4,2,128,128]{4,3,2,1,0:T(8,128)(2,1)S(1)}, u32[]{:S(2)}, u32[]{:S(2)}) %all-to-all-start.2) | async-done | bytes 1048608 | tf_op jit(solution)/shard_map/all_to_all | solution.py:291
  122.0 0.9 reduce_sum.50
  122.9 4.1 %all-to-all-start.3 = ((bf16[4,2,128,128]{3,2,1,0:T(8,128)(2,1)}), bf16[4,2,128,128]{3,2,1,0:T(8,128)(2,1)S(1)}, u32[]{:S(2)}, u32[]{:S(2)}) async-start(bf16[4,2,128,128]{3,2,1,0:T(8,128)(2,1)} %reduce_sum.50), calls=%async_computation.3 | async-start | bytes 524288 | tf_op jit(solution)/shard_map/all_to_all | solution.py:294
  127.0 2.2 %collective-permute-start = (bf16[4,2,128,128]{3,2,1,0:T(8,128)(2,1)S(1)}, bf16[4,2,128,128]{3,2,1,0:T(8,128)(2,1)S(1)}, u32[]{:S(2)}, u32[]{:S(2)}) collective-permute-start(bf16[4,2,128,128]{3,2,1,0:T(8,128)(2,1)S(1)} %get-tuple-element.28), channel_id=1, source_target_pairs={{0,1},{1,2},{2,3},{3,0},{4,5},{5,6},{6,7},{7,4},{8,9},{9,10},{10,1... | collective-permute-start | bytes 786440 | tf_op jit(solution)/shard_map/ppermute | solution.py:298
  129.2 3.7 %collective-permute-start.1 = (bf16[4,2,128,128]{3,2,1,0:T(8,128)(2,1)S(1)}, bf16[4,2,128,128]{3,2,1,0:T(8,128)(2,1)S(1)}, u32[]{:S(2)}, u32[]{:S(2)}) collective-permute-start(bf16[4,2,128,128]{3,2,1,0:T(8,128)(2,1)S(1)} %get-tuple-element.29), channel_id=1, source_target_pairs={{0,2},{1,3},{2,0},{3,1},{4,6},{5,7},{6,4},{7,5},{8,10},{9,11},{10,... | collective-permute-start | bytes 786440 | tf_op jit(solution)/shard_map/ppermute | solution.py:298
  132.9 2.5 %collective-permute-start.2 = (bf16[4,2,128,128]{3,2,1,0:T(8,128)(2,1)S(1)}, bf16[4,2,128,128]{3,2,1,0:T(8,128)(2,1)S(1)}, u32[]{:S(2)}, u32[]{:S(2)}) collective-permute-start(bf16[4,2,128,128]{3,2,1,0:T(8,128)(2,1)S(1)} %get-tuple-element.30), channel_id=1, source_target_pairs={{0,3},{1,0},{2,1},{3,2},{4,7},{5,4},{6,5},{7,6},{8,11},{9,8},{10,9... | collective-permute-start | bytes 786440 | tf_op jit(solution)/shard_map/ppermute | solution.py:298
  135.4 1.3 collective-permute-done
  136.7 4.4 %collective-permute-done.1 = bf16[4,2,128,128]{3,2,1,0:T(8,128)(2,1)S(1)} collective-permute-done((bf16[4,2,128,128]{3,2,1,0:T(8,128)(2,1)S(1)}, bf16[4,2,128,128]{3,2,1,0:T(8,128)(2,1)S(1)}, u32[]{:S(2)}, u32[]{:S(2)}) %collective-permute-start.1) | collective-permute-done | bytes 262176 | tf_op jit(solution)/shard_map/ppermute | solution.py:298
  141.1 3.8 %collective-permute-done.2 = bf16[4,2,128,128]{3,2,1,0:T(8,128)(2,1)S(1)} collective-permute-done((bf16[4,2,128,128]{3,2,1,0:T(8,128)(2,1)S(1)}, bf16[4,2,128,128]{3,2,1,0:T(8,128)(2,1)S(1)}, u32[]{:S(2)}, u32[]{:S(2)}) %collective-permute-start.2) | collective-permute-done | bytes 262176 | tf_op jit(solution)/shard_map/ppermute | solution.py:298
  144.8 0.8 add_convert_fusion
  145.7 11.2 %all-to-all-start.4 = ((bf16[4,2,128,128]{3,2,1,0:T(8,128)(2,1)}), bf16[4,2,128,128]{3,2,1,0:T(8,128)(2,1)S(1)}, u32[]{:S(2)}, u32[]{:S(2)}) async-start(bf16[4,2,128,128]{3,2,1,0:T(8,128)(2,1)} %add_convert_fusion), calls=%async_computation.4 | async-start | bytes 524288 | tf_op jit(solution)/shard_map/all_to_all | solution.py:300
  156.9 15.8 %all-to-all-done.4 = bf16[4,2,128,128]{3,2,1,0:T(8,128)(2,1)S(1)} async-done(((bf16[4,2,128,128]{3,2,1,0:T(8,128)(2,1)}), bf16[4,2,128,128]{3,2,1,0:T(8,128)(2,1)S(1)}, u32[]{:S(2)}, u32[]{:S(2)}) %all-to-all-start.4) | async-done | bytes 262176 | tf_op jit(solution)/shard_map/all_to_all | solution.py:300
  172.7 0.7 pad_maximum_fusion.1
  (21 shorter events, 0.7 us)
Async XLA Ops:
  2.1 21.3 %copy-start.3 = (bf16[2,512,32]{1,2,0:T(8,128)(2,1)S(1)}, bf16[2,512,32]{1,2,0:T(8,128)(2,1)}, u32[]{:S(2)}) copy-start(bf16[2,512,32]{1,2,0:T(8,128)(2,1)} %param.13) | copy-start | bytes 196612
  2.2 38.8 %copy-start = (bf16[2,512,512]{2,1,0:T(8,128)(2,1)S(1)}, bf16[2,512,512]{2,1,0:T(8,128)(2,1)}, u32[]{:S(2)}) copy-start(bf16[2,512,512]{2,1,0:T(8,128)(2,1)} %compress_ref.1) | copy-start | bytes 3145732
  2.2 38.8 %copy-start.1 = (bf16[2,32,128]{2,1,0:T(8,128)(2,1)S(1)}, bf16[2,32,128]{2,1,0:T(8,128)(2,1)}, u32[]{:S(2)}) copy-start(bf16[2,32,128]{2,1,0:T(8,128)(2,1)} %output_ref.1) | copy-start | bytes 49156
  2.2 38.7 %copy-start.2 = (f32[2,128]{1,0:T(2,128)S(1)}, f32[2,128]{1,0:T(2,128)}, u32[]{:S(2)}) copy-start(f32[2,128]{1,0:T(2,128)} %gain_ref.1) | copy-start | bytes 3076
  4.2 36.7 %all-to-all-start = ((bf16[4,560,128]{2,1,0:T(8,128)(2,1)}), bf16[4,560,128]{2,1,0:T(8,128)(2,1)S(1)}, u32[]{:S(2)}, u32[]{:S(2)}) async-start(bf16[4,560,128]{2,1,0:T(8,128)(2,1)} %pad_maximum_fusion), calls=%async_computation | async-start | bytes 1146880 | tf_op jit(solution)/shard_map/all_to_all | solution.py:284
  46.2 47.9 %all-to-all-start.1 = ((bf16[64,5,8,128]{3,2,1,0:T(8,128)(2,1)}), bf16[64,5,8,128]{3,2,1,0:T(8,128)(2,1)S(1)}, u32[]{:S(2)}, u32[]{:S(2)}) async-start(bf16[64,5,8,128]{3,2,1,0:T(8,128)(2,1)} %layers.1), calls=%async_computation.1 | async-start | bytes 1310720 | tf_op jit(solution)/shard_map/all_to_all | solution.py:286
  103.4 18.5 %all-to-all-start.2 = ((bf16[4,4,2,128,128]{4,3,2,1,0:T(8,128)(2,1)}), bf16[4,4,2,128,128]{4,3,2,1,0:T(8,128)(2,1)S(1)}, u32[]{:S(2)}, u32[]{:S(2)}) async-start(bf16[4,4,2,128,128]{4,3,2,1,0:T(8,128)(2,1)} %get-tuple-element.18), calls=%async_computation.2 | async-start | bytes 2097152 | tf_op jit(solution)/shard_map/all_to_all | solution.py:291
  122.9 22.8 %all-to-all-start.3 = ((bf16[4,2,128,128]{3,2,1,0:T(8,128)(2,1)}), bf16[4,2,128,128]{3,2,1,0:T(8,128)(2,1)S(1)}, u32[]{:S(2)}, u32[]{:S(2)}) async-start(bf16[4,2,128,128]{3,2,1,0:T(8,128)(2,1)} %reduce_sum.50), calls=%async_computation.3 | async-start | bytes 524288 | tf_op jit(solution)/shard_map/all_to_all | solution.py:294
  127.0 9.7 %collective-permute-start = (bf16[4,2,128,128]{3,2,1,0:T(8,128)(2,1)S(1)}, bf16[4,2,128,128]{3,2,1,0:T(8,128)(2,1)S(1)}, u32[]{:S(2)}, u32[]{:S(2)}) collective-permute-start(bf16[4,2,128,128]{3,2,1,0:T(8,128)(2,1)S(1)} %get-tuple-element.28), channel_id=1, source_target_pairs={{0,1},{1,2},{2,3},{3,0},{4,5},{5,6},{6,7},{7,4},{8,9},{9,10},{10,1... | collective-permute-start | bytes 786440 | tf_op jit(solution)/shard_map/ppermute | solution.py:298
  129.2 11.9 %collective-permute-start.1 = (bf16[4,2,128,128]{3,2,1,0:T(8,128)(2,1)S(1)}, bf16[4,2,128,128]{3,2,1,0:T(8,128)(2,1)S(1)}, u32[]{:S(2)}, u32[]{:S(2)}) collective-permute-start(bf16[4,2,128,128]{3,2,1,0:T(8,128)(2,1)S(1)} %get-tuple-element.29), channel_id=1, source_target_pairs={{0,2},{1,3},{2,0},{3,1},{4,6},{5,7},{6,4},{7,5},{8,10},{9,11},{10,... | collective-permute-start | bytes 786440 | tf_op jit(solution)/shard_map/ppermute | solution.py:298
  132.9 12.0 %collective-permute-start.2 = (bf16[4,2,128,128]{3,2,1,0:T(8,128)(2,1)S(1)}, bf16[4,2,128,128]{3,2,1,0:T(8,128)(2,1)S(1)}, u32[]{:S(2)}, u32[]{:S(2)}) collective-permute-start(bf16[4,2,128,128]{3,2,1,0:T(8,128)(2,1)S(1)} %get-tuple-element.30), channel_id=1, source_target_pairs={{0,3},{1,0},{2,1},{3,2},{4,7},{5,4},{6,5},{7,6},{8,11},{9,8},{10,9... | collective-permute-start | bytes 786440 | tf_op jit(solution)/shard_map/ppermute | solution.py:298
  145.7 27.0 %all-to-all-start.4 = ((bf16[4,2,128,128]{3,2,1,0:T(8,128)(2,1)}), bf16[4,2,128,128]{3,2,1,0:T(8,128)(2,1)S(1)}, u32[]{:S(2)}, u32[]{:S(2)}) async-start(bf16[4,2,128,128]{3,2,1,0:T(8,128)(2,1)} %add_convert_fusion), calls=%async_computation.4 | async-start | bytes 524288 | tf_op jit(solution)/shard_map/all_to_all | solution.py:300

commit v3 on v2

--- a/solution.py
+++ b/solution.py
@@ -172,16 +172,14 @@
             grads_ref[cap // 2, rows, D:] = (values * table).astype(bf16)
 
 
-def add_rows(first, amount, shift, out_refs, grads_ref, high_ref, low_ref):
+def add_rows(first, amount, groups, out_ref, grads_ref, high_ref, low_ref):
     lanes = 2 * PAIR * DP
     rows_of = (iota((amount, lanes), 0) + first).astype(f32).astype(bf16)
     one = jnp.ones((), bf16)
     zero = jnp.zeros((), bf16)
 
     def block(s, carry):
-        for r in range(N_GRP):
-            group = shift + r
-            group = jnp.where(group >= N_GRP, group - N_GRP, group)
+        for r, group in enumerate(groups):
             want = (s * N_GRP + group).astype(f32)
             total = jnp.zeros((amount, 2 * D), f32)
             for p in range(N_SLOT * CAPACITY // 2):
@@ -192,56 +190,123 @@
                     wanted = jnp.broadcast_to(wanted[None], (amount // 16, 16, lanes)).reshape(amount, lanes)
                     count = count + jnp.where(rows_of == wanted, one, zero)
                 total = total + dot(count, grads_ref[p])
-            out_refs[r][s, 0] = total[:, :D].astype(bf16)
-            out_refs[r][s, 1] = total[:, D:].astype(bf16)
+            out_ref[r, s, 0] = total[:, :D].astype(bf16)
+            out_ref[r, s, 1] = total[:, D:].astype(bf16)
         return carry
 
     lax.fori_loop(0, N_SLOT, block, 0)
 
 
-def first_bags_kernel(amount, got_ref, out_ref, grads_ref, high_ref, low_ref, wide_ref):
+def first_bags_kernel(amount, groups_ref, got_ref, out_ref, grads_ref, high_ref, low_ref, wide_ref):
     prepare_bags(got_ref, wide_ref, grads_ref, high_ref, low_ref)
-    outs = [out_ref.at[r] for r in range(N_GRP)]
-    add_rows(0, amount, jnp.int32(0), outs, grads_ref, high_ref, low_ref)
-
-
-def second_bags_kernel(first, amount, shift_ref, grads_ref, high_ref, low_ref, *out_refs):
-    add_rows(first, amount, shift_ref[0], out_refs, grads_ref, high_ref, low_ref)
+    groups = [groups_ref[0], groups_ref[1]]
+    add_rows(0, amount, groups, out_ref, grads_ref, high_ref, low_ref)
+
+
+def later_bags_kernel(first, amount, groups_ref, grads_ref, high_ref, low_ref, out_ref):
+    groups = [groups_ref[0], groups_ref[1]]
+    add_rows(first, amount, groups, out_ref, grads_ref, high_ref, low_ref)
 
 
 VMEM_SPEC = pl.BlockSpec(memory_space=pltpu.VMEM)
-
-
-def run_first_bags(got, amount):
+SMEM_SPEC = pl.BlockSpec(memory_space=pltpu.SMEM)
+BAGS_COST = pl.CostEstimate(flops=200_000_000, bytes_accessed=1 << 20, transcendentals=0)
+ADD_COST = pl.CostEstimate(flops=1_000_000, bytes_accessed=1 << 20, transcendentals=0)
+
+
+def part_shape(amount):
+    return jax.ShapeDtypeStruct((2, N_SLOT, TABLE_DEV, amount, D), bf16)
+
+
+def run_first_bags(groups, got, amount):
     pairs = N_SLOT * CAPACITY // 2
     lanes = 2 * PAIR * DP
     return pl.pallas_call(
         functools.partial(first_bags_kernel, amount),
         out_shape=(
-            jax.ShapeDtypeStruct((N_GRP, N_SLOT, TABLE_DEV, amount, D), bf16),
+            part_shape(amount),
             jax.ShapeDtypeStruct((pairs, lanes, 2 * D), bf16),
             jax.ShapeDtypeStruct((pairs, BAG, lanes), f32),
             jax.ShapeDtypeStruct((pairs, BAG, lanes), f32),
         ),
-        in_specs=[VMEM_SPEC],
+        in_specs=[SMEM_SPEC, VMEM_SPEC],
         out_specs=(VMEM_SPEC,) * 4,
         scratch_shapes=[pltpu.VMEM((DP * 8, D), f32)],
         compiler_params=pltpu.CompilerParams(vmem_limit_bytes=32 << 20),
-        cost_estimate=pl.CostEstimate(flops=10_000_000_000, bytes_accessed=4 << 20, transcendentals=0),
+        cost_estimate=BAGS_COST,
         name="first_bags",
+    )(groups, got)
+
+
+def run_later_bags(groups, prepared, first, amount, name):
+    return pl.pallas_call(
+        functools.partial(later_bags_kernel, first, amount),
+        out_shape=part_shape(amount),
+        in_specs=[SMEM_SPEC] + [VMEM_SPEC] * 3,
+        out_specs=VMEM_SPEC,
+        compiler_params=pltpu.CompilerParams(vmem_limit_bytes=32 << 20),
+        cost_estimate=BAGS_COST,
+        name=name,
+    )(groups, *prepared)
+
+
+def add_parts_kernel(kept_ref, got_ref, own_ref, sent_ref):
+    for s in range(N_SLOT):
+        own_ref[s] = (kept_ref[0, s].astype(f32) + got_ref[0, s].astype(f32)).astype(bf16)
+        sent_ref[s] = (kept_ref[1, s].astype(f32) + got_ref[1, s].astype(f32)).astype(bf16)
+
+
+def add_parts(kept, got, name):
+    one = jax.ShapeDtypeStruct(kept.shape[1:], bf16)
+    return pl.pallas_call(
+        add_parts_kernel,
+        out_shape=(one, one),
+        in_specs=[VMEM_SPEC] * 2,
+        out_specs=(VMEM_SPEC,) * 2,
+        compiler_params=pltpu.CompilerParams(vmem_limit_bytes=8 << 20),
+        cost_estimate=ADD_COST,
+        name=name,
+    )(kept, got)
+
+
+def join_kernel(low_ref, low_last_ref, high_ref, high_last_ref, out_ref):
+    for s in range(N_SLOT):
+        out_ref[s, 0] = (low_ref[s].astype(f32) + low_last_ref[s].astype(f32)).astype(bf16)
+        out_ref[s, 1] = (high_ref[s].astype(f32) + high_last_ref[s].astype(f32)).astype(bf16)
+
+
+def join_parts(*parts):
+    shape = (parts[0].shape[0], 2, *parts[0].shape[1:])
+    return pl.pallas_call(
+        join_kernel,
+        out_shape=jax.ShapeDtypeStruct(shape, bf16),
+        in_specs=[VMEM_SPEC] * 4,
+        out_specs=VMEM_SPEC,
+        compiler_params=pltpu.CompilerParams(vmem_limit_bytes=8 << 20),
+        cost_estimate=ADD_COST,
+        name="join_parts",
+    )(*parts)
+
+
+def final_kernel(got_ref, out_ref):
+    for half in range(2):
+        for t in range(TABLE_DEV):
+            total = got_ref[0, half, t].astype(f32)
+            for s in range(1, N_SLOT):
+                total = total + got_ref[s, half, t].astype(f32)
+            out_ref[t, half] = total
+
+
+def final_sum(got):
+    return pl.pallas_call(
+        final_kernel,
+        out_shape=jax.ShapeDtypeStruct((TABLE_DEV, 2, ROW_BLOCK // 2, D), f32),
+        in_specs=[VMEM_SPEC],
+        out_specs=VMEM_SPEC,
+        compiler_params=pltpu.CompilerParams(vmem_limit_bytes=8 << 20),
+        cost_estimate=ADD_COST,
+        name="final_sum",
     )(got)
-
-
-def run_second_bags(shift, grads, high, low, first, amount):
-    return pl.pallas_call(
-        functools.partial(second_bags_kernel, first, amount),
-        out_shape=(jax.ShapeDtypeStruct((N_SLOT, TABLE_DEV, amount, D), bf16),) * N_GRP,
-        in_specs=[pl.BlockSpec(memory_space=pltpu.SMEM)] + [VMEM_SPEC] * 3,
-        out_specs=(VMEM_SPEC,) * N_GRP,
-        compiler_params=pltpu.CompilerParams(vmem_limit_bytes=32 << 20),
-        cost_estimate=pl.CostEstimate(flops=10_000_000_000, bytes_accessed=4 << 20, transcendentals=0),
-        name="second_bags",
-    )(shift, grads, high, low)
 
 
 def per_device(
@@ -285,22 +350,25 @@
     sent = run_layers(messages, compress_weight, fm_basis, fm_output, norm_gain)
     got = lax.all_to_all(sent, "dp", split_axis=0, concat_axis=0, tiled=True)
     half = ROW_BLOCK // 2
-    first, grads, high_ids, low_ids = run_first_bags(got, half)
-    shift = lax.axis_index("grp").astype(jnp.int32).reshape(1)
-    second = run_second_bags(shift, grads, high_ids, low_ids, half, half)
-    first = lax.all_to_all(first, "grp", split_axis=0, concat_axis=0, tiled=True)
-    first = jnp.sum(first.astype(f32), axis=0).astype(bf16)
-    first, second = lax.optimization_barrier((first, second))
-    first = lax.all_to_all(first, "slot", split_axis=0, concat_axis=0, tiled=True)
-    pieces = [second[0]]
-    for step in range(1, N_GRP):
-        moves = [(i, (i + step) % N_GRP) for i in range(N_GRP)]
-        pieces.append(lax.ppermute(second[step], "grp", moves))
-    second = sum(piece.astype(f32) for piece in pieces).astype(bf16)
-    second = lax.all_to_all(second, "slot", split_axis=0, concat_axis=0, tiled=True)
-    return jnp.concatenate(
-        [jnp.sum(first.astype(f32), axis=0), jnp.sum(second.astype(f32), axis=0)], axis=1
-    )
+    me = lax.axis_index("grp").astype(jnp.int32)
+    side = me ^ 1
+    mirror = N_GRP - 1 - me
+    across = side ^ 3
+    side_moves = [(i, i ^ 1) for i in range(N_GRP)]
+    mirror_moves = [(i, N_GRP - 1 - i) for i in range(N_GRP)]
+    low_sent, *prepared = run_first_bags(jnp.stack([side, across]), got, half)
+    low_got = lax.ppermute(low_sent, "grp", side_moves)
+    high_sent = run_later_bags(jnp.stack([mirror, across]), prepared, half, half, "high_sent")
+    high_got = lax.ppermute(high_sent, "grp", mirror_moves)
+    low_kept = run_later_bags(jnp.stack([me, mirror]), prepared, 0, half, "low_kept")
+    low, low_next = add_parts(low_kept, low_got, "low_parts")
+    low_last = lax.ppermute(low_next, "grp", mirror_moves)
+    high_kept = run_later_bags(jnp.stack([me, side]), prepared, half, half, "high_kept")
+    high, high_next = add_parts(high_kept, high_got, "high_parts")
+    high_last = lax.ppermute(high_next, "grp", side_moves)
+    totals = join_parts(low, low_last, high, high_last)
+    totals = lax.all_to_all(totals, "slot", split_axis=0, concat_axis=0, tiled=True)
+    return final_sum(totals).reshape(TABLE_DEV, ROW_BLOCK, D)
 
 
 def solution(mesh):

time: 177 us -> 167 us (0.944)
  blocking collectives: 0 us -> 31.7 us
  waiting for transfers between devices: 70.4 us -> 44.6 us
  starting transfers between devices: 73.8 us -> 57.7 us
  Pallas kernels: 22.2 us -> 25.5 us
  other arithmetic: 6.37 us -> 4.11 us
    all_to_all x0 -> x1, blocking collectives: none -> 31.7 us  [per_device(): lax.all_to_all(totals, 'slot', split_axis=0, concat_axis=0, tiled=True)]
    all_to_all x3 -> x0, waiting for transfers between devices: 22.6 us -> none  [the longest x1 15.8 us: per_device(): lax.all_to_all(second, 'slot', split_axis=0, concat_axis=0, tiled=True)]
    all_to_all x3 -> x0, starting transfers between devices: 19.3 us -> none  [the longest x1 11.2 us: per_device(): lax.all_to_all(second, 'slot', split_axis=0, concat_axis=0, tiled=True)]
    pallas_call x2 -> x8, Pallas kernels: 17 us -> 20.3 us  [the longest x3 13.8 us: run_later_bags(): pl.pallas_call(functools.partial(later_bags_kernel, first, amount), out_s...]
    ppermute x3 -> x4, starting transfers between devices: 8.4 us -> 11.5 us  [the longest x1 3.73 us: per_device(): high_got = lax.ppermute(high_sent, 'grp', mirror_moves)]
    ppermute x3 -> x4, waiting for transfers between devices: 9.43 us -> 6.37 us  [the longest x1 5.12 us: per_device(): low_last = lax.ppermute(low_next, 'grp', mirror_moves)]
  transfers between devices with their start and end apart: 8 -> 6, of which waited for: 7 -> 4; matrix products, arithmetic and copies ran while one was open for 1% -> 0% of each run, Pallas kernels for 4% -> 9%
where the time goes in v3:
time: 167 us; the launch traced here: 164 us
  starting transfers between devices  57.7 us (35%)
  waiting for transfers between devices  44.6 us (27%)
  blocking collectives  31.7 us (19%)
  Pallas kernels  25.5 us (15%)
  other arithmetic  4.11 us (2%)
    all_to_all x1, blocking collectives, per_device(): lax.all_to_all(totals, 'slot', split_axis=0, concat_axis=0, tiled=True)  31.7 us
    all_to_all x1, starting transfers between devices, per_device(): got = lax.all_to_all(sent, 'dp', split_axis=0, concat_axis=0, tiled=True)  26.9 us
    all_to_all x1, waiting for transfers between devices, per_device(): got = lax.all_to_all(sent, 'dp', split_axis=0, concat_axis=0, tiled=True)  20.9 us
    all_to_all x1, starting transfers between devices, per_device(): lax.all_to_all(messages, 'slot', split_axis=0, concat_axis=0, tiled=True)  19.3 us
    all_to_all x1, waiting for transfers between devices, per_device(): lax.all_to_all(messages, 'slot', split_axis=0, concat_axis=0, tiled=True)  17.3 us
    pallas_call x3, Pallas kernels, run_later_bags(): pl.pallas_call(functools.partial(later_bags_kernel, first, amount), out_s...  13.8 us
    pallas_call x1, Pallas kernels, run_first_bags(): pl.pallas_call(functools.partial(first_bags_kernel, amount), out_shape=(p...  5.32 us
    pallas_call x1, Pallas kernels, run_layers(): pl.pallas_call(layers_kernel, out_shape=jax.ShapeDtypeStruct((DP, N_SLOT...  5.26 us
  transfers between devices with their start and end apart: 6, of which 4 were waited for; matrix products, arithmetic and copies ran while one was open for 0% of the time, Pallas kernels for 9%

profile of v3, /device:TPU:1, one launch (start us, length us, event | category | flops | bytes accessed | tf_op | source)
XLA Modules:
  0.0 164.3 jit_solution(18330732318754772415)
XLA Ops:
  0.0 0.8 select_reduce_fusion
  0.9 0.2 convert_reduce_fusion
  1.1 0.8 fusion.8
  2.2 2.0 %pad_maximum_fusion = bf16[4,560,128]{2,1,0:T(8,128)(2,1)} fusion(bf16[4,16,128]{2,1,0:T(8,128)(2,1)S(1)} %broadcast_in_dim.21, bf16[4,32,128]{2,1,0:T(8,128)(2,1)S(1)} %copy.18, bf16[4,256,128]{2,1,0:T(8,128)(2,1)} %bitcast.19, bf16[4,256,128]{2,1,0:T(8,128)(2,1)} %bitcast.20), kind=kLoop, calls=%fused_computation | loop fusion | flops 2293760 | bytes 1146880 | tf_op jit(solution)/shard_map/concatenate | solution.py:340
  4.2 19.3 %all-to-all-start = ((bf16[4,560,128]{2,1,0:T(8,128)(2,1)}), bf16[4,560,128]{2,1,0:T(8,128)(2,1)S(1)}, u32[]{:S(2)}, u32[]{:S(2)}) async-start(bf16[4,560,128]{2,1,0:T(8,128)(2,1)} %pad_maximum_fusion), calls=%async_computation | async-start | bytes 1146880 | tf_op jit(solution)/shard_map/all_to_all | solution.py:349
  23.4 0.2 copy.19.basis_ref
  23.6 17.3 %all-to-all-done.x_ref = bf16[4,560,128]{2,1,0:T(8,128)(2,1)S(1)} async-done(((bf16[4,560,128]{2,1,0:T(8,128)(2,1)}), bf16[4,560,128]{2,1,0:T(8,128)(2,1)S(1)}, u32[]{:S(2)}, u32[]{:S(2)}) %all-to-all-start) | async-done | bytes 573472 | tf_op jit(solution)/shard_map/all_to_all | solution.py:349
  40.9 5.3 %layers.1 = bf16[64,5,8,128]{3,2,1,0:T(8,128)(2,1)} custom-call(bf16[4,560,128]{2,1,0:T(8,128)(2,1)S(1)} %all-to-all-done.x_ref, bf16[2,512,512]{2,1,0:T(8,128)(2,1)S(1)} %copy-done, bf16[2,512,32]{2,1,0:T(8,128)(2,1)S(1)} %copy.19.basis_ref, bf16[2,32,128]{2,1,0:T(8,128)(2,1)S(1)} %copy-done.1, f32[2,128]{1,0:T(2,128)S(1)} %copy-done.2), custom_call_target="tpu_custom_call" | custom-call | flops 2000000000 | bytes 4194304 | tf_op jit(solution)/shard_map/layers/pallas_call | solution.py:133
  46.2 26.9 %all-to-all-start.1 = ((bf16[64,5,8,128]{3,2,1,0:T(8,128)(2,1)}), bf16[64,5,8,128]{3,2,1,0:T(8,128)(2,1)S(1)}, u32[]{:S(2)}, u32[]{:S(2)}) async-start(bf16[64,5,8,128]{3,2,1,0:T(8,128)(2,1)} %layers.1), calls=%async_computation.1 | async-start | bytes 1310720 | tf_op jit(solution)/shard_map/all_to_all | solution.py:351
  73.2 20.9 %all-to-all-done.1.got_ref = bf16[64,5,8,128]{3,2,1,0:T(8,128)(2,1)S(1)} async-done(((bf16[64,5,8,128]{3,2,1,0:T(8,128)(2,1)}), bf16[64,5,8,128]{3,2,1,0:T(8,128)(2,1)S(1)}, u32[]{:S(2)}, u32[]{:S(2)}) %all-to-all-start.1) | async-done | bytes 655392 | tf_op jit(solution)/shard_map/all_to_all | solution.py:351
  94.1 5.3 %first_bags.1 = (bf16[2,4,2,128,128]{4,3,2,1,0:T(8,128)(2,1)S(1)}, bf16[8,256,256]{2,1,0:T(8,128)(2,1)S(1)}, f32[8,8,256]{2,1,0:T(8,128)S(1)}, f32[8,8,256]{2,1,0:T(8,128)S(1)}) custom-call(s32[2]{0:T(128)S(1)} %pad_add_fusion.1.groups_ref, bf16[64,5,8,128]{3,2,1,0:T(8,128)(2,1)S(1)} %all-to-all-done.1.got_ref), custom_call_target="tpu_custom_call" | custom-call | flops 200000000 | bytes 1048576 | tf_op jit(solution)/shard_map/first_bags/pallas_call | solution.py:224
  99.4 3.1 %collective-permute-start = (bf16[2,4,2,128,128]{4,3,2,1,0:T(8,128)(2,1)S(1)}, bf16[2,4,2,128,128]{4,3,2,1,0:T(8,128)(2,1)S(1)}, u32[]{:S(2)}, u32[]{:S(2)}) collective-permute-start(bf16[2,4,2,128,128]{4,3,2,1,0:T(8,128)(2,1)S(1)} %get-tuple-element.16), channel_id=1, source_target_pairs={{0,1},{1,0},{2,3},{3,2},{4,5},{5,4},{6,7},{7,6},{8,9},{9,8},{10,11... | collective-permute-start | bytes 1572872 | tf_op jit(solution)/shard_map/ppermute | solution.py:360
  102.6 4.6 %high_sent.1 = bf16[2,4,2,128,128]{4,3,2,1,0:T(8,128)(2,1)S(1)} custom-call(s32[2]{0:T(128)S(1)} %pad_add_fusion.3.groups_ref, bf16[8,256,256]{2,1,0:T(8,128)(2,1)S(1)} %get-tuple-element.13.grads_ref, f32[8,8,256]{2,1,0:T(8,128)S(1)} %get-tuple-element.14.high_ref, f32[8,8,256]{2,1,0:T(8,128)S(1)} %get-tuple-element.15.low_ref), custom_call_target="tpu_custom_call" | custom-call | flops 200000000 | bytes 1048576 | tf_op jit(solution)/shard_map/high_sent/pallas_call | solution.py:242
  107.2 3.7 %collective-permute-start.2 = (bf16[2,4,2,128,128]{4,3,2,1,0:T(8,128)(2,1)S(1)}, bf16[2,4,2,128,128]{4,3,2,1,0:T(8,128)(2,1)S(1)}, u32[]{:S(2)}, u32[]{:S(2)}) collective-permute-start(bf16[2,4,2,128,128]{4,3,2,1,0:T(8,128)(2,1)S(1)} %high_sent.1), channel_id=1, source_target_pairs={{0,3},{1,2},{2,1},{3,0},{4,7},{5,6},{6,5},{7,4},{8,11},{9,10},{10,... | collective-permute-start | bytes 1572872 | tf_op jit(solution)/shard_map/ppermute | solution.py:362
  111.1 4.6 %low_kept.1.kept_ref = bf16[2,4,2,128,128]{4,3,2,1,0:T(8,128)(2,1)S(1)} custom-call(s32[2]{0:T(128)S(1)} %pad_add_fusion.groups_ref, bf16[8,256,256]{2,1,0:T(8,128)(2,1)S(1)} %get-tuple-element.13.grads_ref, f32[8,8,256]{2,1,0:T(8,128)S(1)} %get-tuple-element.14.high_ref, f32[8,8,256]{2,1,0:T(8,128)S(1)} %get-tuple-element.15.low_ref), custom_call_target="tpu_custom_call" | custom-call | flops 200000000 | bytes 1048576 | tf_op jit(solution)/shard_map/low_kept/pallas_call | solution.py:242
  115.7 4.6 %high_kept.1.kept_ref = bf16[2,4,2,128,128]{4,3,2,1,0:T(8,128)(2,1)S(1)} custom-call(s32[2]{0:T(128)S(1)} %pad_add_fusion.2.groups_ref, bf16[8,256,256]{2,1,0:T(8,128)(2,1)S(1)} %get-tuple-element.13.grads_ref, f32[8,8,256]{2,1,0:T(8,128)S(1)} %get-tuple-element.14.high_ref, f32[8,8,256]{2,1,0:T(8,128)S(1)} %get-tuple-element.15.low_ref), custom_call_target="tpu_custom_call" | custom-call | flops 200000000 | bytes 1048576 | tf_op jit(solution)/shard_map/high_kept/pallas_call | solution.py:242
  120.3 0.1 low_parts.1
  120.4 2.8 %collective-permute-start.1 = (bf16[4,2,128,128]{3,2,1,0:T(8,128)(2,1)S(1)}, bf16[4,2,128,128]{3,2,1,0:T(8,128)(2,1)S(1)}, u32[]{:S(2)}, u32[]{:S(2)}) collective-permute-start(bf16[4,2,128,128]{3,2,1,0:T(8,128)(2,1)S(1)} %get-tuple-element.18), channel_id=1, source_target_pairs={{0,3},{1,2},{2,1},{3,0},{4,7},{5,6},{6,5},{7,4},{8,11},{9,10},{10,... | collective-permute-start | bytes 786440 | tf_op jit(solution)/shard_map/ppermute | solution.py:365
  123.2 0.1 high_parts.1
  123.4 1.9 %collective-permute-start.3 = (bf16[4,2,128,128]{3,2,1,0:T(8,128)(2,1)S(1)}, bf16[4,2,128,128]{3,2,1,0:T(8,128)(2,1)S(1)}, u32[]{:S(2)}, u32[]{:S(2)}) collective-permute-start(bf16[4,2,128,128]{3,2,1,0:T(8,128)(2,1)S(1)} %get-tuple-element.20), channel_id=1, source_target_pairs={{0,1},{1,0},{2,3},{3,2},{4,5},{5,4},{6,7},{7,6},{8,9},{9,8},{10,11... | collective-permute-start | bytes 786440 | tf_op jit(solution)/shard_map/ppermute | solution.py:368
  125.3 5.1 %collective-permute-done.1.low_last_ref = bf16[4,2,128,128]{3,2,1,0:T(8,128)(2,1)S(1)} collective-permute-done((bf16[4,2,128,128]{3,2,1,0:T(8,128)(2,1)S(1)}, bf16[4,2,128,128]{3,2,1,0:T(8,128)(2,1)S(1)}, u32[]{:S(2)}, u32[]{:S(2)}) %collective-permute-start.1) | collective-permute-done | bytes 262176 | tf_op jit(solution)/shard_map/ppermute | solution.py:365
  130.4 1.2 collective-permute-done.3.high_last_ref
  131.8 31.7 %all_to_all.15.got_ref = bf16[4,2,2,128,128]{4,3,2,1,0:T(8,128)(2,1)S(1)} all-to-all(bf16[4,2,2,128,128]{4,3,2,1,0:T(8,128)(2,1)S(1)} %join_parts.1), channel_id=1, replica_groups=mesh['dp'=64,'slot'=4,'grp'=4] {'slot'}, dimensions={0} | all-to-all | bytes 1048576 | tf_op jit(solution)/shard_map/all_to_all | solution.py:370
  163.5 0.8 final_sum.1
  (23 shorter events, 0.7 us)
Async XLA Ops:
  2.2 21.3 %copy-start.3 = (bf16[2,512,32]{1,2,0:T(8,128)(2,1)S(1)}, bf16[2,512,32]{1,2,0:T(8,128)(2,1)}, u32[]{:S(2)}) copy-start(bf16[2,512,32]{1,2,0:T(8,128)(2,1)} %param.13) | copy-start | bytes 196612
  2.2 38.7 %copy-start = (bf16[2,512,512]{2,1,0:T(8,128)(2,1)S(1)}, bf16[2,512,512]{2,1,0:T(8,128)(2,1)}, u32[]{:S(2)}) copy-start(bf16[2,512,512]{2,1,0:T(8,128)(2,1)} %compress_ref.1) | copy-start | bytes 3145732
  2.2 38.7 %copy-start.1 = (bf16[2,32,128]{2,1,0:T(8,128)(2,1)S(1)}, bf16[2,32,128]{2,1,0:T(8,128)(2,1)}, u32[]{:S(2)}) copy-start(bf16[2,32,128]{2,1,0:T(8,128)(2,1)} %output_ref.1) | copy-start | bytes 49156
  2.2 38.7 %copy-start.2 = (f32[2,128]{1,0:T(2,128)S(1)}, f32[2,128]{1,0:T(2,128)}, u32[]{:S(2)}) copy-start(f32[2,128]{1,0:T(2,128)} %gain_ref.1) | copy-start | bytes 3076
  4.2 36.7 %all-to-all-start = ((bf16[4,560,128]{2,1,0:T(8,128)(2,1)}), bf16[4,560,128]{2,1,0:T(8,128)(2,1)S(1)}, u32[]{:S(2)}, u32[]{:S(2)}) async-start(bf16[4,560,128]{2,1,0:T(8,128)(2,1)} %pad_maximum_fusion), calls=%async_computation | async-start | bytes 1146880 | tf_op jit(solution)/shard_map/all_to_all | solution.py:349
  46.2 47.9 %all-to-all-start.1 = ((bf16[64,5,8,128]{3,2,1,0:T(8,128)(2,1)}), bf16[64,5,8,128]{3,2,1,0:T(8,128)(2,1)S(1)}, u32[]{:S(2)}, u32[]{:S(2)}) async-start(bf16[64,5,8,128]{3,2,1,0:T(8,128)(2,1)} %layers.1), calls=%async_computation.1 | async-start | bytes 1310720 | tf_op jit(solution)/shard_map/all_to_all | solution.py:351
  99.4 20.8 %collective-permute-start = (bf16[2,4,2,128,128]{4,3,2,1,0:T(8,128)(2,1)S(1)}, bf16[2,4,2,128,128]{4,3,2,1,0:T(8,128)(2,1)S(1)}, u32[]{:S(2)}, u32[]{:S(2)}) collective-permute-start(bf16[2,4,2,128,128]{4,3,2,1,0:T(8,128)(2,1)S(1)} %get-tuple-element.16), channel_id=1, source_target_pairs={{0,1},{1,0},{2,3},{3,2},{4,5},{5,4},{6,7},{7,6},{8,9},{9,8},{10,11... | collective-permute-start | bytes 1572872 | tf_op jit(solution)/shard_map/ppermute | solution.py:360
  107.2 16.0 %collective-permute-start.2 = (bf16[2,4,2,128,128]{4,3,2,1,0:T(8,128)(2,1)S(1)}, bf16[2,4,2,128,128]{4,3,2,1,0:T(8,128)(2,1)S(1)}, u32[]{:S(2)}, u32[]{:S(2)}) collective-permute-start(bf16[2,4,2,128,128]{4,3,2,1,0:T(8,128)(2,1)S(1)} %high_sent.1), channel_id=1, source_target_pairs={{0,3},{1,2},{2,1},{3,0},{4,7},{5,6},{6,5},{7,4},{8,11},{9,10},{10,... | collective-permute-start | bytes 1572872 | tf_op jit(solution)/shard_map/ppermute | solution.py:362
  120.4 10.0 %collective-permute-start.1 = (bf16[4,2,128,128]{3,2,1,0:T(8,128)(2,1)S(1)}, bf16[4,2,128,128]{3,2,1,0:T(8,128)(2,1)S(1)}, u32[]{:S(2)}, u32[]{:S(2)}) collective-permute-start(bf16[4,2,128,128]{3,2,1,0:T(8,128)(2,1)S(1)} %get-tuple-element.18), channel_id=1, source_target_pairs={{0,3},{1,2},{2,1},{3,0},{4,7},{5,6},{6,5},{7,4},{8,11},{9,10},{10,... | collective-permute-start | bytes 786440 | tf_op jit(solution)/shard_map/ppermute | solution.py:365
  123.4 8.3 %collective-permute-start.3 = (bf16[4,2,128,128]{3,2,1,0:T(8,128)(2,1)S(1)}, bf16[4,2,128,128]{3,2,1,0:T(8,128)(2,1)S(1)}, u32[]{:S(2)}, u32[]{:S(2)}) collective-permute-start(bf16[4,2,128,128]{3,2,1,0:T(8,128)(2,1)S(1)} %get-tuple-element.20), channel_id=1, source_target_pairs={{0,1},{1,0},{2,3},{3,2},{4,5},{5,4},{6,7},{7,6},{8,9},{9,8},{10,11... | collective-permute-start | bytes 786440 | tf_op jit(solution)/shard_map/ppermute | solution.py:368

commit v4 on v2

--- a/solution.py
+++ b/solution.py
@@ -172,76 +172,122 @@
             grads_ref[cap // 2, rows, D:] = (values * table).astype(bf16)
 
 
-def add_rows(first, amount, shift, out_refs, grads_ref, high_ref, low_ref):
+def add_rows(blocks_ref, out_ref, grads_ref, high_ref, low_ref):
     lanes = 2 * PAIR * DP
-    rows_of = (iota((amount, lanes), 0) + first).astype(f32).astype(bf16)
+    half = ROW_BLOCK // 2
+    rows_of = iota((half, lanes), 0).astype(f32).astype(bf16)
     one = jnp.ones((), bf16)
     zero = jnp.zeros((), bf16)
 
-    def block(s, carry):
-        for r in range(N_GRP):
-            group = shift + r
-            group = jnp.where(group >= N_GRP, group - N_GRP, group)
-            want = (s * N_GRP + group).astype(f32)
-            total = jnp.zeros((amount, 2 * D), f32)
+    def block(index, carry):
+        want = blocks_ref[index].astype(f32)
+        for part in range(2):
+            total = jnp.zeros((half, 2 * D), f32)
             for p in range(N_SLOT * CAPACITY // 2):
-                match = jnp.where(high_ref[p] == want, low_ref[p], -1.0)
-                count = jnp.zeros((amount, lanes), bf16)
+                match = jnp.where(high_ref[p] == want, low_ref[p] - float(part * half), -1.0)
+                count = jnp.zeros((half, lanes), bf16)
                 for j in range(BAG):
                     wanted = jnp.broadcast_to(match[j : j + 1], (16, lanes)).astype(bf16)
-                    wanted = jnp.broadcast_to(wanted[None], (amount // 16, 16, lanes)).reshape(amount, lanes)
+                    wanted = jnp.broadcast_to(wanted[None], (half // 16, 16, lanes)).reshape(half, lanes)
                     count = count + jnp.where(rows_of == wanted, one, zero)
                 total = total + dot(count, grads_ref[p])
-            out_refs[r][s, 0] = total[:, :D].astype(bf16)
-            out_refs[r][s, 1] = total[:, D:].astype(bf16)
+            rows = slice(part * half, (part + 1) * half)
+            out_ref[index // 2, index % 2, 0, rows] = total[:, :D].astype(bf16)
+            out_ref[index // 2, index % 2, 1, rows] = total[:, D:].astype(bf16)
         return carry
 
-    lax.fori_loop(0, N_SLOT, block, 0)
-
-
-def first_bags_kernel(amount, got_ref, out_ref, grads_ref, high_ref, low_ref, wide_ref):
+    lax.fori_loop(0, 4, block, 0)
+
+
+def first_bags_kernel(blocks_ref, got_ref, out_ref, grads_ref, high_ref, low_ref, wide_ref):
     prepare_bags(got_ref, wide_ref, grads_ref, high_ref, low_ref)
-    outs = [out_ref.at[r] for r in range(N_GRP)]
-    add_rows(0, amount, jnp.int32(0), outs, grads_ref, high_ref, low_ref)
-
-
-def second_bags_kernel(first, amount, shift_ref, grads_ref, high_ref, low_ref, *out_refs):
-    add_rows(first, amount, shift_ref[0], out_refs, grads_ref, high_ref, low_ref)
+    add_rows(blocks_ref, out_ref, grads_ref, high_ref, low_ref)
+
+
+def later_bags_kernel(blocks_ref, grads_ref, high_ref, low_ref, out_ref):
+    add_rows(blocks_ref, out_ref, grads_ref, high_ref, low_ref)
 
 
 VMEM_SPEC = pl.BlockSpec(memory_space=pltpu.VMEM)
-
-
-def run_first_bags(got, amount):
+SMEM_SPEC = pl.BlockSpec(memory_space=pltpu.SMEM)
+BAGS_COST = pl.CostEstimate(flops=200_000_000, bytes_accessed=1 << 20, transcendentals=0)
+ADD_COST = pl.CostEstimate(flops=1_000_000, bytes_accessed=1 << 20, transcendentals=0)
+CHUNK = (TABLE_DEV, ROW_BLOCK, D)
+
+
+def run_first_bags(blocks, got):
     pairs = N_SLOT * CAPACITY // 2
     lanes = 2 * PAIR * DP
     return pl.pallas_call(
-        functools.partial(first_bags_kernel, amount),
+        first_bags_kernel,
         out_shape=(
-            jax.ShapeDtypeStruct((N_GRP, N_SLOT, TABLE_DEV, amount, D), bf16),
+            jax.ShapeDtypeStruct((2, 2, *CHUNK), bf16),
             jax.ShapeDtypeStruct((pairs, lanes, 2 * D), bf16),
             jax.ShapeDtypeStruct((pairs, BAG, lanes), f32),
             jax.ShapeDtypeStruct((pairs, BAG, lanes), f32),
         ),
-        in_specs=[VMEM_SPEC],
+        in_specs=[SMEM_SPEC, VMEM_SPEC],
         out_specs=(VMEM_SPEC,) * 4,
         scratch_shapes=[pltpu.VMEM((DP * 8, D), f32)],
-        compiler_params=pltpu.CompilerParams(vmem_limit_bytes=32 << 20),
-        cost_estimate=pl.CostEstimate(flops=10_000_000_000, bytes_accessed=4 << 20, transcendentals=0),
+        compiler_params=pltpu.CompilerParams(vmem_limit_bytes=24 << 20),
+        cost_estimate=BAGS_COST,
         name="first_bags",
-    )(got)
-
-
-def run_second_bags(shift, grads, high, low, first, amount):
+    )(blocks, got)
+
+
+def run_later_bags(blocks, prepared, name):
     return pl.pallas_call(
-        functools.partial(second_bags_kernel, first, amount),
-        out_shape=(jax.ShapeDtypeStruct((N_SLOT, TABLE_DEV, amount, D), bf16),) * N_GRP,
-        in_specs=[pl.BlockSpec(memory_space=pltpu.SMEM)] + [VMEM_SPEC] * 3,
-        out_specs=(VMEM_SPEC,) * N_GRP,
-        compiler_params=pltpu.CompilerParams(vmem_limit_bytes=32 << 20),
-        cost_estimate=pl.CostEstimate(flops=10_000_000_000, bytes_accessed=4 << 20, transcendentals=0),
-        name="second_bags",
-    )(shift, grads, high, low)
+        later_bags_kernel,
+        out_shape=jax.ShapeDtypeStruct((2, 2, *CHUNK), bf16),
+        in_specs=[SMEM_SPEC] + [VMEM_SPEC] * 3,
+        out_specs=VMEM_SPEC,
+        compiler_params=pltpu.CompilerParams(vmem_limit_bytes=24 << 20),
+        cost_estimate=BAGS_COST,
+        name=name,
+    )(blocks, *prepared)
+
+
+def wide_sum(*refs):
+    total = refs[0][...].astype(f32)
+    for ref in refs[1:]:
+        total = total + ref[...].astype(f32)
+    return total
+
+
+def add_parts_kernel(kept_ref, got_ref, own_ref, sent_ref):
+    own_ref[...] = wide_sum(kept_ref.at[0], got_ref.at[0]).astype(bf16)
+    sent_ref[...] = wide_sum(kept_ref.at[1], got_ref.at[1]).astype(bf16)
+
+
+def relay_kernel(own_ref, got_ref, up_ref, down_ref, near_ref):
+    up_ref[...] = wide_sum(own_ref.at[0, 0], got_ref.at[0, 0]).astype(bf16)
+    down_ref[...] = wide_sum(own_ref.at[0, 1], got_ref.at[0, 1]).astype(bf16)
+    near_ref[...] = wide_sum(own_ref.at[1], got_ref.at[1]).astype(bf16)
+
+
+def join_kernel(own_ref, got_ref, near_ref, up_ref, down_ref, kept_ref, right_ref, left_ref):
+    kept_ref[...] = wide_sum(own_ref.at[0], got_ref.at[0])
+    right_ref[0] = wide_sum(near_ref.at[0], up_ref).astype(bf16)
+    right_ref[1] = near_ref[1]
+    left_ref[0] = wide_sum(own_ref.at[1, 0], got_ref.at[1, 0]).astype(bf16)
+    left_ref[1] = wide_sum(own_ref.at[1, 1], got_ref.at[1, 1], down_ref).astype(bf16)
+
+
+def final_kernel(kept_ref, right_ref, left_ref, out_ref):
+    out_ref[...] = wide_sum(kept_ref, right_ref, left_ref)
+
+
+def small_call(kernel, name, shapes, *args):
+    outs = tuple(jax.ShapeDtypeStruct(shape, dtype) for shape, dtype in shapes)
+    return pl.pallas_call(
+        kernel,
+        out_shape=outs,
+        in_specs=[VMEM_SPEC] * len(args),
+        out_specs=(VMEM_SPEC,) * len(outs),
+        compiler_params=pltpu.CompilerParams(vmem_limit_bytes=8 << 20),
+        cost_estimate=ADD_COST,
+        name=name,
+    )(*args)
 
 
 def per_device(
@@ -284,23 +330,43 @@
     messages = lax.all_to_all(messages, "slot", split_axis=0, concat_axis=0, tiled=True)
     sent = run_layers(messages, compress_weight, fm_basis, fm_output, norm_gain)
     got = lax.all_to_all(sent, "dp", split_axis=0, concat_axis=0, tiled=True)
-    half = ROW_BLOCK // 2
-    first, grads, high_ids, low_ids = run_first_bags(got, half)
-    shift = lax.axis_index("grp").astype(jnp.int32).reshape(1)
-    second = run_second_bags(shift, grads, high_ids, low_ids, half, half)
-    first = lax.all_to_all(first, "grp", split_axis=0, concat_axis=0, tiled=True)
-    first = jnp.sum(first.astype(f32), axis=0).astype(bf16)
-    first, second = lax.optimization_barrier((first, second))
-    first = lax.all_to_all(first, "slot", split_axis=0, concat_axis=0, tiled=True)
-    pieces = [second[0]]
-    for step in range(1, N_GRP):
-        moves = [(i, (i + step) % N_GRP) for i in range(N_GRP)]
-        pieces.append(lax.ppermute(second[step], "grp", moves))
-    second = sum(piece.astype(f32) for piece in pieces).astype(bf16)
-    second = lax.all_to_all(second, "slot", split_axis=0, concat_axis=0, tiled=True)
-    return jnp.concatenate(
-        [jnp.sum(first.astype(f32), axis=0), jnp.sum(second.astype(f32), axis=0)], axis=1
-    )
+    me = lax.axis_index("grp").astype(jnp.int32)
+    side = me ^ 1
+    mirror = N_GRP - 1 - me
+    across = side ^ 3
+    here = lax.axis_index("slot").astype(jnp.int32)
+    far, after, before = (here + 2) % N_SLOT, (here + 1) % N_SLOT, (here + 3) % N_SLOT
+
+    def blocks(groups, chunks):
+        return jnp.stack([chunk * N_GRP + group for group in groups for chunk in chunks])
+
+    half_a, half_b = (far, after), (here, before)
+    side_moves = [(i, i ^ 1) for i in range(N_GRP)]
+    mirror_moves = [(i, N_GRP - 1 - i) for i in range(N_GRP)]
+    up_moves = [(i, (i + 1) % N_SLOT) for i in range(N_SLOT)]
+    down_moves = [(i, (i - 1) % N_SLOT) for i in range(N_SLOT)]
+    a_sent, *prepared = run_first_bags(blocks((side, across), half_a), got)
+    a_got = lax.ppermute(a_sent, "grp", side_moves)
+    b_sent = run_later_bags(blocks((mirror, across), half_b), prepared, "b_sent")
+    b_got = lax.ppermute(b_sent, "grp", mirror_moves)
+    a_kept = run_later_bags(blocks((me, mirror), half_a), prepared, "a_kept")
+    part = ((2, *CHUNK), bf16)
+    a_own, a_next = small_call(add_parts_kernel, "add_a", (part, part), a_kept, a_got)
+    a_last = lax.ppermute(a_next, "grp", mirror_moves)
+    b_blocks, a_own = lax.optimization_barrier((blocks((me, side), half_b), a_own))
+    b_kept = run_later_bags(b_blocks, prepared, "b_kept")
+    b_own, b_next = small_call(add_parts_kernel, "add_b", (part, part), b_kept, b_got)
+    b_last = lax.ppermute(b_next, "grp", side_moves)
+    table = (CHUNK[1:], bf16)
+    up, down, near = small_call(relay_kernel, "relay", (table, table, (CHUNK, bf16)), a_own, a_last)
+    up = lax.ppermute(up, "slot", up_moves)
+    down = lax.ppermute(down, "slot", down_moves)
+    kept, right, left = small_call(
+        join_kernel, "join", ((CHUNK, f32), (CHUNK, bf16), (CHUNK, bf16)), b_own, b_last, near, up, down
+    )
+    right = lax.ppermute(right, "slot", up_moves)
+    left = lax.ppermute(left, "slot", down_moves)
+    return small_call(final_kernel, "final_sum", ((CHUNK, f32),), kept, right, left)[0]
 
 
 def solution(mesh):

time: 177 us -> 163 us (0.921); the launches traced: 173 us -> 163 us
  waiting for transfers between devices: 70.4 us -> 56 us
  Pallas kernels: 22.2 us -> 25.5 us
  starting transfers between devices: 73.8 us -> 76.4 us
  other arithmetic: 6.37 us -> 4.12 us
    all_to_all x3 -> x0, waiting for transfers between devices: 22.6 us -> none  [the longest x1 15.8 us: per_device(): lax.all_to_all(second, 'slot', split_axis=0, concat_axis=0, tiled=True)]
    ppermute x3 -> x8, starting transfers between devices: 8.4 us -> 30.3 us  [the longest x1 7.09 us: per_device(): down = lax.ppermute(down, 'slot', down_moves)]
    all_to_all x3 -> x0, starting transfers between devices: 19.3 us -> none  [the longest x1 11.2 us: per_device(): lax.all_to_all(second, 'slot', split_axis=0, concat_axis=0, tiled=True)]
    ppermute x3 -> x8, waiting for transfers between devices: 9.43 us -> 17.8 us  [the longest x1 12 us: per_device(): left = lax.ppermute(left, 'slot', down_moves)]
    pallas_call x2 -> x9, Pallas kernels: 17 us -> 20.3 us  [the longest x3 13.8 us: run_later_bags(): pl.pallas_call(later_bags_kernel, out_shape=jax.ShapeDtypeStruct((2, 2, *...]
  transfers between devices with their start and end apart: 8 -> 10, of which waited for: 7 -> 7; matrix products, arithmetic and copies ran while one was open for 1% -> 0% of each run, Pallas kernels for 4% -> 9%
where the time goes in v4:
time: 163 us
  starting transfers between devices  76.4 us (47%)
  waiting for transfers between devices  56 us (34%)
  Pallas kernels  25.5 us (16%)
  other arithmetic  4.12 us (3%)
    all_to_all x1, starting transfers between devices, per_device(): got = lax.all_to_all(sent, 'dp', split_axis=0, concat_axis=0, tiled=True)  26.9 us
    all_to_all x1, waiting for transfers between devices, per_device(): got = lax.all_to_all(sent, 'dp', split_axis=0, concat_axis=0, tiled=True)  20.9 us
    all_to_all x1, starting transfers between devices, per_device(): lax.all_to_all(messages, 'slot', split_axis=0, concat_axis=0, tiled=True)  19.3 us
    all_to_all x1, waiting for transfers between devices, per_device(): lax.all_to_all(messages, 'slot', split_axis=0, concat_axis=0, tiled=True)  17.3 us
    pallas_call x3, Pallas kernels, run_later_bags(): pl.pallas_call(later_bags_kernel, out_shape=jax.ShapeDtypeStruct((2, 2, *...  13.8 us
    ppermute x1, waiting for transfers between devices, per_device(): left = lax.ppermute(left, 'slot', down_moves)  12 us
    ppermute x1, starting transfers between devices, per_device(): down = lax.ppermute(down, 'slot', down_moves)  7.09 us
    pallas_call x1, Pallas kernels, run_first_bags(): pl.pallas_call(first_bags_kernel, out_shape=(jax.ShapeDtypeStruct((2, 2,...  5.32 us
  transfers between devices with their start and end apart: 10, of which 7 were waited for; matrix products, arithmetic and copies ran while one was open for 0% of the time, Pallas kernels for 9%

profile of v4, /device:TPU:1, one launch (start us, length us, event | category | flops | bytes accessed | tf_op | source)
XLA Modules:
  0.0 162.8 jit_solution(15728384222124098084)
XLA Ops:
  0.0 0.8 select_reduce_fusion
  0.9 0.8 fusion.8
  2.2 2.0 %pad_maximum_fusion = bf16[4,560,128]{2,1,0:T(8,128)(2,1)} fusion(bf16[4,16,128]{2,1,0:T(8,128)(2,1)S(1)} %broadcast_in_dim.21, bf16[4,32,128]{2,1,0:T(8,128)(2,1)S(1)} %copy.18, bf16[4,256,128]{2,1,0:T(8,128)(2,1)} %bitcast.30, bf16[4,256,128]{2,1,0:T(8,128)(2,1)} %bitcast.31), kind=kLoop, calls=%fused_computation | loop fusion | flops 2293760 | bytes 1146880 | tf_op jit(solution)/shard_map/concatenate | solution.py:321
  4.2 19.3 %all-to-all-start = ((bf16[4,560,128]{2,1,0:T(8,128)(2,1)}), bf16[4,560,128]{2,1,0:T(8,128)(2,1)S(1)}, u32[]{:S(2)}, u32[]{:S(2)}) async-start(bf16[4,560,128]{2,1,0:T(8,128)(2,1)} %pad_maximum_fusion), calls=%async_computation | async-start | bytes 1146880 | tf_op jit(solution)/shard_map/all_to_all | solution.py:330
  23.6 17.3 %all-to-all-done.x_ref = bf16[4,560,128]{2,1,0:T(8,128)(2,1)S(1)} async-done(((bf16[4,560,128]{2,1,0:T(8,128)(2,1)}), bf16[4,560,128]{2,1,0:T(8,128)(2,1)S(1)}, u32[]{:S(2)}, u32[]{:S(2)}) %all-to-all-start) | async-done | bytes 573472 | tf_op jit(solution)/shard_map/all_to_all | solution.py:330
  40.9 5.3 %layers.1 = bf16[64,5,8,128]{3,2,1,0:T(8,128)(2,1)} custom-call(bf16[4,560,128]{2,1,0:T(8,128)(2,1)S(1)} %all-to-all-done.x_ref, bf16[2,512,512]{2,1,0:T(8,128)(2,1)S(1)} %copy-done, bf16[2,512,32]{2,1,0:T(8,128)(2,1)S(1)} %copy.19.basis_ref, bf16[2,32,128]{2,1,0:T(8,128)(2,1)S(1)} %copy-done.1, f32[2,128]{1,0:T(2,128)S(1)} %copy-done.2), custom_call_target="tpu_custom_call" | custom-call | flops 2000000000 | bytes 4194304 | tf_op jit(solution)/shard_map/layers/pallas_call | solution.py:133
  46.2 26.9 %all-to-all-start.1 = ((bf16[64,5,8,128]{3,2,1,0:T(8,128)(2,1)}), bf16[64,5,8,128]{3,2,1,0:T(8,128)(2,1)S(1)}, u32[]{:S(2)}, u32[]{:S(2)}) async-start(bf16[64,5,8,128]{3,2,1,0:T(8,128)(2,1)} %layers.1), calls=%async_computation.1 | async-start | bytes 1310720 | tf_op jit(solution)/shard_map/all_to_all | solution.py:332
  73.2 20.9 %all-to-all-done.1.got_ref = bf16[64,5,8,128]{3,2,1,0:T(8,128)(2,1)S(1)} async-done(((bf16[64,5,8,128]{3,2,1,0:T(8,128)(2,1)}), bf16[64,5,8,128]{3,2,1,0:T(8,128)(2,1)S(1)}, u32[]{:S(2)}, u32[]{:S(2)}) %all-to-all-start.1) | async-done | bytes 655392 | tf_op jit(solution)/shard_map/all_to_all | solution.py:332
  94.1 5.3 %first_bags.1 = (bf16[2,2,2,256,128]{4,3,2,1,0:T(8,128)(2,1)S(1)}, bf16[8,256,256]{2,1,0:T(8,128)(2,1)S(1)}, f32[8,8,256]{2,1,0:T(8,128)S(1)}, f32[8,8,256]{2,1,0:T(8,128)S(1)}) custom-call(s32[4]{0:T(128)S(1)} %pad_add_fusion.2.blocks_ref, bf16[64,5,8,128]{3,2,1,0:T(8,128)(2,1)S(1)} %all-to-all-done.1.got_ref), custom_call_target="tpu_custom_call" | custom-call | flops 200000000 | bytes 1048576 | tf_op jit(solution)/shard_map/first_bags/pallas_call | solution.py:221
  99.4 3.1 %collective-permute-start = (bf16[2,2,2,256,128]{4,3,2,1,0:T(8,128)(2,1)S(1)}, bf16[2,2,2,256,128]{4,3,2,1,0:T(8,128)(2,1)S(1)}, u32[]{:S(2)}, u32[]{:S(2)}) collective-permute-start(bf16[2,2,2,256,128]{4,3,2,1,0:T(8,128)(2,1)S(1)} %get-tuple-element.24), channel_id=1, source_target_pairs={{0,1},{1,0},{2,3},{3,2},{4,5},{5,4},{6,7},{7,6},{8,9},{9,8},{10,11... | collective-permute-start | bytes 1572872 | tf_op jit(solution)/shard_map/ppermute | solution.py:349
  102.6 4.6 %b_sent.1 = bf16[2,2,2,256,128]{4,3,2,1,0:T(8,128)(2,1)S(1)} custom-call(s32[4]{0:T(128)S(1)} %pad_add_fusion.3.blocks_ref, bf16[8,256,256]{2,1,0:T(8,128)(2,1)S(1)} %get-tuple-element.21.grads_ref, f32[8,8,256]{2,1,0:T(8,128)S(1)} %get-tuple-element.22.high_ref, f32[8,8,256]{2,1,0:T(8,128)S(1)} %get-tuple-element.23.low_ref), custom_call_target="tpu_custom_call" | custom-call | flops 200000000 | bytes 1048576 | tf_op jit(solution)/shard_map/b_sent/pallas_call | solution.py:239
  107.3 3.7 %collective-permute-start.1 = (bf16[2,2,2,256,128]{4,3,2,1,0:T(8,128)(2,1)S(1)}, bf16[2,2,2,256,128]{4,3,2,1,0:T(8,128)(2,1)S(1)}, u32[]{:S(2)}, u32[]{:S(2)}) collective-permute-start(bf16[2,2,2,256,128]{4,3,2,1,0:T(8,128)(2,1)S(1)} %b_sent.1), channel_id=1, source_target_pairs={{0,3},{1,2},{2,1},{3,0},{4,7},{5,6},{6,5},{7,4},{8,11},{9,10},{10,... | collective-permute-start | bytes 1572872 | tf_op jit(solution)/shard_map/ppermute | solution.py:351
  111.1 4.6 %a_kept.1.kept_ref = bf16[2,2,2,256,128]{4,3,2,1,0:T(8,128)(2,1)S(1)} custom-call(s32[4]{0:T(128)S(1)} %pad_add_fusion.1.blocks_ref, bf16[8,256,256]{2,1,0:T(8,128)(2,1)S(1)} %get-tuple-element.21.grads_ref, f32[8,8,256]{2,1,0:T(8,128)S(1)} %get-tuple-element.22.high_ref, f32[8,8,256]{2,1,0:T(8,128)S(1)} %get-tuple-element.23.low_ref), custom_call_target="tpu_custom_call" | custom-call | flops 200000000 | bytes 1048576 | tf_op jit(solution)/shard_map/a_kept/pallas_call | solution.py:239
  115.8 3.1 %collective-permute-start.3 = (bf16[2,2,256,128]{3,2,1,0:T(8,128)(2,1)S(1)}, bf16[2,2,256,128]{3,2,1,0:T(8,128)(2,1)S(1)}, u32[]{:S(2)}, u32[]{:S(2)}) collective-permute-start(bf16[2,2,256,128]{3,2,1,0:T(8,128)(2,1)S(1)} %get-tuple-element.30), channel_id=1, source_target_pairs={{0,3},{1,2},{2,1},{3,0},{4,7},{5,6},{6,5},{7,4},{8,11},{9,10},{10,... | collective-permute-start | bytes 786440 | tf_op jit(solution)/shard_map/ppermute | solution.py:355
  119.1 4.6 %b_kept.1.kept_ref = bf16[2,2,2,256,128]{4,3,2,1,0:T(8,128)(2,1)S(1)} custom-call(s32[4]{0:T(128)S(1)} %pad_add_fusion.blocks_ref, bf16[8,256,256]{2,1,0:T(8,128)(2,1)S(1)} %get-tuple-element.21.grads_ref, f32[8,8,256]{2,1,0:T(8,128)S(1)} %get-tuple-element.22.high_ref, f32[8,8,256]{2,1,0:T(8,128)S(1)} %get-tuple-element.23.low_ref), custom_call_target="tpu_custom_call" | custom-call | flops 200000000 | bytes 1048576 | tf_op jit(solution)/shard_map/b_kept/pallas_call | solution.py:239
  123.8 1.9 %collective-permute-start.2 = (bf16[2,2,256,128]{3,2,1,0:T(8,128)(2,1)S(1)}, bf16[2,2,256,128]{3,2,1,0:T(8,128)(2,1)S(1)}, u32[]{:S(2)}, u32[]{:S(2)}) collective-permute-start(bf16[2,2,256,128]{3,2,1,0:T(8,128)(2,1)S(1)} %get-tuple-element.28), channel_id=1, source_target_pairs={{0,1},{1,0},{2,3},{3,2},{4,5},{5,4},{6,7},{7,6},{8,9},{9,8},{10,11... | collective-permute-start | bytes 786440 | tf_op jit(solution)/shard_map/ppermute | solution.py:359
  125.7 3.1 %collective-permute-done.3.got_ref = bf16[2,2,256,128]{3,2,1,0:T(8,128)(2,1)S(1)} collective-permute-done((bf16[2,2,256,128]{3,2,1,0:T(8,128)(2,1)S(1)}, bf16[2,2,256,128]{3,2,1,0:T(8,128)(2,1)S(1)}, u32[]{:S(2)}, u32[]{:S(2)}) %collective-permute-start.3) | collective-permute-done | bytes 262176 | tf_op jit(solution)/shard_map/ppermute | solution.py:355
  128.9 2.1 %collective-permute-start.4 = (bf16[256,128]{1,0:T(8,128)(2,1)S(1)}, bf16[256,128]{1,0:T(8,128)(2,1)S(1)}, u32[]{:S(2)}, u32[]{:S(2)}) collective-permute-start(bf16[256,128]{1,0:T(8,128)(2,1)S(1)} %get-tuple-element.32), channel_id=1, source_target_pairs={{0,4},{4,8},{8,12},{12,0},{1,5},{5,9},{9,13},{13,1},{2,6},{6,10},{... | collective-permute-start | bytes 196616 | tf_op jit(solution)/shard_map/ppermute | solution.py:362
  131.0 7.1 %collective-permute-start.5 = (bf16[256,128]{1,0:T(8,128)(2,1)S(1)}, bf16[256,128]{1,0:T(8,128)(2,1)S(1)}, u32[]{:S(2)}, u32[]{:S(2)}) collective-permute-start(bf16[256,128]{1,0:T(8,128)(2,1)S(1)} %get-tuple-element.33), channel_id=1, source_target_pairs={{0,12},{4,0},{8,4},{12,8},{1,13},{5,1},{9,5},{13,9},{2,14},{6,2},{... | collective-permute-start | bytes 196616 | tf_op jit(solution)/shard_map/ppermute | solution.py:363
  138.1 1.5 collective-permute-done.4.up_ref
  140.4 4.7 %collective-permute-start.6 = (bf16[2,256,128]{2,1,0:T(8,128)(2,1)S(1)}, bf16[2,256,128]{2,1,0:T(8,128)(2,1)S(1)}, u32[]{:S(2)}, u32[]{:S(2)}) collective-permute-start(bf16[2,256,128]{2,1,0:T(8,128)(2,1)S(1)} %get-tuple-element.35), channel_id=1, source_target_pairs={{0,4},{4,8},{8,12},{12,0},{1,5},{5,9},{9,13},{13,1},{2,6},{6,10},{... | collective-permute-start | bytes 393224 | tf_op jit(solution)/shard_map/ppermute | solution.py:367
  145.0 4.5 %collective-permute-start.7 = (bf16[2,256,128]{2,1,0:T(8,128)(2,1)S(1)}, bf16[2,256,128]{2,1,0:T(8,128)(2,1)S(1)}, u32[]{:S(2)}, u32[]{:S(2)}) collective-permute-start(bf16[2,256,128]{2,1,0:T(8,128)(2,1)S(1)} %get-tuple-element.36), channel_id=1, source_target_pairs={{0,12},{4,0},{8,4},{12,8},{1,13},{5,1},{9,5},{13,9},{2,14},{6,2},{... | collective-permute-start | bytes 393224 | tf_op jit(solution)/shard_map/ppermute | solution.py:368
  150.1 12.0 %collective-permute-done.7.left_ref = bf16[2,256,128]{2,1,0:T(8,128)(2,1)S(1)} collective-permute-done((bf16[2,256,128]{2,1,0:T(8,128)(2,1)S(1)}, bf16[2,256,128]{2,1,0:T(8,128)(2,1)S(1)}, u32[]{:S(2)}, u32[]{:S(2)}) %collective-permute-start.7) | collective-permute-done | bytes 131104 | tf_op jit(solution)/shard_map/ppermute | solution.py:368
  162.1 0.7 final_sum.1
  (31 shorter events, 2.5 us)
Async XLA Ops:
  2.1 21.3 %copy-start.3 = (bf16[2,512,32]{1,2,0:T(8,128)(2,1)S(1)}, bf16[2,512,32]{1,2,0:T(8,128)(2,1)}, u32[]{:S(2)}) copy-start(bf16[2,512,32]{1,2,0:T(8,128)(2,1)} %param.13) | copy-start | bytes 196612
  2.2 38.7 %copy-start = (bf16[2,512,512]{2,1,0:T(8,128)(2,1)S(1)}, bf16[2,512,512]{2,1,0:T(8,128)(2,1)}, u32[]{:S(2)}) copy-start(bf16[2,512,512]{2,1,0:T(8,128)(2,1)} %compress_ref.1) | copy-start | bytes 3145732
  2.2 38.7 %copy-start.1 = (bf16[2,32,128]{2,1,0:T(8,128)(2,1)S(1)}, bf16[2,32,128]{2,1,0:T(8,128)(2,1)}, u32[]{:S(2)}) copy-start(bf16[2,32,128]{2,1,0:T(8,128)(2,1)} %output_ref.1) | copy-start | bytes 49156
  2.2 38.7 %copy-start.2 = (f32[2,128]{1,0:T(2,128)S(1)}, f32[2,128]{1,0:T(2,128)}, u32[]{:S(2)}) copy-start(f32[2,128]{1,0:T(2,128)} %gain_ref.1) | copy-start | bytes 3076
  4.2 36.7 %all-to-all-start = ((bf16[4,560,128]{2,1,0:T(8,128)(2,1)}), bf16[4,560,128]{2,1,0:T(8,128)(2,1)S(1)}, u32[]{:S(2)}, u32[]{:S(2)}) async-start(bf16[4,560,128]{2,1,0:T(8,128)(2,1)} %pad_maximum_fusion), calls=%async_computation | async-start | bytes 1146880 | tf_op jit(solution)/shard_map/all_to_all | solution.py:330
  46.2 47.9 %all-to-all-start.1 = ((bf16[64,5,8,128]{3,2,1,0:T(8,128)(2,1)}), bf16[64,5,8,128]{3,2,1,0:T(8,128)(2,1)S(1)}, u32[]{:S(2)}, u32[]{:S(2)}) async-start(bf16[64,5,8,128]{3,2,1,0:T(8,128)(2,1)} %layers.1), calls=%async_computation.1 | async-start | bytes 1310720 | tf_op jit(solution)/shard_map/all_to_all | solution.py:332
  99.4 16.3 %collective-permute-start = (bf16[2,2,2,256,128]{4,3,2,1,0:T(8,128)(2,1)S(1)}, bf16[2,2,2,256,128]{4,3,2,1,0:T(8,128)(2,1)S(1)}, u32[]{:S(2)}, u32[]{:S(2)}) collective-permute-start(bf16[2,2,2,256,128]{4,3,2,1,0:T(8,128)(2,1)S(1)} %get-tuple-element.24), channel_id=1, source_target_pairs={{0,1},{1,0},{2,3},{3,2},{4,5},{5,4},{6,7},{7,6},{8,9},{9,8},{10,11... | collective-permute-start | bytes 1572872 | tf_op jit(solution)/shard_map/ppermute | solution.py:349
  107.3 16.4 %collective-permute-start.1 = (bf16[2,2,2,256,128]{4,3,2,1,0:T(8,128)(2,1)S(1)}, bf16[2,2,2,256,128]{4,3,2,1,0:T(8,128)(2,1)S(1)}, u32[]{:S(2)}, u32[]{:S(2)}) collective-permute-start(bf16[2,2,2,256,128]{4,3,2,1,0:T(8,128)(2,1)S(1)} %b_sent.1), channel_id=1, source_target_pairs={{0,3},{1,2},{2,1},{3,0},{4,7},{5,6},{6,5},{7,4},{8,11},{9,10},{10,... | collective-permute-start | bytes 1572872 | tf_op jit(solution)/shard_map/ppermute | solution.py:351
  115.8 13.0 %collective-permute-start.3 = (bf16[2,2,256,128]{3,2,1,0:T(8,128)(2,1)S(1)}, bf16[2,2,256,128]{3,2,1,0:T(8,128)(2,1)S(1)}, u32[]{:S(2)}, u32[]{:S(2)}) collective-permute-start(bf16[2,2,256,128]{3,2,1,0:T(8,128)(2,1)S(1)} %get-tuple-element.30), channel_id=1, source_target_pairs={{0,3},{1,2},{2,1},{3,0},{4,7},{5,6},{6,5},{7,4},{8,11},{9,10},{10,... | collective-permute-start | bytes 786440 | tf_op jit(solution)/shard_map/ppermute | solution.py:355
  123.8 14.3 %collective-permute-start.2 = (bf16[2,2,256,128]{3,2,1,0:T(8,128)(2,1)S(1)}, bf16[2,2,256,128]{3,2,1,0:T(8,128)(2,1)S(1)}, u32[]{:S(2)}, u32[]{:S(2)}) collective-permute-start(bf16[2,2,256,128]{3,2,1,0:T(8,128)(2,1)S(1)} %get-tuple-element.28), channel_id=1, source_target_pairs={{0,1},{1,0},{2,3},{3,2},{4,5},{5,4},{6,7},{7,6},{8,9},{9,8},{10,11... | collective-permute-start | bytes 786440 | tf_op jit(solution)/shard_map/ppermute | solution.py:359
  128.9 10.8 %collective-permute-start.4 = (bf16[256,128]{1,0:T(8,128)(2,1)S(1)}, bf16[256,128]{1,0:T(8,128)(2,1)S(1)}, u32[]{:S(2)}, u32[]{:S(2)}) collective-permute-start(bf16[256,128]{1,0:T(8,128)(2,1)S(1)} %get-tuple-element.32), channel_id=1, source_target_pairs={{0,4},{4,8},{8,12},{12,0},{1,5},{5,9},{9,13},{13,1},{2,6},{6,10},{... | collective-permute-start | bytes 196616 | tf_op jit(solution)/shard_map/ppermute | solution.py:362
  131.0 9.3 %collective-permute-start.5 = (bf16[256,128]{1,0:T(8,128)(2,1)S(1)}, bf16[256,128]{1,0:T(8,128)(2,1)S(1)}, u32[]{:S(2)}, u32[]{:S(2)}) collective-permute-start(bf16[256,128]{1,0:T(8,128)(2,1)S(1)} %get-tuple-element.33), channel_id=1, source_target_pairs={{0,12},{4,0},{8,4},{12,8},{1,13},{5,1},{9,5},{13,9},{2,14},{6,2},{... | collective-permute-start | bytes 196616 | tf_op jit(solution)/shard_map/ppermute | solution.py:363
  140.4 9.7 %collective-permute-start.6 = (bf16[2,256,128]{2,1,0:T(8,128)(2,1)S(1)}, bf16[2,256,128]{2,1,0:T(8,128)(2,1)S(1)}, u32[]{:S(2)}, u32[]{:S(2)}) collective-permute-start(bf16[2,256,128]{2,1,0:T(8,128)(2,1)S(1)} %get-tuple-element.35), channel_id=1, source_target_pairs={{0,4},{4,8},{8,12},{12,0},{1,5},{5,9},{9,13},{13,1},{2,6},{6,10},{... | collective-permute-start | bytes 393224 | tf_op jit(solution)/shard_map/ppermute | solution.py:367
  145.0 17.1 %collective-permute-start.7 = (bf16[2,256,128]{2,1,0:T(8,128)(2,1)S(1)}, bf16[2,256,128]{2,1,0:T(8,128)(2,1)S(1)}, u32[]{:S(2)}, u32[]{:S(2)}) collective-permute-start(bf16[2,256,128]{2,1,0:T(8,128)(2,1)S(1)} %get-tuple-element.36), channel_id=1, source_target_pairs={{0,12},{4,0},{8,4},{12,8},{1,13},{5,1},{9,5},{13,9},{2,14},{6,2},{... | collective-permute-start | bytes 393224 | tf_op jit(solution)/shard_map/ppermute | solution.py:368

commit v5 on v4

--- a/solution.py
+++ b/solution.py
@@ -23,13 +23,18 @@
 ROW_BLOCK = 256
 DEAD = 64
 ID_ROWS = 32
-MSG_ROWS = 2 * PAIR * SLOT_DEV + 48
+POOLED_ROWS = PAIR * SLOT_DEV
+MSG_ROWS = 2 * POOLED_ROWS + ID_ROWS + 16
 
 norm_eps = 1e-05
 f32 = jnp.float32
 bf16 = jnp.bfloat16
 
 
+VMEM_SPEC = pl.BlockSpec(memory_space=pltpu.VMEM)
+SMEM_SPEC = pl.BlockSpec(memory_space=pltpu.SMEM)
+
+
 def dot(a, b, ca=1, cb=0):
     return lax.dot_general(a, b, (((ca,), (cb,)), ((), ())), preferred_element_type=f32)
 
@@ -38,9 +43,55 @@
     return lax.broadcasted_iota(jnp.int32, shape, dim)
 
 
-def layers_kernel(x_ref, compress_ref, basis_ref, output_ref, gain_ref, out_ref):
+def messages_kernel(
+    here_ref, pooled_ref, cotangent_ref, ids_ref, lengths_ref, slot_ref, home_ref, *out_refs
+):
+    slots = slot_ref[...]
+    hot = jnp.where(iota((SLOT_DEV, SLOT_DEV), 0) == slots, 1.0, 0.0).astype(bf16)
+    homes = jnp.broadcast_to(home_ref[...].astype(f32), (8, SLOT_DEV)).astype(bf16)
+    across = dot(homes, hot)[:1].astype(jnp.int32)
+    down = dot(hot, homes, 0, 1)[:, :1].astype(jnp.int32)
+    earlier = iota((SLOT_DEV, SLOT_DEV), 0) < iota((SLOT_DEV, SLOT_DEV), 1)
+    same = (down // TABLE_DEV == across // TABLE_DEV) & earlier
+    rank = jnp.sum(jnp.where(same, 1.0, 0.0), axis=0, keepdims=True)
+    target = (across // TABLE_DEV * CAPACITY).astype(f32) + rank
+    table = across % TABLE_DEV * 16
+    marks = jnp.broadcast_to(target, (16, SLOT_DEV)).astype(bf16)
+    entry = iota((BAG, SLOT_DEV), 0)
+    for r, out_ref in enumerate(out_refs):
+        dest = lax.rem(here_ref[0] + r, N_SLOT)
+        out_ref[:POOLED_ROWS] = pooled_ref[dest]
+        out_ref[POOLED_ROWS : 2 * POOLED_ROWS] = cotangent_ref[dest]
+        parts = []
+        for b in range(PAIR):
+            ids = ids_ref[dest * PAIR + b]
+            live = entry < lengths_ref[dest * PAIR + b]
+            parts.append((jnp.where(live, ids // ROW_BLOCK, DEAD) + table).astype(f32))
+            parts.append((ids % ROW_BLOCK).astype(f32))
+        out_ref[2 * POOLED_ROWS : 2 * POOLED_ROWS + ID_ROWS] = jnp.concatenate(parts, axis=0).astype(bf16)
+        out_ref[2 * POOLED_ROWS + ID_ROWS :] = marks
+
+
+def make_messages(here, *args):
+    message = jax.ShapeDtypeStruct((MSG_ROWS, D), bf16)
+    return pl.pallas_call(
+        messages_kernel,
+        out_shape=(message,) * N_SLOT,
+        in_specs=[SMEM_SPEC] + [VMEM_SPEC] * len(args),
+        out_specs=(VMEM_SPEC,) * N_SLOT,
+        compiler_params=pltpu.CompilerParams(vmem_limit_bytes=16 << 20),
+        cost_estimate=pl.CostEstimate(flops=1_000_000, bytes_accessed=2 << 20, transcendentals=0),
+        name="messages",
+    )(here, *args)
+
+
+def layers_kernel(
+    here_ref, own_ref, before_ref, far_ref, after_ref, compress_ref, basis_ref, output_ref, gain_ref, out_ref, x_ref
+):
+    for r, ref in enumerate((own_ref, after_ref, far_ref, before_ref)):
+        x_ref[lax.rem(here_ref[0] + r, N_SLOT)] = ref[...]
     gain = gain_ref[...]
-    pair_rows = PAIR * SLOT_DEV
+    pair_rows = POOLED_ROWS
     current = []
     upstream = []
     for b in range(PAIR):
@@ -112,33 +163,29 @@
     row = iota(shape, 0)
     row_key = row // 8 * CAPACITY + row % 8 * 1024
     column_key = jnp.concatenate([targets[k] + k * 1024 for k in range(N_SLOT)], axis=1)
-    unpacked = []
-    lane_in = iota((D, D), 0)
-    lane_out = iota((D, D), 1)
-    for k in range(N_SLOT):
-        packed = x_ref[k, 2 * pair_rows : 2 * pair_rows + ID_ROWS, :]
-        for q in range(D // ID_ROWS):
-            spread = jnp.where(lane_in == q * 32 + lane_out % 32, 1.0, 0.0).astype(bf16)
-            unpacked.append(dot(packed, spread).astype(bf16))
-    unpacked = jnp.concatenate(unpacked, axis=0)
+    unpacked = jnp.concatenate(
+        [x_ref[k, 2 * pair_rows : 2 * pair_rows + ID_ROWS, :] for k in range(N_SLOT)], axis=1
+    )
+    unpacked = jnp.concatenate([unpacked] * CAPACITY, axis=0)
     rank_lane = iota((1, D), 1) // 32
     ids = jnp.zeros((DP * 8, D), f32)
     for rank in range(CAPACITY):
         placing = jnp.where(row_key + rank == column_key, 1.0, 0.0).astype(bf16)
-        ids = ids + jnp.where(rank_lane == rank, dot(placing, unpacked), 0.0)
+        ids = ids + jnp.where(rank_lane == rank, dot(placing, unpacked, 1, 1), 0.0)
     out_ref[:, N_SLOT] = ids.astype(bf16).reshape(DP, 8, D)
 
 
-def run_layers(messages, compress, basis, outputs, gain):
+def run_layers(here, *args):
     return pl.pallas_call(
         layers_kernel,
         out_shape=jax.ShapeDtypeStruct((DP, N_SLOT + 1, 8, D), bf16),
-        in_specs=[pl.BlockSpec(memory_space=pltpu.VMEM)] * 5,
-        out_specs=pl.BlockSpec(memory_space=pltpu.VMEM),
-        compiler_params=pltpu.CompilerParams(vmem_limit_bytes=48 << 20),
+        in_specs=[SMEM_SPEC] + [VMEM_SPEC] * len(args),
+        out_specs=VMEM_SPEC,
+        scratch_shapes=[pltpu.VMEM((N_SLOT, MSG_ROWS, D), bf16)],
+        compiler_params=pltpu.CompilerParams(vmem_limit_bytes=20 << 20),
         cost_estimate=pl.CostEstimate(flops=2_000_000_000, bytes_accessed=4 << 20, transcendentals=4096),
         name="layers",
-    )(messages, compress, basis, outputs, gain)
+    )(here, *args)
 
 
 def prepare_bags(got_ref, wide_ref, grads_ref, high_ref, low_ref):
@@ -208,8 +255,6 @@
     add_rows(blocks_ref, out_ref, grads_ref, high_ref, low_ref)
 
 
-VMEM_SPEC = pl.BlockSpec(memory_space=pltpu.VMEM)
-SMEM_SPEC = pl.BlockSpec(memory_space=pltpu.SMEM)
 BAGS_COST = pl.CostEstimate(flops=200_000_000, bytes_accessed=1 << 20, transcendentals=0)
 ADD_COST = pl.CostEstimate(flops=1_000_000, bytes_accessed=1 << 20, transcendentals=0)
 CHUNK = (TABLE_DEV, ROW_BLOCK, D)
@@ -259,22 +304,18 @@
     sent_ref[...] = wide_sum(kept_ref.at[1], got_ref.at[1]).astype(bf16)
 
 
-def relay_kernel(own_ref, got_ref, up_ref, down_ref, near_ref):
-    up_ref[...] = wide_sum(own_ref.at[0, 0], got_ref.at[0, 0]).astype(bf16)
-    down_ref[...] = wide_sum(own_ref.at[0, 1], got_ref.at[0, 1]).astype(bf16)
-    near_ref[...] = wide_sum(own_ref.at[1], got_ref.at[1]).astype(bf16)
-
-
-def join_kernel(own_ref, got_ref, near_ref, up_ref, down_ref, kept_ref, right_ref, left_ref):
+def sum_a_kernel(own_ref, got_ref, far_ref, after_ref):
+    far_ref[...] = wide_sum(own_ref.at[0], got_ref.at[0]).astype(bf16)
+    after_ref[...] = wide_sum(own_ref.at[1], got_ref.at[1]).astype(bf16)
+
+
+def sum_b_kernel(own_ref, got_ref, kept_ref, before_ref):
     kept_ref[...] = wide_sum(own_ref.at[0], got_ref.at[0])
-    right_ref[0] = wide_sum(near_ref.at[0], up_ref).astype(bf16)
-    right_ref[1] = near_ref[1]
-    left_ref[0] = wide_sum(own_ref.at[1, 0], got_ref.at[1, 0]).astype(bf16)
-    left_ref[1] = wide_sum(own_ref.at[1, 1], got_ref.at[1, 1], down_ref).astype(bf16)
-
-
-def final_kernel(kept_ref, right_ref, left_ref, out_ref):
-    out_ref[...] = wide_sum(kept_ref, right_ref, left_ref)
+    before_ref[...] = wide_sum(own_ref.at[1], got_ref.at[1]).astype(bf16)
+
+
+def final_kernel(kept_ref, far_ref, before_ref, after_ref, out_ref):
+    out_ref[...] = wide_sum(kept_ref, far_ref, before_ref, after_ref)
 
 
 def small_call(kernel, name, shapes, *args):
@@ -302,39 +343,31 @@
     slot_table,
     table_home,
 ):
-    slot_count = pooled.shape[1]
-    matches = slot_table[:, None] == jnp.arange(table_home.shape[0], dtype=jnp.int32)[None, :]
-    position = jnp.sum(jnp.where(matches, table_home[None, :], 0), axis=1)
-    owner = position // TABLE_DEV
-    table = position % TABLE_DEV
-    order = jnp.arange(slot_count, dtype=jnp.int32)
-    rank = jnp.sum(
-        ((owner[None, :] == owner[:, None]) & (order[None, :] < order[:, None])).astype(jnp.int32), axis=1
-    )
-    target = owner * CAPACITY + rank
-    live = jnp.arange(BAG, dtype=jnp.int32)[None, None, :] < bag_lengths[:, :, None]
-    high = jnp.where(live, bag_ids // ROW_BLOCK, DEAD) + table[None, :, None] * 16
-    low = bag_ids % ROW_BLOCK
-    parts = jnp.stack([high, low], axis=2).astype(bf16)
-    parts = parts.reshape(N_SLOT, PAIR, 4, 32, 16).transpose(0, 3, 2, 1, 4).reshape(N_SLOT, ID_ROWS, D)
-    marks = jnp.broadcast_to(target.astype(bf16)[None, None, :], (N_SLOT, 16, slot_count))
-    messages = jnp.concatenate(
-        [
-            pooled.reshape(N_SLOT, PAIR * slot_count, D),
-            cotangent.reshape(N_SLOT, PAIR * slot_count, D),
-            parts,
-            marks,
-        ],
-        axis=1,
-    )
-    messages = lax.all_to_all(messages, "slot", split_axis=0, concat_axis=0, tiled=True)
-    sent = run_layers(messages, compress_weight, fm_basis, fm_output, norm_gain)
+    here = lax.axis_index("slot").astype(jnp.int32)
+    at_slot = here.reshape(1)
+    up_moves, far_moves, down_moves = (
+        [(i, (i + step) % N_SLOT) for i in range(N_SLOT)] for step in (1, 2, 3)
+    )
+    own, to_after, to_far, to_before = make_messages(
+        at_slot,
+        pooled.reshape(N_SLOT, POOLED_ROWS, D),
+        cotangent.reshape(N_SLOT, POOLED_ROWS, D),
+        jnp.transpose(bag_ids, (0, 2, 1)),
+        bag_lengths.reshape(-1, 1, SLOT_DEV),
+        slot_table.reshape(1, SLOT_DEV),
+        table_home.reshape(1, -1),
+    )
+    from_far = lax.ppermute(to_far, "slot", far_moves)
+    from_before = lax.ppermute(to_after, "slot", up_moves)
+    from_after = lax.ppermute(to_before, "slot", down_moves)
+    sent = run_layers(
+        at_slot, own, from_before, from_far, from_after, compress_weight, fm_basis, fm_output, norm_gain
+    )
     got = lax.all_to_all(sent, "dp", split_axis=0, concat_axis=0, tiled=True)
     me = lax.axis_index("grp").astype(jnp.int32)
     side = me ^ 1
     mirror = N_GRP - 1 - me
     across = side ^ 3
-    here = lax.axis_index("slot").astype(jnp.int32)
     far, after, before = (here + 2) % N_SLOT, (here + 1) % N_SLOT, (here + 3) % N_SLOT
 
     def blocks(groups, chunks):
@@ -343,8 +376,6 @@
     half_a, half_b = (far, after), (here, before)
     side_moves = [(i, i ^ 1) for i in range(N_GRP)]
     mirror_moves = [(i, N_GRP - 1 - i) for i in range(N_GRP)]
-    up_moves = [(i, (i + 1) % N_SLOT) for i in range(N_SLOT)]
-    down_moves = [(i, (i - 1) % N_SLOT) for i in range(N_SLOT)]
     a_sent, *prepared = run_first_bags(blocks((side, across), half_a), got)
     a_got = lax.ppermute(a_sent, "grp", side_moves)
     b_sent = run_later_bags(blocks((mirror, across), half_b), prepared, "b_sent")
@@ -357,16 +388,13 @@
     b_kept = run_later_bags(b_blocks, prepared, "b_kept")
     b_own, b_next = small_call(add_parts_kernel, "add_b", (part, part), b_kept, b_got)
     b_last = lax.ppermute(b_next, "grp", side_moves)
-    table = (CHUNK[1:], bf16)
-    up, down, near = small_call(relay_kernel, "relay", (table, table, (CHUNK, bf16)), a_own, a_last)
-    up = lax.ppermute(up, "slot", up_moves)
-    down = lax.ppermute(down, "slot", down_moves)
-    kept, right, left = small_call(
-        join_kernel, "join", ((CHUNK, f32), (CHUNK, bf16), (CHUNK, bf16)), b_own, b_last, near, up, down
-    )
-    right = lax.ppermute(right, "slot", up_moves)
-    left = lax.ppermute(left, "slot", down_moves)
-    return small_call(final_kernel, "final_sum", ((CHUNK, f32),), kept, right, left)[0]
+    chunk = (CHUNK, bf16)
+    to_far, to_after = small_call(sum_a_kernel, "sum_a", (chunk, chunk), a_own, a_last)
+    from_far = lax.ppermute(to_far, "slot", far_moves)
+    from_before = lax.ppermute(to_after, "slot", up_moves)
+    kept, to_before = small_call(sum_b_kernel, "sum_b", ((CHUNK, f32), chunk), b_own, b_last)
+    from_after = lax.ppermute(to_before, "slot", down_moves)
+    return small_call(final_kernel, "final_sum", ((CHUNK, f32),), kept, from_far, from_before, from_after)[0]
 
 
 def solution(mesh):

time: 163 us -> 165 us (1.012)
  waiting for transfers between devices: 56 us -> 62.6 us
  starting transfers between devices: 76.4 us -> 70.3 us
  local copies, waits for them, and re-layouts: 0.43 us -> 4.75 us
  other arithmetic: 4.12 us -> 0.31 us
    ppermute x4 -> x6, starting transfers between devices: 18.4 us -> 48.3 us  [the longest x2 24.3 us: per_device(): from_far = lax.ppermute(to_far, 'slot', far_moves)]
    ppermute x4 -> x6, waiting for transfers between devices: 14.7 us -> 38.5 us  [the longest x2 18.4 us: per_device(): from_after = lax.ppermute(to_before, 'slot', down_moves)]
    all_to_all x1 -> x0, starting transfers between devices: 19.3 us -> none  [per_device(): lax.all_to_all(messages, 'slot', split_axis=0, concat_axis=0, tiled=True)]
    all_to_all x1 -> x0, waiting for transfers between devices: 17.3 us -> none  [per_device(): lax.all_to_all(messages, 'slot', split_axis=0, concat_axis=0, tiled=True)]
    all_to_all x1, starting transfers between devices: 26.9 us -> 10.2 us  [per_device(): got = lax.all_to_all(sent, 'dp', split_axis=0, concat_axis=0, tiled=True)]
    unnamed x9 -> x21, local copies, waits for them, and re-layouts: 0.19 us -> 4.75 us
    concatenate x1 -> x0, other arithmetic: 1.97 us -> none  [per_device(): jnp.concatenate([pooled.reshape(N_SLOT, PAIR * slot_count, D), cotangent....]
  transfers between devices with their start and end apart: 10 -> 11, of which waited for: 7 -> 6; matrix products, arithmetic and copies ran while one was open for 0% -> 0% of each run, Pallas kernels for 9% -> 9%
where the time goes in v5:
time: 165 us; the launch traced here: 164 us
  starting transfers between devices  70.3 us (43%)
  waiting for transfers between devices  62.6 us (38%)
  Pallas kernels  25.7 us (16%)
  local copies, waits for them, and re-layouts  4.75 us (3%)
    ppermute x2, starting transfers between devices, per_device(): from_far = lax.ppermute(to_far, 'slot', far_moves)  24.3 us
    all_to_all x1, waiting for transfers between devices, per_device(): got = lax.all_to_all(sent, 'dp', split_axis=0, concat_axis=0, tiled=True)  20.9 us
    ppermute x2, waiting for transfers between devices, per_device(): from_after = lax.ppermute(to_before, 'slot', down_moves)  18.4 us
    ppermute x2, waiting for transfers between devices, per_device(): from_far = lax.ppermute(to_far, 'slot', far_moves)  16.3 us
    ppermute x2, starting transfers between devices, per_device(): from_before = lax.ppermute(to_after, 'slot', up_moves)  15.5 us
    pallas_call x3, Pallas kernels, run_later_bags(): pl.pallas_call(later_bags_kernel, out_shape=jax.ShapeDtypeStruct((2, 2, *...  13.8 us
    all_to_all x1, starting transfers between devices, per_device(): got = lax.all_to_all(sent, 'dp', split_axis=0, concat_axis=0, tiled=True)  10.2 us
    ppermute x2, starting transfers between devices, per_device(): from_after = lax.ppermute(to_before, 'slot', down_moves)  8.49 us
  transfers between devices with their start and end apart: 11, of which 6 were waited for; matrix products, arithmetic and copies ran while one was open for 0% of the time, Pallas kernels for 9%

profile of v5, /device:TPU:1, one launch (start us, length us, event | category | flops | bytes accessed | tf_op | source)
XLA Modules:
  0.0 164.0 jit_solution(9681275852368951048)
XLA Ops:
  0.7 0.9 copy-done
  3.7 11.5 %collective-permute-start = (bf16[560,128]{1,0:T(8,128)(2,1)S(1)}, bf16[560,128]{1,0:T(8,128)(2,1)S(1)}, u32[]{:S(2)}, u32[]{:S(2)}) collective-permute-start(bf16[560,128]{1,0:T(8,128)(2,1)S(1)} %get-tuple-element.24), channel_id=1, source_target_pairs={{0,4},{4,8},{8,12},{12,0},{1,5},{5,9},{9,13},{13,1},{2,6},{6,10},{... | collective-permute-start | bytes 430088 | tf_op jit(solution)/shard_map/ppermute | solution.py:361
  15.1 14.3 %collective-permute-start.1 = (bf16[560,128]{1,0:T(8,128)(2,1)S(1)}, bf16[560,128]{1,0:T(8,128)(2,1)S(1)}, u32[]{:S(2)}, u32[]{:S(2)}) collective-permute-start(bf16[560,128]{1,0:T(8,128)(2,1)S(1)} %get-tuple-element.25), channel_id=1, source_target_pairs={{0,8},{4,12},{8,0},{12,4},{1,9},{5,13},{9,1},{13,5},{2,10},{6,14},... | collective-permute-start | bytes 430088 | tf_op jit(solution)/shard_map/ppermute | solution.py:360
  29.4 3.4 %collective-permute-start.2 = (bf16[560,128]{1,0:T(8,128)(2,1)S(1)}, bf16[560,128]{1,0:T(8,128)(2,1)S(1)}, u32[]{:S(2)}, u32[]{:S(2)}) collective-permute-start(bf16[560,128]{1,0:T(8,128)(2,1)S(1)} %get-tuple-element.26), channel_id=1, source_target_pairs={{0,12},{4,0},{8,4},{12,8},{1,13},{5,1},{9,5},{13,9},{2,14},{6,2},{... | collective-permute-start | bytes 430088 | tf_op jit(solution)/shard_map/ppermute | solution.py:362
  33.0 16.3 %collective-permute-done.1.far_ref = bf16[560,128]{1,0:T(8,128)(2,1)S(1)} collective-permute-done((bf16[560,128]{1,0:T(8,128)(2,1)S(1)}, bf16[560,128]{1,0:T(8,128)(2,1)S(1)}, u32[]{:S(2)}, u32[]{:S(2)}) %collective-permute-start.1) | collective-permute-done | bytes 143392 | tf_op jit(solution)/shard_map/ppermute | solution.py:360
  49.3 4.9 %collective-permute-done.2.after_ref = bf16[560,128]{1,0:T(8,128)(2,1)S(1)} collective-permute-done((bf16[560,128]{1,0:T(8,128)(2,1)S(1)}, bf16[560,128]{1,0:T(8,128)(2,1)S(1)}, u32[]{:S(2)}, u32[]{:S(2)}) %collective-permute-start.2) | collective-permute-done | bytes 143392 | tf_op jit(solution)/shard_map/ppermute | solution.py:362
  54.2 1.2 copy-done.6
  55.5 5.2 %layers.1 = bf16[64,5,8,128]{3,2,1,0:T(8,128)(2,1)} custom-call(s32[1]{0:T(128)} %bitcast.12.here_ref, bf16[560,128]{1,0:T(8,128)(2,1)S(1)} %get-tuple-element.23.own_ref, bf16[560,128]{1,0:T(8,128)(2,1)S(1)} %collective-permute-done.before_ref, bf16[560,128]{1,0:T(8,128)(2,1)S(1)} %collective-permute-done.1.far_ref, ...), custom_call_target="tpu_custom_call" | custom-call | flops 2000000000 | bytes 4194304 | tf_op jit(solution)/shard_map/layers/pallas_call | solution.py:179
  60.6 10.2 %all-to-all-start = ((bf16[64,5,8,128]{3,2,1,0:T(8,128)(2,1)}), bf16[64,5,8,128]{3,2,1,0:T(8,128)(2,1)S(1)}, u32[]{:S(2)}, u32[]{:S(2)}) async-start(bf16[64,5,8,128]{3,2,1,0:T(8,128)(2,1)} %layers.1), calls=%async_computation | async-start | bytes 1310720 | tf_op jit(solution)/shard_map/all_to_all | solution.py:366
  71.0 20.9 %all-to-all-done.got_ref = bf16[64,5,8,128]{3,2,1,0:T(8,128)(2,1)S(1)} async-done(((bf16[64,5,8,128]{3,2,1,0:T(8,128)(2,1)}), bf16[64,5,8,128]{3,2,1,0:T(8,128)(2,1)S(1)}, u32[]{:S(2)}, u32[]{:S(2)}) %all-to-all-start) | async-done | bytes 655392 | tf_op jit(solution)/shard_map/all_to_all | solution.py:366
  91.9 5.3 %first_bags.1 = (bf16[2,2,2,256,128]{4,3,2,1,0:T(8,128)(2,1)S(1)}, bf16[8,256,256]{2,1,0:T(8,128)(2,1)S(1)}, f32[8,8,256]{2,1,0:T(8,128)S(1)}, f32[8,8,256]{2,1,0:T(8,128)S(1)}) custom-call(s32[4]{0:T(128)S(1)} %pad_add_fusion.2.blocks_ref, bf16[64,5,8,128]{3,2,1,0:T(8,128)(2,1)S(1)} %all-to-all-done.got_ref), custom_call_target="tpu_custom_call" | custom-call | flops 200000000 | bytes 1048576 | tf_op jit(solution)/shard_map/first_bags/pallas_call | solution.py:266
  97.3 3.1 %collective-permute-start.3 = (bf16[2,2,2,256,128]{4,3,2,1,0:T(8,128)(2,1)S(1)}, bf16[2,2,2,256,128]{4,3,2,1,0:T(8,128)(2,1)S(1)}, u32[]{:S(2)}, u32[]{:S(2)}) collective-permute-start(bf16[2,2,2,256,128]{4,3,2,1,0:T(8,128)(2,1)S(1)} %get-tuple-element.30), channel_id=1, source_target_pairs={{0,1},{1,0},{2,3},{3,2},{4,5},{5,4},{6,7},{7,6},{8,9},{9,8},{10,11... | collective-permute-start | bytes 1572872 | tf_op jit(solution)/shard_map/ppermute | solution.py:380
  100.5 4.6 %b_sent.1 = bf16[2,2,2,256,128]{4,3,2,1,0:T(8,128)(2,1)S(1)} custom-call(s32[4]{0:T(128)S(1)} %pad_add_fusion.3.blocks_ref, bf16[8,256,256]{2,1,0:T(8,128)(2,1)S(1)} %get-tuple-element.27.grads_ref, f32[8,8,256]{2,1,0:T(8,128)S(1)} %get-tuple-element.28.high_ref, f32[8,8,256]{2,1,0:T(8,128)S(1)} %get-tuple-element.29.low_ref), custom_call_target="tpu_custom_call" | custom-call | flops 200000000 | bytes 1048576 | tf_op jit(solution)/shard_map/b_sent/pallas_call | solution.py:284
  105.1 3.7 %collective-permute-start.4 = (bf16[2,2,2,256,128]{4,3,2,1,0:T(8,128)(2,1)S(1)}, bf16[2,2,2,256,128]{4,3,2,1,0:T(8,128)(2,1)S(1)}, u32[]{:S(2)}, u32[]{:S(2)}) collective-permute-start(bf16[2,2,2,256,128]{4,3,2,1,0:T(8,128)(2,1)S(1)} %b_sent.1), channel_id=1, source_target_pairs={{0,3},{1,2},{2,1},{3,0},{4,7},{5,6},{6,5},{7,4},{8,11},{9,10},{10,... | collective-permute-start | bytes 1572872 | tf_op jit(solution)/shard_map/ppermute | solution.py:382
  109.0 4.6 %a_kept.1.kept_ref = bf16[2,2,2,256,128]{4,3,2,1,0:T(8,128)(2,1)S(1)} custom-call(s32[4]{0:T(128)S(1)} %pad_add_fusion.1.blocks_ref, bf16[8,256,256]{2,1,0:T(8,128)(2,1)S(1)} %get-tuple-element.27.grads_ref, f32[8,8,256]{2,1,0:T(8,128)S(1)} %get-tuple-element.28.high_ref, f32[8,8,256]{2,1,0:T(8,128)S(1)} %get-tuple-element.29.low_ref), custom_call_target="tpu_custom_call" | custom-call | flops 200000000 | bytes 1048576 | tf_op jit(solution)/shard_map/a_kept/pallas_call | solution.py:284
  113.7 3.1 %collective-permute-start.6 = (bf16[2,2,256,128]{3,2,1,0:T(8,128)(2,1)S(1)}, bf16[2,2,256,128]{3,2,1,0:T(8,128)(2,1)S(1)}, u32[]{:S(2)}, u32[]{:S(2)}) collective-permute-start(bf16[2,2,256,128]{3,2,1,0:T(8,128)(2,1)S(1)} %get-tuple-element.37), channel_id=1, source_target_pairs={{0,3},{1,2},{2,1},{3,0},{4,7},{5,6},{6,5},{7,4},{8,11},{9,10},{10,... | collective-permute-start | bytes 786440 | tf_op jit(solution)/shard_map/ppermute | solution.py:386
  116.8 4.6 %b_kept.1.kept_ref = bf16[2,2,2,256,128]{4,3,2,1,0:T(8,128)(2,1)S(1)} custom-call(s32[4]{0:T(128)S(1)} %pad_add_fusion.blocks_ref, bf16[8,256,256]{2,1,0:T(8,128)(2,1)S(1)} %get-tuple-element.27.grads_ref, f32[8,8,256]{2,1,0:T(8,128)S(1)} %get-tuple-element.28.high_ref, f32[8,8,256]{2,1,0:T(8,128)S(1)} %get-tuple-element.29.low_ref), custom_call_target="tpu_custom_call" | custom-call | flops 200000000 | bytes 1048576 | tf_op jit(solution)/shard_map/b_kept/pallas_call | solution.py:284
  121.5 1.9 %collective-permute-start.5 = (bf16[2,2,256,128]{3,2,1,0:T(8,128)(2,1)S(1)}, bf16[2,2,256,128]{3,2,1,0:T(8,128)(2,1)S(1)}, u32[]{:S(2)}, u32[]{:S(2)}) collective-permute-start(bf16[2,2,256,128]{3,2,1,0:T(8,128)(2,1)S(1)} %get-tuple-element.34), channel_id=1, source_target_pairs={{0,1},{1,0},{2,3},{3,2},{4,5},{5,4},{6,7},{7,6},{8,9},{9,8},{10,11... | collective-permute-start | bytes 786440 | tf_op jit(solution)/shard_map/ppermute | solution.py:390
  123.5 3.1 %collective-permute-done.6.got_ref = bf16[2,2,256,128]{3,2,1,0:T(8,128)(2,1)S(1)} collective-permute-done((bf16[2,2,256,128]{3,2,1,0:T(8,128)(2,1)S(1)}, bf16[2,2,256,128]{3,2,1,0:T(8,128)(2,1)S(1)}, u32[]{:S(2)}, u32[]{:S(2)}) %collective-permute-start.6) | collective-permute-done | bytes 262176 | tf_op jit(solution)/shard_map/ppermute | solution.py:386
  126.7 10.0 %collective-permute-start.7 = (bf16[2,256,128]{2,1,0:T(8,128)(2,1)S(1)}, bf16[2,256,128]{2,1,0:T(8,128)(2,1)S(1)}, u32[]{:S(2)}, u32[]{:S(2)}) collective-permute-start(bf16[2,256,128]{2,1,0:T(8,128)(2,1)S(1)} %get-tuple-element.38), channel_id=1, source_target_pairs={{0,8},{4,12},{8,0},{12,4},{1,9},{5,13},{9,1},{13,5},{2,10},{6,14},... | collective-permute-start | bytes 393224 | tf_op jit(solution)/shard_map/ppermute | solution.py:393
  136.7 4.1 %collective-permute-start.8 = (bf16[2,256,128]{2,1,0:T(8,128)(2,1)S(1)}, bf16[2,256,128]{2,1,0:T(8,128)(2,1)S(1)}, u32[]{:S(2)}, u32[]{:S(2)}) collective-permute-start(bf16[2,256,128]{2,1,0:T(8,128)(2,1)S(1)} %get-tuple-element.39), channel_id=1, source_target_pairs={{0,4},{4,8},{8,12},{12,0},{1,5},{5,9},{9,13},{13,1},{2,6},{6,10},{... | collective-permute-start | bytes 393224 | tf_op jit(solution)/shard_map/ppermute | solution.py:394
  140.8 5.1 %collective-permute-start.9 = (bf16[2,256,128]{2,1,0:T(8,128)(2,1)S(1)}, bf16[2,256,128]{2,1,0:T(8,128)(2,1)S(1)}, u32[]{:S(2)}, u32[]{:S(2)}) collective-permute-start(bf16[2,256,128]{2,1,0:T(8,128)(2,1)S(1)} %get-tuple-element.40), channel_id=1, source_target_pairs={{0,12},{4,0},{8,4},{12,8},{1,13},{5,1},{9,5},{13,9},{2,14},{6,2},{... | collective-permute-start | bytes 393224 | tf_op jit(solution)/shard_map/ppermute | solution.py:396
  146.0 3.8 %collective-permute-done.8.before_ref = bf16[2,256,128]{2,1,0:T(8,128)(2,1)S(1)} collective-permute-done((bf16[2,256,128]{2,1,0:T(8,128)(2,1)S(1)}, bf16[2,256,128]{2,1,0:T(8,128)(2,1)S(1)}, u32[]{:S(2)}, u32[]{:S(2)}) %collective-permute-start.8) | collective-permute-done | bytes 131104 | tf_op jit(solution)/shard_map/ppermute | solution.py:394
  149.7 13.5 %collective-permute-done.9.after_ref = bf16[2,256,128]{2,1,0:T(8,128)(2,1)S(1)} collective-permute-done((bf16[2,256,128]{2,1,0:T(8,128)(2,1)S(1)}, bf16[2,256,128]{2,1,0:T(8,128)(2,1)S(1)}, u32[]{:S(2)}, u32[]{:S(2)}) %collective-permute-start.9) | collective-permute-done | bytes 131104 | tf_op jit(solution)/shard_map/ppermute | solution.py:396
  (34 shorter events, 4.3 us)
Async XLA Ops:
  0.0 0.7 copy-start.3
  0.0 0.7 copy-start.4
  0.0 0.7 copy-start.5
  0.7 1.0 copy-start
  1.6 0.9 copy-start.1
  2.6 0.8 copy-start.2
  3.4 29.4 %copy-start.9 = (bf16[2,512,32]{1,2,0:T(8,128)(2,1)S(1)}, bf16[2,512,32]{1,2,0:T(8,128)(2,1)}, u32[]{:S(2)}) copy-start(bf16[2,512,32]{1,2,0:T(8,128)(2,1)} %param.13) | copy-start | bytes 196612
  3.7 29.3 %collective-permute-start = (bf16[560,128]{1,0:T(8,128)(2,1)S(1)}, bf16[560,128]{1,0:T(8,128)(2,1)S(1)}, u32[]{:S(2)}, u32[]{:S(2)}) collective-permute-start(bf16[560,128]{1,0:T(8,128)(2,1)S(1)} %get-tuple-element.24), channel_id=1, source_target_pairs={{0,4},{4,8},{8,12},{12,0},{1,5},{5,9},{9,13},{13,1},{2,6},{6,10},{... | collective-permute-start | bytes 430088 | tf_op jit(solution)/shard_map/ppermute | solution.py:361
  15.1 34.2 %collective-permute-start.1 = (bf16[560,128]{1,0:T(8,128)(2,1)S(1)}, bf16[560,128]{1,0:T(8,128)(2,1)S(1)}, u32[]{:S(2)}, u32[]{:S(2)}) collective-permute-start(bf16[560,128]{1,0:T(8,128)(2,1)S(1)} %get-tuple-element.25), channel_id=1, source_target_pairs={{0,8},{4,12},{8,0},{12,4},{1,9},{5,13},{9,1},{13,5},{2,10},{6,14},... | collective-permute-start | bytes 430088 | tf_op jit(solution)/shard_map/ppermute | solution.py:360
  29.4 24.8 %copy-start.7 = (bf16[2,32,128]{2,1,0:T(8,128)(2,1)S(1)}, bf16[2,32,128]{2,1,0:T(8,128)(2,1)}, u32[]{:S(2)}) copy-start(bf16[2,32,128]{2,1,0:T(8,128)(2,1)} %output_ref.1) | copy-start | bytes 49156
  29.4 24.8 %collective-permute-start.2 = (bf16[560,128]{1,0:T(8,128)(2,1)S(1)}, bf16[560,128]{1,0:T(8,128)(2,1)S(1)}, u32[]{:S(2)}, u32[]{:S(2)}) collective-permute-start(bf16[560,128]{1,0:T(8,128)(2,1)S(1)} %get-tuple-element.26), channel_id=1, source_target_pairs={{0,12},{4,0},{8,4},{12,8},{1,13},{5,1},{9,5},{13,9},{2,14},{6,2},{... | collective-permute-start | bytes 430088 | tf_op jit(solution)/shard_map/ppermute | solution.py:362
  33.0 21.3 %copy-start.8 = (f32[2,128]{1,0:T(2,128)S(1)}, f32[2,128]{1,0:T(2,128)}, u32[]{:S(2)}) copy-start(f32[2,128]{1,0:T(2,128)} %gain_ref.1) | copy-start | bytes 3076
  54.2 1.2 copy-start.6
  60.6 31.3 %all-to-all-start = ((bf16[64,5,8,128]{3,2,1,0:T(8,128)(2,1)}), bf16[64,5,8,128]{3,2,1,0:T(8,128)(2,1)S(1)}, u32[]{:S(2)}, u32[]{:S(2)}) async-start(bf16[64,5,8,128]{3,2,1,0:T(8,128)(2,1)} %layers.1), calls=%async_computation | async-start | bytes 1310720 | tf_op jit(solution)/shard_map/all_to_all | solution.py:366
  97.3 16.3 %collective-permute-start.3 = (bf16[2,2,2,256,128]{4,3,2,1,0:T(8,128)(2,1)S(1)}, bf16[2,2,2,256,128]{4,3,2,1,0:T(8,128)(2,1)S(1)}, u32[]{:S(2)}, u32[]{:S(2)}) collective-permute-start(bf16[2,2,2,256,128]{4,3,2,1,0:T(8,128)(2,1)S(1)} %get-tuple-element.30), channel_id=1, source_target_pairs={{0,1},{1,0},{2,3},{3,2},{4,5},{5,4},{6,7},{7,6},{8,9},{9,8},{10,11... | collective-permute-start | bytes 1572872 | tf_op jit(solution)/shard_map/ppermute | solution.py:380
  105.1 16.3 %collective-permute-start.4 = (bf16[2,2,2,256,128]{4,3,2,1,0:T(8,128)(2,1)S(1)}, bf16[2,2,2,256,128]{4,3,2,1,0:T(8,128)(2,1)S(1)}, u32[]{:S(2)}, u32[]{:S(2)}) collective-permute-start(bf16[2,2,2,256,128]{4,3,2,1,0:T(8,128)(2,1)S(1)} %b_sent.1), channel_id=1, source_target_pairs={{0,3},{1,2},{2,1},{3,0},{4,7},{5,6},{6,5},{7,4},{8,11},{9,10},{10,... | collective-permute-start | bytes 1572872 | tf_op jit(solution)/shard_map/ppermute | solution.py:382
  113.7 12.9 %collective-permute-start.6 = (bf16[2,2,256,128]{3,2,1,0:T(8,128)(2,1)S(1)}, bf16[2,2,256,128]{3,2,1,0:T(8,128)(2,1)S(1)}, u32[]{:S(2)}, u32[]{:S(2)}) collective-permute-start(bf16[2,2,256,128]{3,2,1,0:T(8,128)(2,1)S(1)} %get-tuple-element.37), channel_id=1, source_target_pairs={{0,3},{1,2},{2,1},{3,0},{4,7},{5,6},{6,5},{7,4},{8,11},{9,10},{10,... | collective-permute-start | bytes 786440 | tf_op jit(solution)/shard_map/ppermute | solution.py:386
  121.5 19.2 %collective-permute-start.5 = (bf16[2,2,256,128]{3,2,1,0:T(8,128)(2,1)S(1)}, bf16[2,2,256,128]{3,2,1,0:T(8,128)(2,1)S(1)}, u32[]{:S(2)}, u32[]{:S(2)}) collective-permute-start(bf16[2,2,256,128]{3,2,1,0:T(8,128)(2,1)S(1)} %get-tuple-element.34), channel_id=1, source_target_pairs={{0,1},{1,0},{2,3},{3,2},{4,5},{5,4},{6,7},{7,6},{8,9},{9,8},{10,11... | collective-permute-start | bytes 786440 | tf_op jit(solution)/shard_map/ppermute | solution.py:390
  126.7 19.3 %collective-permute-start.7 = (bf16[2,256,128]{2,1,0:T(8,128)(2,1)S(1)}, bf16[2,256,128]{2,1,0:T(8,128)(2,1)S(1)}, u32[]{:S(2)}, u32[]{:S(2)}) collective-permute-start(bf16[2,256,128]{2,1,0:T(8,128)(2,1)S(1)} %get-tuple-element.38), channel_id=1, source_target_pairs={{0,8},{4,12},{8,0},{12,4},{1,9},{5,13},{9,1},{13,5},{2,10},{6,14},... | collective-permute-start | bytes 393224 | tf_op jit(solution)/shard_map/ppermute | solution.py:393
  136.7 13.1 %collective-permute-start.8 = (bf16[2,256,128]{2,1,0:T(8,128)(2,1)S(1)}, bf16[2,256,128]{2,1,0:T(8,128)(2,1)S(1)}, u32[]{:S(2)}, u32[]{:S(2)}) collective-permute-start(bf16[2,256,128]{2,1,0:T(8,128)(2,1)S(1)} %get-tuple-element.39), channel_id=1, source_target_pairs={{0,4},{4,8},{8,12},{12,0},{1,5},{5,9},{9,13},{13,1},{2,6},{6,10},{... | collective-permute-start | bytes 393224 | tf_op jit(solution)/shard_map/ppermute | solution.py:394
  140.8 22.4 %collective-permute-start.9 = (bf16[2,256,128]{2,1,0:T(8,128)(2,1)S(1)}, bf16[2,256,128]{2,1,0:T(8,128)(2,1)S(1)}, u32[]{:S(2)}, u32[]{:S(2)}) collective-permute-start(bf16[2,256,128]{2,1,0:T(8,128)(2,1)S(1)} %get-tuple-element.40), channel_id=1, source_target_pairs={{0,12},{4,0},{8,4},{12,8},{1,13},{5,1},{9,5},{13,9},{2,14},{6,2},{... | collective-permute-start | bytes 393224 | tf_op jit(solution)/shard_map/ppermute | solution.py:396

commit v6 on v5

--- a/solution.py
+++ b/solution.py
@@ -31,6 +31,7 @@
 bf16 = jnp.bfloat16
 
 
+ANY_SPEC = pl.BlockSpec(memory_space=pl.ANY)
 VMEM_SPEC = pl.BlockSpec(memory_space=pltpu.VMEM)
 SMEM_SPEC = pl.BlockSpec(memory_space=pltpu.SMEM)
 
@@ -44,8 +45,22 @@
 
 
 def messages_kernel(
-    here_ref, pooled_ref, cotangent_ref, ids_ref, lengths_ref, slot_ref, home_ref, *out_refs
+    place_ref, pooled_ref, cotangent_ref, ids_any, lengths_any, slot_ref, home_ref, *refs
 ):
+    out_refs, (ids_ref, lengths_ref, tail_ref, sems, small_sems) = refs[:N_SLOT], refs[N_SLOT:]
+    small = [
+        pltpu.make_async_copy(ids_any, ids_ref, small_sems.at[0]),
+        pltpu.make_async_copy(lengths_any, lengths_ref, small_sems.at[1]),
+    ]
+    for copy in small:
+        copy.start()
+    copies = []
+    for r in (2, 1, 3, 0):
+        dest = lax.rem(place_ref[0] + r, N_SLOT)
+        for part, source in enumerate((pooled_ref, cotangent_ref)):
+            rows = pl.ds(part * POOLED_ROWS, POOLED_ROWS)
+            copies.append(pltpu.make_async_copy(source.at[dest], out_refs[r].at[rows], sems.at[r, part]))
+            copies[-1].start()
     slots = slot_ref[...]
     hot = jnp.where(iota((SLOT_DEV, SLOT_DEV), 0) == slots, 1.0, 0.0).astype(bf16)
     homes = jnp.broadcast_to(home_ref[...].astype(f32), (8, SLOT_DEV)).astype(bf16)
@@ -58,38 +73,61 @@
     table = across % TABLE_DEV * 16
     marks = jnp.broadcast_to(target, (16, SLOT_DEV)).astype(bf16)
     entry = iota((BAG, SLOT_DEV), 0)
+    for copy in small:
+        copy.wait()
     for r, out_ref in enumerate(out_refs):
-        dest = lax.rem(here_ref[0] + r, N_SLOT)
-        out_ref[:POOLED_ROWS] = pooled_ref[dest]
-        out_ref[POOLED_ROWS : 2 * POOLED_ROWS] = cotangent_ref[dest]
+        dest = lax.rem(place_ref[0] + r, N_SLOT)
         parts = []
         for b in range(PAIR):
             ids = ids_ref[dest * PAIR + b]
-            live = entry < lengths_ref[dest * PAIR + b]
+            live = entry < lengths_ref[pl.ds(dest * PAIR + b, 1), :]
             parts.append((jnp.where(live, ids // ROW_BLOCK, DEAD) + table).astype(f32))
             parts.append((ids % ROW_BLOCK).astype(f32))
-        out_ref[2 * POOLED_ROWS : 2 * POOLED_ROWS + ID_ROWS] = jnp.concatenate(parts, axis=0).astype(bf16)
-        out_ref[2 * POOLED_ROWS + ID_ROWS :] = marks
-
-
-def make_messages(here, *args):
+        tail_ref[r, :ID_ROWS] = jnp.concatenate(parts, axis=0).astype(bf16)
+        tail_ref[r, ID_ROWS:] = marks
+        rows = pl.ds(2 * POOLED_ROWS, ID_ROWS + 16)
+        copies.append(pltpu.make_async_copy(tail_ref.at[r], out_ref.at[rows], sems.at[r, 2]))
+        copies[-1].start()
+    for copy in copies:
+        copy.wait()
+
+
+def make_messages(place, *args):
     message = jax.ShapeDtypeStruct((MSG_ROWS, D), bf16)
     return pl.pallas_call(
         messages_kernel,
         out_shape=(message,) * N_SLOT,
-        in_specs=[SMEM_SPEC] + [VMEM_SPEC] * len(args),
-        out_specs=(VMEM_SPEC,) * N_SLOT,
-        compiler_params=pltpu.CompilerParams(vmem_limit_bytes=16 << 20),
+        in_specs=[SMEM_SPEC] + [ANY_SPEC] * 4 + [VMEM_SPEC] * 2,
+        out_specs=(ANY_SPEC,) * N_SLOT,
+        scratch_shapes=[
+            pltpu.VMEM((N_SLOT * PAIR, BAG, SLOT_DEV), jnp.int32),
+            pltpu.VMEM((N_SLOT * PAIR, SLOT_DEV), jnp.int32),
+            pltpu.VMEM((N_SLOT, ID_ROWS + 16, SLOT_DEV), bf16),
+            pltpu.SemaphoreType.DMA((N_SLOT, 3)),
+            pltpu.SemaphoreType.DMA((2,)),
+        ],
+        compiler_params=pltpu.CompilerParams(vmem_limit_bytes=56 << 20),
         cost_estimate=pl.CostEstimate(flops=1_000_000, bytes_accessed=2 << 20, transcendentals=0),
         name="messages",
-    )(here, *args)
+    )(place, *args)
 
 
 def layers_kernel(
-    here_ref, own_ref, before_ref, far_ref, after_ref, compress_ref, basis_ref, output_ref, gain_ref, out_ref, x_ref
+    place_ref, own_ref, before_ref, far_ref, after_ref, compress_any, basis_ref, output_ref, gain_ref,
+    out_ref, x_ref, compress_ref, sems
 ):
+    inputs = []
     for r, ref in enumerate((own_ref, after_ref, far_ref, before_ref)):
-        x_ref[lax.rem(here_ref[0] + r, N_SLOT)] = ref[...]
+        index = lax.rem(place_ref[0] + r, N_SLOT)
+        inputs.append(pltpu.make_async_copy(ref, x_ref.at[index], sems.at[LAYERS + r]))
+        inputs[-1].start()
+    fetches = [
+        pltpu.make_async_copy(compress_any.at[k], compress_ref.at[k], sems.at[k]) for k in range(LAYERS)
+    ]
+    for fetch in fetches:
+        fetch.start()
+    for copy in inputs:
+        copy.wait()
     gain = gain_ref[...]
     pair_rows = POOLED_ROWS
     current = []
@@ -103,6 +141,7 @@
     for layer in range(LAYERS):
         wide = jnp.concatenate(current, axis=1)
         coefficient = dot(basis_ref[layer], wide, 0, 0).astype(bf16)
+        fetches[layer].wait()
         mixed = dot(compress_ref[layer], wide)
         following = []
         entry = []
@@ -175,17 +214,21 @@
     out_ref[:, N_SLOT] = ids.astype(bf16).reshape(DP, 8, D)
 
 
-def run_layers(here, *args):
+def run_layers(place, *args):
     return pl.pallas_call(
         layers_kernel,
         out_shape=jax.ShapeDtypeStruct((DP, N_SLOT + 1, 8, D), bf16),
-        in_specs=[SMEM_SPEC] + [VMEM_SPEC] * len(args),
+        in_specs=[SMEM_SPEC] + [ANY_SPEC] * 5 + [VMEM_SPEC] * 3,
         out_specs=VMEM_SPEC,
-        scratch_shapes=[pltpu.VMEM((N_SLOT, MSG_ROWS, D), bf16)],
-        compiler_params=pltpu.CompilerParams(vmem_limit_bytes=20 << 20),
+        scratch_shapes=[
+            pltpu.VMEM((N_SLOT, MSG_ROWS, D), bf16),
+            pltpu.VMEM((LAYERS, SLOTS, SLOTS), bf16),
+            pltpu.SemaphoreType.DMA((LAYERS + N_SLOT,)),
+        ],
+        compiler_params=pltpu.CompilerParams(vmem_limit_bytes=56 << 20),
         cost_estimate=pl.CostEstimate(flops=2_000_000_000, bytes_accessed=4 << 20, transcendentals=4096),
         name="layers",
-    )(here, *args)
+    )(place, *args)
 
 
 def prepare_bags(got_ref, wide_ref, grads_ref, high_ref, low_ref):
@@ -219,7 +262,7 @@
             grads_ref[cap // 2, rows, D:] = (values * table).astype(bf16)
 
 
-def add_rows(blocks_ref, out_ref, grads_ref, high_ref, low_ref):
+def add_rows(ahead, place_ref, out_ref, grads_ref, high_ref, low_ref, more_ref=None):
     lanes = 2 * PAIR * DP
     half = ROW_BLOCK // 2
     rows_of = iota((half, lanes), 0).astype(f32).astype(bf16)
@@ -227,7 +270,9 @@
     zero = jnp.zeros((), bf16)
 
     def block(index, carry):
-        want = blocks_ref[index].astype(f32)
+        chunk = lax.rem(place_ref[0] + index, N_SLOT)
+        group = lax.rem(place_ref[1] + ahead, N_GRP)
+        want = (chunk * N_GRP + group).astype(f32)
         for part in range(2):
             total = jnp.zeros((half, 2 * D), f32)
             for p in range(N_SLOT * CAPACITY // 2):
@@ -239,34 +284,37 @@
                     count = count + jnp.where(rows_of == wanted, one, zero)
                 total = total + dot(count, grads_ref[p])
             rows = slice(part * half, (part + 1) * half)
-            out_ref[index // 2, index % 2, 0, rows] = total[:, :D].astype(bf16)
-            out_ref[index // 2, index % 2, 1, rows] = total[:, D:].astype(bf16)
+            sums = [total[:, :D], total[:, D:]]
+            if more_ref is not None:
+                sums = [sums[t] + more_ref[index, t, rows].astype(f32) for t in range(TABLE_DEV)]
+            for t in range(TABLE_DEV):
+                out_ref[index, t, rows] = sums[t].astype(bf16)
         return carry
 
-    lax.fori_loop(0, 4, block, 0)
-
-
-def first_bags_kernel(blocks_ref, got_ref, out_ref, grads_ref, high_ref, low_ref, wide_ref):
+    lax.fori_loop(0, N_SLOT, block, 0)
+
+
+def first_bags_kernel(ahead, place_ref, got_ref, out_ref, grads_ref, high_ref, low_ref, wide_ref):
     prepare_bags(got_ref, wide_ref, grads_ref, high_ref, low_ref)
-    add_rows(blocks_ref, out_ref, grads_ref, high_ref, low_ref)
-
-
-def later_bags_kernel(blocks_ref, grads_ref, high_ref, low_ref, out_ref):
-    add_rows(blocks_ref, out_ref, grads_ref, high_ref, low_ref)
-
-
-BAGS_COST = pl.CostEstimate(flops=200_000_000, bytes_accessed=1 << 20, transcendentals=0)
+    add_rows(ahead, place_ref, out_ref, grads_ref, high_ref, low_ref)
+
+
+def later_bags_kernel(ahead, place_ref, grads_ref, high_ref, low_ref, *refs):
+    add_rows(ahead, place_ref, refs[-1], grads_ref, high_ref, low_ref, *refs[:-1])
+
+
+BAGS_COST = pl.CostEstimate(flops=1000, bytes_accessed=1000, transcendentals=0)
 ADD_COST = pl.CostEstimate(flops=1_000_000, bytes_accessed=1 << 20, transcendentals=0)
 CHUNK = (TABLE_DEV, ROW_BLOCK, D)
 
 
-def run_first_bags(blocks, got):
+def run_first_bags(ahead, place, got):
     pairs = N_SLOT * CAPACITY // 2
     lanes = 2 * PAIR * DP
     return pl.pallas_call(
-        first_bags_kernel,
+        functools.partial(first_bags_kernel, ahead),
         out_shape=(
-            jax.ShapeDtypeStruct((2, 2, *CHUNK), bf16),
+            jax.ShapeDtypeStruct((N_SLOT, *CHUNK), bf16),
             jax.ShapeDtypeStruct((pairs, lanes, 2 * D), bf16),
             jax.ShapeDtypeStruct((pairs, BAG, lanes), f32),
             jax.ShapeDtypeStruct((pairs, BAG, lanes), f32),
@@ -277,19 +325,19 @@
         compiler_params=pltpu.CompilerParams(vmem_limit_bytes=24 << 20),
         cost_estimate=BAGS_COST,
         name="first_bags",
-    )(blocks, got)
-
-
-def run_later_bags(blocks, prepared, name):
+    )(place, got)
+
+
+def run_later_bags(ahead, place, prepared, name, *more):
     return pl.pallas_call(
-        later_bags_kernel,
-        out_shape=jax.ShapeDtypeStruct((2, 2, *CHUNK), bf16),
-        in_specs=[SMEM_SPEC] + [VMEM_SPEC] * 3,
+        functools.partial(later_bags_kernel, ahead),
+        out_shape=jax.ShapeDtypeStruct((N_SLOT, *CHUNK), bf16),
+        in_specs=[SMEM_SPEC] + [VMEM_SPEC] * (3 + len(more)),
         out_specs=VMEM_SPEC,
         compiler_params=pltpu.CompilerParams(vmem_limit_bytes=24 << 20),
         cost_estimate=BAGS_COST,
         name=name,
-    )(blocks, *prepared)
+    )(place, *prepared, *more)
 
 
 def wide_sum(*refs):
@@ -299,19 +347,11 @@
     return total
 
 
-def add_parts_kernel(kept_ref, got_ref, own_ref, sent_ref):
-    own_ref[...] = wide_sum(kept_ref.at[0], got_ref.at[0]).astype(bf16)
-    sent_ref[...] = wide_sum(kept_ref.at[1], got_ref.at[1]).astype(bf16)
-
-
-def sum_a_kernel(own_ref, got_ref, far_ref, after_ref):
-    far_ref[...] = wide_sum(own_ref.at[0], got_ref.at[0]).astype(bf16)
-    after_ref[...] = wide_sum(own_ref.at[1], got_ref.at[1]).astype(bf16)
-
-
-def sum_b_kernel(own_ref, got_ref, kept_ref, before_ref):
-    kept_ref[...] = wide_sum(own_ref.at[0], got_ref.at[0])
-    before_ref[...] = wide_sum(own_ref.at[1], got_ref.at[1]).astype(bf16)
+def grp_sum_kernel(own_ref, a_ref, b_ref, kept_ref, after_ref, far_ref, before_ref):
+    parts = (own_ref, a_ref, b_ref)
+    kept_ref[...] = wide_sum(*(part.at[0] for part in parts))
+    for r, ref in ((1, after_ref), (2, far_ref), (3, before_ref)):
+        ref[...] = wide_sum(*(part.at[r] for part in parts)).astype(bf16)
 
 
 def final_kernel(kept_ref, far_ref, before_ref, after_ref, out_ref):
@@ -343,17 +383,16 @@
     slot_table,
     table_home,
 ):
-    here = lax.axis_index("slot").astype(jnp.int32)
-    at_slot = here.reshape(1)
+    place = jnp.stack([lax.axis_index("slot"), lax.axis_index("grp")]).astype(jnp.int32)
     up_moves, far_moves, down_moves = (
         [(i, (i + step) % N_SLOT) for i in range(N_SLOT)] for step in (1, 2, 3)
     )
     own, to_after, to_far, to_before = make_messages(
-        at_slot,
+        place,
         pooled.reshape(N_SLOT, POOLED_ROWS, D),
         cotangent.reshape(N_SLOT, POOLED_ROWS, D),
         jnp.transpose(bag_ids, (0, 2, 1)),
-        bag_lengths.reshape(-1, 1, SLOT_DEV),
+        bag_lengths,
         slot_table.reshape(1, SLOT_DEV),
         table_home.reshape(1, -1),
     )
@@ -361,38 +400,22 @@
     from_before = lax.ppermute(to_after, "slot", up_moves)
     from_after = lax.ppermute(to_before, "slot", down_moves)
     sent = run_layers(
-        at_slot, own, from_before, from_far, from_after, compress_weight, fm_basis, fm_output, norm_gain
+        place, own, from_before, from_far, from_after, compress_weight, fm_basis, fm_output, norm_gain
     )
     got = lax.all_to_all(sent, "dp", split_axis=0, concat_axis=0, tiled=True)
-    me = lax.axis_index("grp").astype(jnp.int32)
-    side = me ^ 1
-    mirror = N_GRP - 1 - me
-    across = side ^ 3
-    far, after, before = (here + 2) % N_SLOT, (here + 1) % N_SLOT, (here + 3) % N_SLOT
-
-    def blocks(groups, chunks):
-        return jnp.stack([chunk * N_GRP + group for group in groups for chunk in chunks])
-
-    half_a, half_b = (far, after), (here, before)
-    side_moves = [(i, i ^ 1) for i in range(N_GRP)]
-    mirror_moves = [(i, N_GRP - 1 - i) for i in range(N_GRP)]
-    a_sent, *prepared = run_first_bags(blocks((side, across), half_a), got)
-    a_got = lax.ppermute(a_sent, "grp", side_moves)
-    b_sent = run_later_bags(blocks((mirror, across), half_b), prepared, "b_sent")
-    b_got = lax.ppermute(b_sent, "grp", mirror_moves)
-    a_kept = run_later_bags(blocks((me, mirror), half_a), prepared, "a_kept")
-    part = ((2, *CHUNK), bf16)
-    a_own, a_next = small_call(add_parts_kernel, "add_a", (part, part), a_kept, a_got)
-    a_last = lax.ppermute(a_next, "grp", mirror_moves)
-    b_blocks, a_own = lax.optimization_barrier((blocks((me, side), half_b), a_own))
-    b_kept = run_later_bags(b_blocks, prepared, "b_kept")
-    b_own, b_next = small_call(add_parts_kernel, "add_b", (part, part), b_kept, b_got)
-    b_last = lax.ppermute(b_next, "grp", side_moves)
+    far_part, *prepared = run_first_bags(2, place, got)
+    far_part = lax.ppermute(far_part, "grp", far_moves)
+    next_part = run_later_bags(1, place, prepared, "next_rows")
+    next_part = lax.ppermute(next_part, "grp", up_moves)
+    last_part = run_later_bags(3, place, prepared, "last_rows")
+    last_part = lax.ppermute(last_part, "grp", down_moves)
+    own_part = run_later_bags(0, place, prepared, "own_rows", far_part)
     chunk = (CHUNK, bf16)
-    to_far, to_after = small_call(sum_a_kernel, "sum_a", (chunk, chunk), a_own, a_last)
+    kept, to_after, to_far, to_before = small_call(
+        grp_sum_kernel, "grp_sum", ((CHUNK, f32), chunk, chunk, chunk), own_part, next_part, last_part
+    )
     from_far = lax.ppermute(to_far, "slot", far_moves)
     from_before = lax.ppermute(to_after, "slot", up_moves)
-    kept, to_before = small_call(sum_b_kernel, "sum_b", ((CHUNK, f32), chunk), b_own, b_last)
     from_after = lax.ppermute(to_before, "slot", down_moves)
     return small_call(final_kernel, "final_sum", ((CHUNK, f32),), kept, from_far, from_before, from_after)[0]
 

time: 165 us -> 183 us (1.11)
  blocking collectives: 0 us -> 31.3 us
  Pallas kernels: 25.7 us -> 45.3 us
  waiting for transfers between devices: 62.6 us -> 43.8 us
  starting transfers between devices: 70.3 us -> 59.4 us
  local copies, waits for them, and re-layouts: 4.75 us -> 1.52 us
    all_to_all x0 -> x1, blocking collectives: none -> 31.3 us  [per_device(): got = lax.all_to_all(sent, 'dp', split_axis=0, concat_axis=0, tiled=True)]
    all_to_all x1 -> x0, waiting for transfers between devices: 20.9 us -> none  [per_device(): got = lax.all_to_all(sent, 'dp', split_axis=0, concat_axis=0, tiled=True)]
    pallas_call x1, Pallas kernels: 0.3 us -> 17.9 us  [make_messages(): pl.pallas_call(messages_kernel, out_shape=(message,) * N_SLOT, in_specs=[...]
    all_to_all x1 -> x0, starting transfers between devices: 10.2 us -> none  [per_device(): got = lax.all_to_all(sent, 'dp', split_axis=0, concat_axis=0, tiled=True)]
    unnamed x21 -> x11, local copies, waits for them, and re-layouts: 4.75 us -> 1.52 us
    ppermute x4 -> x3, waiting for transfers between devices: 3.14 us -> 5.63 us  [the longest x1 3.44 us: per_device(): next_part = lax.ppermute(next_part, 'grp', up_moves)]
    pallas_call x1, Pallas kernels: 5.16 us -> 7.31 us  [run_layers(): pl.pallas_call(layers_kernel, out_shape=jax.ShapeDtypeStruct((DP, N_SLOT...]
    ppermute x4 -> x3, starting transfers between devices: 11.8 us -> 11.1 us  [the longest x1 4.65 us: per_device(): far_part = lax.ppermute(far_part, 'grp', far_moves)]
  transfers between devices with their start and end apart: 11 -> 9, of which waited for: 6 -> 6; matrix products, arithmetic and copies ran while one was open for 0% -> 0% of each run, Pallas kernels for 9% -> 8%
where the time goes in v6:
time: 183 us; the launch traced here: 182 us
  starting transfers between devices  59.4 us (32%)
  Pallas kernels  45.3 us (25%)
  waiting for transfers between devices  43.8 us (24%)
  blocking collectives  31.3 us (17%)
    all_to_all x1, blocking collectives, per_device(): got = lax.all_to_all(sent, 'dp', split_axis=0, concat_axis=0, tiled=True)  31.3 us
    ppermute x2, starting transfers between devices, per_device(): from_far = lax.ppermute(to_far, 'slot', far_moves)  24.2 us
    ppermute x2, waiting for transfers between devices, per_device(): from_after = lax.ppermute(to_before, 'slot', down_moves)  18.2 us
    pallas_call x1, Pallas kernels, make_messages(): pl.pallas_call(messages_kernel, out_shape=(message,) * N_SLOT, in_specs=[...  17.9 us
    ppermute x2, waiting for transfers between devices, per_device(): from_far = lax.ppermute(to_far, 'slot', far_moves)  15.9 us
    ppermute x2, starting transfers between devices, per_device(): from_before = lax.ppermute(to_after, 'slot', up_moves)  15.5 us
    pallas_call x3, Pallas kernels, run_later_bags(): pl.pallas_call(functools.partial(later_bags_kernel, ahead), out_shape=jax...  13.8 us
    ppermute x2, starting transfers between devices, per_device(): from_after = lax.ppermute(to_before, 'slot', down_moves)  8.47 us
  transfers between devices with their start and end apart: 9, of which 6 were waited for; matrix products, arithmetic and copies ran while one was open for 0% of the time, Pallas kernels for 8%

profile of v6, /device:TPU:1, one launch (start us, length us, event | category | flops | bytes accessed | tf_op | source)
XLA Modules:
  0.0 182.1 jit_solution(327054919929498663)
XLA Ops:
  0.6 17.9 %messages.1 = (bf16[560,128]{1,0:T(8,128)(2,1)}, bf16[560,128]{1,0:T(8,128)(2,1)}, bf16[560,128]{1,0:T(8,128)(2,1)}, bf16[560,128]{1,0:T(8,128)(2,1)}) custom-call(s32[2]{0:T(128)} %pad_add_fusion.place_ref, bf16[4,256,128]{2,1,0:T(8,128)(2,1)} %bitcast.7, bf16[4,256,128]{2,1,0:T(8,128)(2,1)} %bitcast.8, s32[8,8,128]{2,1,0:T(8,128)} %bitcast.9, ...), custom_call_target="tpu_custom_call" | custom-call | flops 1000000 | bytes 2097152 | tf_op jit(solution)/shard_map/messages/pallas_call | solution.py:97
  18.5 11.5 %collective-permute-start = (bf16[560,128]{1,0:T(8,128)(2,1)}, bf16[560,128]{1,0:T(8,128)(2,1)S(1)}, u32[]{:S(2)}, u32[]{:S(2)}) collective-permute-start(bf16[560,128]{1,0:T(8,128)(2,1)} %get-tuple-element.18), channel_id=1, source_target_pairs={{0,4},{4,8},{8,12},{12,0},{1,5},{5,9},{9,13},{13,1},{2,6},{6,10},{... | collective-permute-start | bytes 430088 | tf_op jit(solution)/shard_map/ppermute | solution.py:400
  30.0 14.3 %collective-permute-start.1 = (bf16[560,128]{1,0:T(8,128)(2,1)}, bf16[560,128]{1,0:T(8,128)(2,1)S(1)}, u32[]{:S(2)}, u32[]{:S(2)}) collective-permute-start(bf16[560,128]{1,0:T(8,128)(2,1)} %get-tuple-element.19), channel_id=1, source_target_pairs={{0,8},{4,12},{8,0},{12,4},{1,9},{5,13},{9,1},{13,5},{2,10},{6,14},... | collective-permute-start | bytes 430088 | tf_op jit(solution)/shard_map/ppermute | solution.py:399
  44.3 3.4 %collective-permute-start.2 = (bf16[560,128]{1,0:T(8,128)(2,1)}, bf16[560,128]{1,0:T(8,128)(2,1)S(1)}, u32[]{:S(2)}, u32[]{:S(2)}) collective-permute-start(bf16[560,128]{1,0:T(8,128)(2,1)} %get-tuple-element.20), channel_id=1, source_target_pairs={{0,12},{4,0},{8,4},{12,8},{1,13},{5,1},{9,5},{13,9},{2,14},{6,2},{... | collective-permute-start | bytes 430088 | tf_op jit(solution)/shard_map/ppermute | solution.py:401
  47.7 0.8 copy.11.basis_ref
  48.5 15.9 %collective-permute-done.1.far_ref = bf16[560,128]{1,0:T(8,128)(2,1)S(1)} collective-permute-done((bf16[560,128]{1,0:T(8,128)(2,1)}, bf16[560,128]{1,0:T(8,128)(2,1)S(1)}, u32[]{:S(2)}, u32[]{:S(2)}) %collective-permute-start.1) | collective-permute-done | bytes 143392 | tf_op jit(solution)/shard_map/ppermute | solution.py:399
  64.4 4.9 %collective-permute-done.2.after_ref = bf16[560,128]{1,0:T(8,128)(2,1)S(1)} collective-permute-done((bf16[560,128]{1,0:T(8,128)(2,1)}, bf16[560,128]{1,0:T(8,128)(2,1)S(1)}, u32[]{:S(2)}, u32[]{:S(2)}) %collective-permute-start.2) | collective-permute-done | bytes 143392 | tf_op jit(solution)/shard_map/ppermute | solution.py:401
  70.0 7.3 %layers.1 = bf16[64,5,8,128]{3,2,1,0:T(8,128)(2,1)} custom-call(s32[2]{0:T(128)} %pad_add_fusion.place_ref, bf16[560,128]{1,0:T(8,128)(2,1)} %get-tuple-element.17.own_ref, bf16[560,128]{1,0:T(8,128)(2,1)} %copy-done.2, bf16[560,128]{1,0:T(8,128)(2,1)} %copy-done.3, bf16[560,128]{1,0:T(8,128)(2,1)} %copy-done.4, bf16[2,512,512]{2,1,0:T(8,128)(2,1)} %compress_any.1, ...), custom_call_target="tpu_custom_call" | custom-call | flops 2000000000 | bytes 4194304 | tf_op jit(solution)/shard_map/layers/pallas_call | solution.py:218
  77.3 31.3 %all_to_all.5.got_ref = bf16[64,5,8,128]{3,2,1,0:T(8,128)(2,1)S(1)} all-to-all(bf16[64,5,8,128]{3,2,1,0:T(8,128)(2,1)} %layers.1), channel_id=1, replica_groups=mesh['dp'=64,'slot'=4,'grp'=4] {'dp'}, dimensions={0} | all-to-all | bytes 1310720 | tf_op jit(solution)/shard_map/all_to_all | solution.py:405
  108.6 5.3 %first_bags.1 = (bf16[4,2,256,128]{3,2,1,0:T(8,128)(2,1)S(1)}, bf16[8,256,256]{2,1,0:T(8,128)(2,1)S(1)}, f32[8,8,256]{2,1,0:T(8,128)S(1)}, f32[8,8,256]{2,1,0:T(8,128)S(1)}) custom-call(s32[2]{0:T(128)S(1)} %copy-done, bf16[64,5,8,128]{3,2,1,0:T(8,128)(2,1)S(1)} %all_to_all.5.got_ref), custom_call_target="tpu_custom_call" | custom-call | flops 1000 | bytes 1000 | tf_op jit(solution)/shard_map/first_bags/pallas_call | solution.py:314
  114.0 4.6 %collective-permute-start.3 = (bf16[4,2,256,128]{3,2,1,0:T(8,128)(2,1)S(1)}, bf16[4,2,256,128]{3,2,1,0:T(8,128)(2,1)S(1)}, u32[]{:S(2)}, u32[]{:S(2)}) collective-permute-start(bf16[4,2,256,128]{3,2,1,0:T(8,128)(2,1)S(1)} %get-tuple-element.24), channel_id=1, source_target_pairs={{0,2},{1,3},{2,0},{3,1},{4,6},{5,7},{6,4},{7,5},{8,10},{9,11},{10,... | collective-permute-start | bytes 1572872 | tf_op jit(solution)/shard_map/ppermute | solution.py:407
  118.6 4.6 %next_rows.1 = bf16[4,2,256,128]{3,2,1,0:T(8,128)(2,1)S(1)} custom-call(s32[2]{0:T(128)S(1)} %copy-done, bf16[8,256,256]{2,1,0:T(8,128)(2,1)S(1)} %get-tuple-element.21.grads_ref, f32[8,8,256]{2,1,0:T(8,128)S(1)} %get-tuple-element.22.high_ref, f32[8,8,256]{2,1,0:T(8,128)S(1)} %get-tuple-element.23.low_ref), custom_call_target="tpu_custom_call" | custom-call | flops 1000 | bytes 1000 | tf_op jit(solution)/shard_map/next_rows/pallas_call | solution.py:332
  123.3 2.2 %collective-permute-start.4 = (bf16[4,2,256,128]{3,2,1,0:T(8,128)(2,1)S(1)}, bf16[4,2,256,128]{3,2,1,0:T(8,128)(2,1)S(1)}, u32[]{:S(2)}, u32[]{:S(2)}) collective-permute-start(bf16[4,2,256,128]{3,2,1,0:T(8,128)(2,1)S(1)} %next_rows.1), channel_id=1, source_target_pairs={{0,1},{1,2},{2,3},{3,0},{4,5},{5,6},{6,7},{7,4},{8,9},{9,10},{10,1... | collective-permute-start | bytes 1572872 | tf_op jit(solution)/shard_map/ppermute | solution.py:409
  125.5 4.6 %last_rows.1 = bf16[4,2,256,128]{3,2,1,0:T(8,128)(2,1)S(1)} custom-call(s32[2]{0:T(128)S(1)} %copy-done, bf16[8,256,256]{2,1,0:T(8,128)(2,1)S(1)} %get-tuple-element.21.grads_ref, f32[8,8,256]{2,1,0:T(8,128)S(1)} %get-tuple-element.22.high_ref, f32[8,8,256]{2,1,0:T(8,128)S(1)} %get-tuple-element.23.low_ref), custom_call_target="tpu_custom_call" | custom-call | flops 1000 | bytes 1000 | tf_op jit(solution)/shard_map/last_rows/pallas_call | solution.py:332
  130.1 4.3 %collective-permute-start.5 = (bf16[4,2,256,128]{3,2,1,0:T(8,128)(2,1)S(1)}, bf16[4,2,256,128]{3,2,1,0:T(8,128)(2,1)S(1)}, u32[]{:S(2)}, u32[]{:S(2)}) collective-permute-start(bf16[4,2,256,128]{3,2,1,0:T(8,128)(2,1)S(1)} %last_rows.1), channel_id=1, source_target_pairs={{0,3},{1,0},{2,1},{3,2},{4,7},{5,4},{6,5},{7,6},{8,11},{9,8},{10,9... | collective-permute-start | bytes 1572872 | tf_op jit(solution)/shard_map/ppermute | solution.py:411
  134.4 4.6 %own_rows.1.own_ref = bf16[4,2,256,128]{3,2,1,0:T(8,128)(2,1)S(1)} custom-call(s32[2]{0:T(128)S(1)} %copy-done, bf16[8,256,256]{2,1,0:T(8,128)(2,1)S(1)} %get-tuple-element.21.grads_ref, f32[8,8,256]{2,1,0:T(8,128)S(1)} %get-tuple-element.22.high_ref, f32[8,8,256]{2,1,0:T(8,128)S(1)} %get-tuple-element.23.low_ref, ...), custom_call_target="tpu_custom_call" | custom-call | flops 1000 | bytes 1000 | tf_op jit(solution)/shard_map/own_rows/pallas_call | solution.py:332
  139.0 3.4 %collective-permute-done.4.a_ref = bf16[4,2,256,128]{3,2,1,0:T(8,128)(2,1)S(1)} collective-permute-done((bf16[4,2,256,128]{3,2,1,0:T(8,128)(2,1)S(1)}, bf16[4,2,256,128]{3,2,1,0:T(8,128)(2,1)S(1)}, u32[]{:S(2)}, u32[]{:S(2)}) %collective-permute-start.4) | collective-permute-done | bytes 524320 | tf_op jit(solution)/shard_map/ppermute | solution.py:409
  142.5 2.2 %collective-permute-done.5.b_ref = bf16[4,2,256,128]{3,2,1,0:T(8,128)(2,1)S(1)} collective-permute-done((bf16[4,2,256,128]{3,2,1,0:T(8,128)(2,1)S(1)}, bf16[4,2,256,128]{3,2,1,0:T(8,128)(2,1)S(1)}, u32[]{:S(2)}, u32[]{:S(2)}) %collective-permute-start.5) | collective-permute-done | bytes 524320 | tf_op jit(solution)/shard_map/ppermute | solution.py:411
  144.8 10.0 %collective-permute-start.6 = (bf16[2,256,128]{2,1,0:T(8,128)(2,1)S(1)}, bf16[2,256,128]{2,1,0:T(8,128)(2,1)S(1)}, u32[]{:S(2)}, u32[]{:S(2)}) collective-permute-start(bf16[2,256,128]{2,1,0:T(8,128)(2,1)S(1)} %get-tuple-element.26), channel_id=1, source_target_pairs={{0,8},{4,12},{8,0},{12,4},{1,9},{5,13},{9,1},{13,5},{2,10},{6,14},... | collective-permute-start | bytes 393224 | tf_op jit(solution)/shard_map/ppermute | solution.py:417
  154.8 4.1 %collective-permute-start.7 = (bf16[2,256,128]{2,1,0:T(8,128)(2,1)S(1)}, bf16[2,256,128]{2,1,0:T(8,128)(2,1)S(1)}, u32[]{:S(2)}, u32[]{:S(2)}) collective-permute-start(bf16[2,256,128]{2,1,0:T(8,128)(2,1)S(1)} %get-tuple-element.27), channel_id=1, source_target_pairs={{0,4},{4,8},{8,12},{12,0},{1,5},{5,9},{9,13},{13,1},{2,6},{6,10},{... | collective-permute-start | bytes 393224 | tf_op jit(solution)/shard_map/ppermute | solution.py:418
  158.9 5.1 %collective-permute-start.8 = (bf16[2,256,128]{2,1,0:T(8,128)(2,1)S(1)}, bf16[2,256,128]{2,1,0:T(8,128)(2,1)S(1)}, u32[]{:S(2)}, u32[]{:S(2)}) collective-permute-start(bf16[2,256,128]{2,1,0:T(8,128)(2,1)S(1)} %get-tuple-element.28), channel_id=1, source_target_pairs={{0,12},{4,0},{8,4},{12,8},{1,13},{5,1},{9,5},{13,9},{2,14},{6,2},{... | collective-permute-start | bytes 393224 | tf_op jit(solution)/shard_map/ppermute | solution.py:419
  164.0 4.1 %collective-permute-done.7.before_ref = bf16[2,256,128]{2,1,0:T(8,128)(2,1)S(1)} collective-permute-done((bf16[2,256,128]{2,1,0:T(8,128)(2,1)S(1)}, bf16[2,256,128]{2,1,0:T(8,128)(2,1)S(1)}, u32[]{:S(2)}, u32[]{:S(2)}) %collective-permute-start.7) | collective-permute-done | bytes 131104 | tf_op jit(solution)/shard_map/ppermute | solution.py:418
  168.1 13.3 %collective-permute-done.8.after_ref = bf16[2,256,128]{2,1,0:T(8,128)(2,1)S(1)} collective-permute-done((bf16[2,256,128]{2,1,0:T(8,128)(2,1)S(1)}, bf16[2,256,128]{2,1,0:T(8,128)(2,1)S(1)}, u32[]{:S(2)}, u32[]{:S(2)}) %collective-permute-start.8) | collective-permute-done | bytes 131104 | tf_op jit(solution)/shard_map/ppermute | solution.py:419
  181.4 0.8 final_sum.1
  (15 shorter events, 1.5 us)
Async XLA Ops:
  0.6 47.1 %copy-start.1 = (bf16[2,512,32]{1,2,0:T(8,128)(2,1)S(1)}, bf16[2,512,32]{1,2,0:T(8,128)(2,1)}, u32[]{:S(2)}) copy-start(bf16[2,512,32]{1,2,0:T(8,128)(2,1)} %param.13) | copy-start | bytes 196612
  18.5 30.0 %collective-permute-start = (bf16[560,128]{1,0:T(8,128)(2,1)}, bf16[560,128]{1,0:T(8,128)(2,1)S(1)}, u32[]{:S(2)}, u32[]{:S(2)}) collective-permute-start(bf16[560,128]{1,0:T(8,128)(2,1)} %get-tuple-element.18), channel_id=1, source_target_pairs={{0,4},{4,8},{8,12},{12,0},{1,5},{5,9},{9,13},{13,1},{2,6},{6,10},{... | collective-permute-start | bytes 430088 | tf_op jit(solution)/shard_map/ppermute | solution.py:400
  30.0 34.4 %collective-permute-start.1 = (bf16[560,128]{1,0:T(8,128)(2,1)}, bf16[560,128]{1,0:T(8,128)(2,1)S(1)}, u32[]{:S(2)}, u32[]{:S(2)}) collective-permute-start(bf16[560,128]{1,0:T(8,128)(2,1)} %get-tuple-element.19), channel_id=1, source_target_pairs={{0,8},{4,12},{8,0},{12,4},{1,9},{5,13},{9,1},{13,5},{2,10},{6,14},... | collective-permute-start | bytes 430088 | tf_op jit(solution)/shard_map/ppermute | solution.py:399
  44.3 25.0 %collective-permute-start.2 = (bf16[560,128]{1,0:T(8,128)(2,1)}, bf16[560,128]{1,0:T(8,128)(2,1)S(1)}, u32[]{:S(2)}, u32[]{:S(2)}) collective-permute-start(bf16[560,128]{1,0:T(8,128)(2,1)} %get-tuple-element.20), channel_id=1, source_target_pairs={{0,12},{4,0},{8,4},{12,8},{1,13},{5,1},{9,5},{13,9},{2,14},{6,2},{... | collective-permute-start | bytes 430088 | tf_op jit(solution)/shard_map/ppermute | solution.py:401
  48.5 20.8 %copy-start.2 = (bf16[560,128]{1,0:T(8,128)(2,1)}, bf16[560,128]{1,0:T(8,128)(2,1)S(1)}, u32[]{:S(2)}) copy-start(bf16[560,128]{1,0:T(8,128)(2,1)S(1)} %collective-permute-done.before_ref) | copy-start | bytes 430084
  64.4 4.9 %copy-start.3 = (bf16[560,128]{1,0:T(8,128)(2,1)}, bf16[560,128]{1,0:T(8,128)(2,1)S(1)}, u32[]{:S(2)}) copy-start(bf16[560,128]{1,0:T(8,128)(2,1)S(1)} %collective-permute-done.1.far_ref) | copy-start | bytes 430084
  69.3 0.7 copy-start.4
  77.3 31.3 %copy-start = (s32[2]{0:T(128)S(1)}, s32[2]{0:T(128)}, u32[]{:S(2)}) copy-start(s32[2]{0:T(128)} %pad_add_fusion.place_ref) | copy-start | bytes 28
  114.0 20.4 %collective-permute-start.3 = (bf16[4,2,256,128]{3,2,1,0:T(8,128)(2,1)S(1)}, bf16[4,2,256,128]{3,2,1,0:T(8,128)(2,1)S(1)}, u32[]{:S(2)}, u32[]{:S(2)}) collective-permute-start(bf16[4,2,256,128]{3,2,1,0:T(8,128)(2,1)S(1)} %get-tuple-element.24), channel_id=1, source_target_pairs={{0,2},{1,3},{2,0},{3,1},{4,6},{5,7},{6,4},{7,5},{8,10},{9,11},{10,... | collective-permute-start | bytes 1572872 | tf_op jit(solution)/shard_map/ppermute | solution.py:407
  123.3 19.2 %collective-permute-start.4 = (bf16[4,2,256,128]{3,2,1,0:T(8,128)(2,1)S(1)}, bf16[4,2,256,128]{3,2,1,0:T(8,128)(2,1)S(1)}, u32[]{:S(2)}, u32[]{:S(2)}) collective-permute-start(bf16[4,2,256,128]{3,2,1,0:T(8,128)(2,1)S(1)} %next_rows.1), channel_id=1, source_target_pairs={{0,1},{1,2},{2,3},{3,0},{4,5},{5,6},{6,7},{7,4},{8,9},{9,10},{10,1... | collective-permute-start | bytes 1572872 | tf_op jit(solution)/shard_map/ppermute | solution.py:409
  130.1 14.5 %collective-permute-start.5 = (bf16[4,2,256,128]{3,2,1,0:T(8,128)(2,1)S(1)}, bf16[4,2,256,128]{3,2,1,0:T(8,128)(2,1)S(1)}, u32[]{:S(2)}, u32[]{:S(2)}) collective-permute-start(bf16[4,2,256,128]{3,2,1,0:T(8,128)(2,1)S(1)} %last_rows.1), channel_id=1, source_target_pairs={{0,3},{1,0},{2,1},{3,2},{4,7},{5,4},{6,5},{7,6},{8,11},{9,8},{10,9... | collective-permute-start | bytes 1572872 | tf_op jit(solution)/shard_map/ppermute | solution.py:411
  144.8 19.2 %collective-permute-start.6 = (bf16[2,256,128]{2,1,0:T(8,128)(2,1)S(1)}, bf16[2,256,128]{2,1,0:T(8,128)(2,1)S(1)}, u32[]{:S(2)}, u32[]{:S(2)}) collective-permute-start(bf16[2,256,128]{2,1,0:T(8,128)(2,1)S(1)} %get-tuple-element.26), channel_id=1, source_target_pairs={{0,8},{4,12},{8,0},{12,4},{1,9},{5,13},{9,1},{13,5},{2,10},{6,14},... | collective-permute-start | bytes 393224 | tf_op jit(solution)/shard_map/ppermute | solution.py:417
  154.8 13.3 %collective-permute-start.7 = (bf16[2,256,128]{2,1,0:T(8,128)(2,1)S(1)}, bf16[2,256,128]{2,1,0:T(8,128)(2,1)S(1)}, u32[]{:S(2)}, u32[]{:S(2)}) collective-permute-start(bf16[2,256,128]{2,1,0:T(8,128)(2,1)S(1)} %get-tuple-element.27), channel_id=1, source_target_pairs={{0,4},{4,8},{8,12},{12,0},{1,5},{5,9},{9,13},{13,1},{2,6},{6,10},{... | collective-permute-start | bytes 393224 | tf_op jit(solution)/shard_map/ppermute | solution.py:418
  158.9 22.5 %collective-permute-start.8 = (bf16[2,256,128]{2,1,0:T(8,128)(2,1)S(1)}, bf16[2,256,128]{2,1,0:T(8,128)(2,1)S(1)}, u32[]{:S(2)}, u32[]{:S(2)}) collective-permute-start(bf16[2,256,128]{2,1,0:T(8,128)(2,1)S(1)} %get-tuple-element.28), channel_id=1, source_target_pairs={{0,12},{4,0},{8,4},{12,8},{1,13},{5,1},{9,5},{13,9},{2,14},{6,2},{... | collective-permute-start | bytes 393224 | tf_op jit(solution)/shard_map/ppermute | solution.py:419

commit v7 on v5

--- a/solution.py
+++ b/solution.py
@@ -31,6 +31,7 @@
 bf16 = jnp.bfloat16
 
 
+ANY_SPEC = pl.BlockSpec(memory_space=pl.ANY)
 VMEM_SPEC = pl.BlockSpec(memory_space=pltpu.VMEM)
 SMEM_SPEC = pl.BlockSpec(memory_space=pltpu.SMEM)
 
@@ -43,9 +44,21 @@
     return lax.broadcasted_iota(jnp.int32, shape, dim)
 
 
-def messages_kernel(
-    here_ref, pooled_ref, cotangent_ref, ids_ref, lengths_ref, slot_ref, home_ref, *out_refs
-):
+def messages_kernel(place_ref, pooled_any, cotangent_any, ids_any, lengths_any, slot_ref, home_ref, *refs):
+    out_refs, (x_ref, ids_ref, lengths_ref, sems, small_sems) = refs[:N_SLOT], refs[N_SLOT:]
+    small = [
+        pltpu.make_async_copy(ids_any, ids_ref, small_sems.at[0]),
+        pltpu.make_async_copy(lengths_any, lengths_ref, small_sems.at[1]),
+    ]
+    for copy in small:
+        copy.start()
+    fetches = []
+    for part, source in enumerate((pooled_any, cotangent_any)):
+        rows = pl.ds(part * POOLED_ROWS, POOLED_ROWS)
+        for r in range(N_SLOT):
+            dest = lax.rem(place_ref[0] + r, N_SLOT)
+            fetches.append(pltpu.make_async_copy(source.at[dest], x_ref.at[r, rows], sems.at[part, r]))
+            fetches[-1].start()
     slots = slot_ref[...]
     hot = jnp.where(iota((SLOT_DEV, SLOT_DEV), 0) == slots, 1.0, 0.0).astype(bf16)
     homes = jnp.broadcast_to(home_ref[...].astype(f32), (8, SLOT_DEV)).astype(bf16)
@@ -58,31 +71,45 @@
     table = across % TABLE_DEV * 16
     marks = jnp.broadcast_to(target, (16, SLOT_DEV)).astype(bf16)
     entry = iota((BAG, SLOT_DEV), 0)
-    for r, out_ref in enumerate(out_refs):
-        dest = lax.rem(here_ref[0] + r, N_SLOT)
-        out_ref[:POOLED_ROWS] = pooled_ref[dest]
-        out_ref[POOLED_ROWS : 2 * POOLED_ROWS] = cotangent_ref[dest]
+    for copy in small:
+        copy.wait()
+    for r in range(N_SLOT):
+        dest = lax.rem(place_ref[0] + r, N_SLOT)
         parts = []
         for b in range(PAIR):
             ids = ids_ref[dest * PAIR + b]
-            live = entry < lengths_ref[dest * PAIR + b]
+            live = entry < lengths_ref[pl.ds(dest * PAIR + b, 1), :]
             parts.append((jnp.where(live, ids // ROW_BLOCK, DEAD) + table).astype(f32))
             parts.append((ids % ROW_BLOCK).astype(f32))
-        out_ref[2 * POOLED_ROWS : 2 * POOLED_ROWS + ID_ROWS] = jnp.concatenate(parts, axis=0).astype(bf16)
-        out_ref[2 * POOLED_ROWS + ID_ROWS :] = marks
-
-
-def make_messages(here, *args):
+        x_ref[r, 2 * POOLED_ROWS : 2 * POOLED_ROWS + ID_ROWS] = jnp.concatenate(parts, axis=0).astype(bf16)
+        x_ref[r, 2 * POOLED_ROWS + ID_ROWS :] = marks
+    for copy in fetches:
+        copy.wait()
+    stores = [pltpu.make_async_copy(x_ref.at[r], out_refs[r], sems.at[2, r]) for r in range(N_SLOT)]
+    for copy in stores:
+        copy.start()
+    for copy in stores:
+        copy.wait()
+
+
+def make_messages(place, *args):
     message = jax.ShapeDtypeStruct((MSG_ROWS, D), bf16)
     return pl.pallas_call(
         messages_kernel,
         out_shape=(message,) * N_SLOT,
-        in_specs=[SMEM_SPEC] + [VMEM_SPEC] * len(args),
-        out_specs=(VMEM_SPEC,) * N_SLOT,
-        compiler_params=pltpu.CompilerParams(vmem_limit_bytes=16 << 20),
+        in_specs=[SMEM_SPEC] + [ANY_SPEC] * 4 + [VMEM_SPEC] * 2,
+        out_specs=(ANY_SPEC,) * N_SLOT,
+        scratch_shapes=[
+            pltpu.VMEM((N_SLOT, MSG_ROWS, D), bf16),
+            pltpu.VMEM((N_SLOT * PAIR, BAG, SLOT_DEV), jnp.int32),
+            pltpu.VMEM((N_SLOT * PAIR, SLOT_DEV), jnp.int32),
+            pltpu.SemaphoreType.DMA((3, N_SLOT)),
+            pltpu.SemaphoreType.DMA((2,)),
+        ],
+        compiler_params=pltpu.CompilerParams(vmem_limit_bytes=56 << 20),
         cost_estimate=pl.CostEstimate(flops=1_000_000, bytes_accessed=2 << 20, transcendentals=0),
         name="messages",
-    )(here, *args)
+    )(place, *args)
 
 
 def layers_kernel(
@@ -175,6 +202,25 @@
     out_ref[:, N_SLOT] = ids.astype(bf16).reshape(DP, 8, D)
 
 
+def fetch_kernel(source_any, out_ref, sem):
+    copy = pltpu.make_async_copy(source_any, out_ref, sem)
+    copy.start()
+    copy.wait()
+
+
+def fetch(source):
+    return pl.pallas_call(
+        fetch_kernel,
+        out_shape=jax.ShapeDtypeStruct(source.shape, source.dtype),
+        in_specs=[ANY_SPEC],
+        out_specs=VMEM_SPEC,
+        scratch_shapes=[pltpu.SemaphoreType.DMA],
+        compiler_params=pltpu.CompilerParams(vmem_limit_bytes=8 << 20),
+        cost_estimate=pl.CostEstimate(flops=0, bytes_accessed=2 << 20, transcendentals=0),
+        name="fetch_weights",
+    )(source)
+
+
 def run_layers(here, *args):
     return pl.pallas_call(
         layers_kernel,
@@ -221,29 +267,34 @@
 
 def add_rows(blocks_ref, out_ref, grads_ref, high_ref, low_ref):
     lanes = 2 * PAIR * DP
-    half = ROW_BLOCK // 2
-    rows_of = iota((half, lanes), 0).astype(f32).astype(bf16)
-    one = jnp.ones((), bf16)
+    rows_of = iota((ROW_BLOCK, lanes), 0).astype(f32).astype(bf16)
     zero = jnp.zeros((), bf16)
 
+    def spread(row):
+        row = jnp.broadcast_to(row, (16, lanes)).astype(bf16)
+        return jnp.broadcast_to(row[None], (ROW_BLOCK // 16, 16, lanes)).reshape(ROW_BLOCK, lanes)
+
     def block(index, carry):
-        want = blocks_ref[index].astype(f32)
-        for part in range(2):
-            total = jnp.zeros((half, 2 * D), f32)
-            for p in range(N_SLOT * CAPACITY // 2):
-                match = jnp.where(high_ref[p] == want, low_ref[p] - float(part * half), -1.0)
-                count = jnp.zeros((half, lanes), bf16)
-                for j in range(BAG):
-                    wanted = jnp.broadcast_to(match[j : j + 1], (16, lanes)).astype(bf16)
-                    wanted = jnp.broadcast_to(wanted[None], (half // 16, 16, lanes)).reshape(half, lanes)
-                    count = count + jnp.where(rows_of == wanted, one, zero)
-                total = total + dot(count, grads_ref[p])
-            rows = slice(part * half, (part + 1) * half)
-            out_ref[index // 2, index % 2, 0, rows] = total[:, :D].astype(bf16)
-            out_ref[index // 2, index % 2, 1, rows] = total[:, D:].astype(bf16)
+        first = blocks_ref[2 * index].astype(f32)
+        second = blocks_ref[2 * index + 1].astype(f32)
+        totals = [jnp.zeros((ROW_BLOCK, 2 * D), f32)] * 2
+        for p in range(N_SLOT * CAPACITY // 2):
+            high = high_ref[p]
+            low = low_ref[p]
+            weight = jnp.where(high == first, 1.0, jnp.where(high == second, 16.0, 0.0))
+            packed = jnp.zeros((ROW_BLOCK, lanes), bf16)
+            for j in range(BAG):
+                hit = rows_of == spread(low[j : j + 1])
+                packed = packed + jnp.where(hit, spread(weight[j : j + 1]), zero)
+            upper = ((packed - 7.5) + 3072.0) - 3072.0
+            totals = [totals[0] + dot(packed - upper, grads_ref[p]), totals[1] + dot(upper, grads_ref[p])]
+        for c, scale in ((0, 1.0), (1, 0.0625)):
+            total = totals[c] * scale
+            out_ref[index, c, 0] = total[:, :D].astype(bf16)
+            out_ref[index, c, 1] = total[:, D:].astype(bf16)
         return carry
 
-    lax.fori_loop(0, 4, block, 0)
+    lax.fori_loop(0, 2, block, 0)
 
 
 def first_bags_kernel(blocks_ref, got_ref, out_ref, grads_ref, high_ref, low_ref, wide_ref):
@@ -353,7 +404,7 @@
         pooled.reshape(N_SLOT, POOLED_ROWS, D),
         cotangent.reshape(N_SLOT, POOLED_ROWS, D),
         jnp.transpose(bag_ids, (0, 2, 1)),
-        bag_lengths.reshape(-1, 1, SLOT_DEV),
+        bag_lengths,
         slot_table.reshape(1, SLOT_DEV),
         table_home.reshape(1, -1),
     )
@@ -361,7 +412,7 @@
     from_before = lax.ppermute(to_after, "slot", up_moves)
     from_after = lax.ppermute(to_before, "slot", down_moves)
     sent = run_layers(
-        at_slot, own, from_before, from_far, from_after, compress_weight, fm_basis, fm_output, norm_gain
+        at_slot, own, from_before, from_far, from_after, fetch(compress_weight), fm_basis, fm_output, norm_gain
     )
     got = lax.all_to_all(sent, "dp", split_axis=0, concat_axis=0, tiled=True)
     me = lax.axis_index("grp").astype(jnp.int32)

time: 165 us -> 159 us (0.964)
  Pallas kernels: 25.7 us -> 21.3 us
  local copies, waits for them, and re-layouts: 4.75 us -> 2.15 us
    pallas_call x3, Pallas kernels: 13.8 us -> 8.63 us  [run_later_bags(): pl.pallas_call(later_bags_kernel, out_shape=jax.ShapeDtypeStruct((2, 2, *...]
    unnamed x21 -> x11, local copies, waits for them, and re-layouts: 4.75 us -> 2.15 us
    pallas_call x1, Pallas kernels: 0.3 us -> 2.67 us  [make_messages(): pl.pallas_call(messages_kernel, out_shape=(message,) * N_SLOT, in_specs=[...]
    ppermute x1, waiting for transfers between devices: 0.01 us -> 2.16 us  [per_device(): a_got = lax.ppermute(a_sent, 'grp', side_moves)]
    ppermute x2, waiting for transfers between devices: 16.3 us -> 14.5 us  [per_device(): from_far = lax.ppermute(to_far, 'slot', far_moves)]
    pallas_call x1, Pallas kernels: 5.32 us -> 3.58 us  [run_first_bags(): pl.pallas_call(first_bags_kernel, out_shape=(jax.ShapeDtypeStruct((2, 2,...]
  transfers between devices with their start and end apart: 11 -> 11, of which waited for: 6 -> 7; matrix products, arithmetic and copies ran while one was open for 0% -> 0% of each run, Pallas kernels for 9% -> 6%
where the time goes in v7:
time: 159 us
  starting transfers between devices  71.6 us (45%)
  waiting for transfers between devices  62.9 us (40%)
  Pallas kernels  21.3 us (13%)
  local copies, waits for them, and re-layouts  2.15 us (1%)
    ppermute x2, starting transfers between devices, per_device(): from_far = lax.ppermute(to_far, 'slot', far_moves)  24.2 us
    all_to_all x1, waiting for transfers between devices, per_device(): got = lax.all_to_all(sent, 'dp', split_axis=0, concat_axis=0, tiled=True)  20.9 us
    ppermute x2, waiting for transfers between devices, per_device(): from_after = lax.ppermute(to_before, 'slot', down_moves)  18.4 us
    ppermute x2, starting transfers between devices, per_device(): from_before = lax.ppermute(to_after, 'slot', up_moves)  15.6 us
    ppermute x2, waiting for transfers between devices, per_device(): from_far = lax.ppermute(to_far, 'slot', far_moves)  14.5 us
    all_to_all x1, starting transfers between devices, per_device(): got = lax.all_to_all(sent, 'dp', split_axis=0, concat_axis=0, tiled=True)  10.3 us
    pallas_call x3, Pallas kernels, run_later_bags(): pl.pallas_call(later_bags_kernel, out_shape=jax.ShapeDtypeStruct((2, 2, *...  8.63 us
    ppermute x2, starting transfers between devices, per_device(): from_after = lax.ppermute(to_before, 'slot', down_moves)  8.46 us
  transfers between devices with their start and end apart: 11, of which 7 were waited for; matrix products, arithmetic and copies ran while one was open for 0% of the time, Pallas kernels for 6%

profile of v7, /device:TPU:1, one launch (start us, length us, event | category | flops | bytes accessed | tf_op | source)
XLA Modules:
  0.0 158.6 jit_solution(6737012270814146897)
XLA Ops:
  0.0 2.7 %messages.1 = (bf16[560,128]{1,0:T(8,128)(2,1)}, bf16[560,128]{1,0:T(8,128)(2,1)}, bf16[560,128]{1,0:T(8,128)(2,1)}, bf16[560,128]{1,0:T(8,128)(2,1)}) custom-call(s32[1]{0:T(128)} %bitcast.12.place_ref.here_ref, bf16[4,256,128]{2,1,0:T(8,128)(2,1)} %bitcast.22, bf16[4,256,128]{2,1,0:T(8,128)(2,1)} %bitcast.23, s32[8,8,128]{2,1,0:T(8,128)} %bitcast.24, ...), custom_call_target="tpu_custom_call" | custom-call | flops 1000000 | bytes 2097152 | tf_op jit(solution)/shard_map/messages/pallas_call | solution.py:97
  2.7 11.5 %collective-permute-start = (bf16[560,128]{1,0:T(8,128)(2,1)}, bf16[560,128]{1,0:T(8,128)(2,1)S(1)}, u32[]{:S(2)}, u32[]{:S(2)}) collective-permute-start(bf16[560,128]{1,0:T(8,128)(2,1)} %get-tuple-element.24), channel_id=1, source_target_pairs={{0,4},{4,8},{8,12},{12,0},{1,5},{5,9},{9,13},{13,1},{2,6},{6,10},{... | collective-permute-start | bytes 430088 | tf_op jit(solution)/shard_map/ppermute | solution.py:412
  14.2 14.3 %collective-permute-start.1 = (bf16[560,128]{1,0:T(8,128)(2,1)}, bf16[560,128]{1,0:T(8,128)(2,1)S(1)}, u32[]{:S(2)}, u32[]{:S(2)}) collective-permute-start(bf16[560,128]{1,0:T(8,128)(2,1)} %get-tuple-element.25), channel_id=1, source_target_pairs={{0,8},{4,12},{8,0},{12,4},{1,9},{5,13},{9,1},{13,5},{2,10},{6,14},... | collective-permute-start | bytes 430088 | tf_op jit(solution)/shard_map/ppermute | solution.py:411
  28.4 3.4 %collective-permute-start.2 = (bf16[560,128]{1,0:T(8,128)(2,1)}, bf16[560,128]{1,0:T(8,128)(2,1)S(1)}, u32[]{:S(2)}, u32[]{:S(2)}) collective-permute-start(bf16[560,128]{1,0:T(8,128)(2,1)} %get-tuple-element.26), channel_id=1, source_target_pairs={{0,12},{4,0},{8,4},{12,8},{1,13},{5,1},{9,5},{13,9},{2,14},{6,2},{... | collective-permute-start | bytes 430088 | tf_op jit(solution)/shard_map/ppermute | solution.py:413
  34.1 14.5 %collective-permute-done.1.far_ref = bf16[560,128]{1,0:T(8,128)(2,1)S(1)} collective-permute-done((bf16[560,128]{1,0:T(8,128)(2,1)}, bf16[560,128]{1,0:T(8,128)(2,1)S(1)}, u32[]{:S(2)}, u32[]{:S(2)}) %collective-permute-start.1) | collective-permute-done | bytes 143392 | tf_op jit(solution)/shard_map/ppermute | solution.py:411
  48.5 4.9 %collective-permute-done.2.after_ref = bf16[560,128]{1,0:T(8,128)(2,1)S(1)} collective-permute-done((bf16[560,128]{1,0:T(8,128)(2,1)}, bf16[560,128]{1,0:T(8,128)(2,1)S(1)}, u32[]{:S(2)}, u32[]{:S(2)}) %collective-permute-start.2) | collective-permute-done | bytes 143392 | tf_op jit(solution)/shard_map/ppermute | solution.py:413
  53.5 5.2 %layers.1 = bf16[64,5,8,128]{3,2,1,0:T(8,128)(2,1)} custom-call(s32[1]{0:T(128)} %bitcast.12.place_ref.here_ref, bf16[560,128]{1,0:T(8,128)(2,1)S(1)} %copy-done.1, bf16[560,128]{1,0:T(8,128)(2,1)S(1)} %collective-permute-done.before_ref, bf16[560,128]{1,0:T(8,128)(2,1)S(1)} %collective-permute-done.1.far_ref, ...), custom_call_target="tpu_custom_call" | custom-call | flops 2000000000 | bytes 4194304 | tf_op jit(solution)/shard_map/layers/pallas_call | solution.py:225
  58.6 10.3 %all-to-all-start = ((bf16[64,5,8,128]{3,2,1,0:T(8,128)(2,1)}), bf16[64,5,8,128]{3,2,1,0:T(8,128)(2,1)S(1)}, u32[]{:S(2)}, u32[]{:S(2)}) async-start(bf16[64,5,8,128]{3,2,1,0:T(8,128)(2,1)} %layers.1), calls=%async_computation | async-start | bytes 1310720 | tf_op jit(solution)/shard_map/all_to_all | solution.py:417
  69.0 20.9 %all-to-all-done.got_ref = bf16[64,5,8,128]{3,2,1,0:T(8,128)(2,1)S(1)} async-done(((bf16[64,5,8,128]{3,2,1,0:T(8,128)(2,1)}), bf16[64,5,8,128]{3,2,1,0:T(8,128)(2,1)S(1)}, u32[]{:S(2)}, u32[]{:S(2)}) %all-to-all-start) | async-done | bytes 655392 | tf_op jit(solution)/shard_map/all_to_all | solution.py:417
  90.0 3.6 %first_bags.1 = (bf16[2,2,2,256,128]{4,3,2,1,0:T(8,128)(2,1)S(1)}, bf16[8,256,256]{2,1,0:T(8,128)(2,1)S(1)}, f32[8,8,256]{2,1,0:T(8,128)S(1)}, f32[8,8,256]{2,1,0:T(8,128)S(1)}) custom-call(s32[4]{0:T(128)S(1)} %pad_add_fusion.2.blocks_ref, bf16[64,5,8,128]{3,2,1,0:T(8,128)(2,1)S(1)} %all-to-all-done.got_ref), custom_call_target="tpu_custom_call" | custom-call | flops 200000000 | bytes 1048576 | tf_op jit(solution)/shard_map/first_bags/pallas_call | solution.py:317
  93.5 3.1 %collective-permute-start.3 = (bf16[2,2,2,256,128]{4,3,2,1,0:T(8,128)(2,1)S(1)}, bf16[2,2,2,256,128]{4,3,2,1,0:T(8,128)(2,1)S(1)}, u32[]{:S(2)}, u32[]{:S(2)}) collective-permute-start(bf16[2,2,2,256,128]{4,3,2,1,0:T(8,128)(2,1)S(1)} %get-tuple-element.30), channel_id=1, source_target_pairs={{0,1},{1,0},{2,3},{3,2},{4,5},{5,4},{6,7},{7,6},{8,9},{9,8},{10,11... | collective-permute-start | bytes 1572872 | tf_op jit(solution)/shard_map/ppermute | solution.py:431
  96.8 2.9 %b_sent.1 = bf16[2,2,2,256,128]{4,3,2,1,0:T(8,128)(2,1)S(1)} custom-call(s32[4]{0:T(128)S(1)} %pad_add_fusion.3.blocks_ref, bf16[8,256,256]{2,1,0:T(8,128)(2,1)S(1)} %get-tuple-element.27.grads_ref, f32[8,8,256]{2,1,0:T(8,128)S(1)} %get-tuple-element.28.high_ref, f32[8,8,256]{2,1,0:T(8,128)S(1)} %get-tuple-element.29.low_ref), custom_call_target="tpu_custom_call" | custom-call | flops 200000000 | bytes 1048576 | tf_op jit(solution)/shard_map/b_sent/pallas_call | solution.py:335
  99.6 3.7 %collective-permute-start.4 = (bf16[2,2,2,256,128]{4,3,2,1,0:T(8,128)(2,1)S(1)}, bf16[2,2,2,256,128]{4,3,2,1,0:T(8,128)(2,1)S(1)}, u32[]{:S(2)}, u32[]{:S(2)}) collective-permute-start(bf16[2,2,2,256,128]{4,3,2,1,0:T(8,128)(2,1)S(1)} %b_sent.1), channel_id=1, source_target_pairs={{0,3},{1,2},{2,1},{3,0},{4,7},{5,6},{6,5},{7,4},{8,11},{9,10},{10,... | collective-permute-start | bytes 1572872 | tf_op jit(solution)/shard_map/ppermute | solution.py:433
  103.5 2.9 %a_kept.1.kept_ref = bf16[2,2,2,256,128]{4,3,2,1,0:T(8,128)(2,1)S(1)} custom-call(s32[4]{0:T(128)S(1)} %pad_add_fusion.1.blocks_ref, bf16[8,256,256]{2,1,0:T(8,128)(2,1)S(1)} %get-tuple-element.27.grads_ref, f32[8,8,256]{2,1,0:T(8,128)S(1)} %get-tuple-element.28.high_ref, f32[8,8,256]{2,1,0:T(8,128)S(1)} %get-tuple-element.29.low_ref), custom_call_target="tpu_custom_call" | custom-call | flops 200000000 | bytes 1048576 | tf_op jit(solution)/shard_map/a_kept/pallas_call | solution.py:335
  106.4 2.2 %collective-permute-done.3.got_ref = bf16[2,2,2,256,128]{4,3,2,1,0:T(8,128)(2,1)S(1)} collective-permute-done((bf16[2,2,2,256,128]{4,3,2,1,0:T(8,128)(2,1)S(1)}, bf16[2,2,2,256,128]{4,3,2,1,0:T(8,128)(2,1)S(1)}, u32[]{:S(2)}, u32[]{:S(2)}) %collective-permute-start.3) | collective-permute-done | bytes 524320 | tf_op jit(solution)/shard_map/ppermute | solution.py:431
  108.7 4.4 %collective-permute-start.6 = (bf16[2,2,256,128]{3,2,1,0:T(8,128)(2,1)S(1)}, bf16[2,2,256,128]{3,2,1,0:T(8,128)(2,1)S(1)}, u32[]{:S(2)}, u32[]{:S(2)}) collective-permute-start(bf16[2,2,256,128]{3,2,1,0:T(8,128)(2,1)S(1)} %get-tuple-element.37), channel_id=1, source_target_pairs={{0,3},{1,2},{2,1},{3,0},{4,7},{5,6},{6,5},{7,4},{8,11},{9,10},{10,... | collective-permute-start | bytes 786440 | tf_op jit(solution)/shard_map/ppermute | solution.py:437
  113.1 2.9 %b_kept.1.kept_ref = bf16[2,2,2,256,128]{4,3,2,1,0:T(8,128)(2,1)S(1)} custom-call(s32[4]{0:T(128)S(1)} %pad_add_fusion.blocks_ref, bf16[8,256,256]{2,1,0:T(8,128)(2,1)S(1)} %get-tuple-element.27.grads_ref, f32[8,8,256]{2,1,0:T(8,128)S(1)} %get-tuple-element.28.high_ref, f32[8,8,256]{2,1,0:T(8,128)S(1)} %get-tuple-element.29.low_ref), custom_call_target="tpu_custom_call" | custom-call | flops 200000000 | bytes 1048576 | tf_op jit(solution)/shard_map/b_kept/pallas_call | solution.py:335
  116.1 1.9 %collective-permute-start.5 = (bf16[2,2,256,128]{3,2,1,0:T(8,128)(2,1)S(1)}, bf16[2,2,256,128]{3,2,1,0:T(8,128)(2,1)S(1)}, u32[]{:S(2)}, u32[]{:S(2)}) collective-permute-start(bf16[2,2,256,128]{3,2,1,0:T(8,128)(2,1)S(1)} %get-tuple-element.34), channel_id=1, source_target_pairs={{0,1},{1,0},{2,3},{3,2},{4,5},{5,4},{6,7},{7,6},{8,9},{9,8},{10,11... | collective-permute-start | bytes 786440 | tf_op jit(solution)/shard_map/ppermute | solution.py:441
  118.0 3.1 %collective-permute-done.6.got_ref = bf16[2,2,256,128]{3,2,1,0:T(8,128)(2,1)S(1)} collective-permute-done((bf16[2,2,256,128]{3,2,1,0:T(8,128)(2,1)S(1)}, bf16[2,2,256,128]{3,2,1,0:T(8,128)(2,1)S(1)}, u32[]{:S(2)}, u32[]{:S(2)}) %collective-permute-start.6) | collective-permute-done | bytes 262176 | tf_op jit(solution)/shard_map/ppermute | solution.py:437
  121.2 10.0 %collective-permute-start.7 = (bf16[2,256,128]{2,1,0:T(8,128)(2,1)S(1)}, bf16[2,256,128]{2,1,0:T(8,128)(2,1)S(1)}, u32[]{:S(2)}, u32[]{:S(2)}) collective-permute-start(bf16[2,256,128]{2,1,0:T(8,128)(2,1)S(1)} %get-tuple-element.38), channel_id=1, source_target_pairs={{0,8},{4,12},{8,0},{12,4},{1,9},{5,13},{9,1},{13,5},{2,10},{6,14},... | collective-permute-start | bytes 393224 | tf_op jit(solution)/shard_map/ppermute | solution.py:444
  131.2 4.1 %collective-permute-start.8 = (bf16[2,256,128]{2,1,0:T(8,128)(2,1)S(1)}, bf16[2,256,128]{2,1,0:T(8,128)(2,1)S(1)}, u32[]{:S(2)}, u32[]{:S(2)}) collective-permute-start(bf16[2,256,128]{2,1,0:T(8,128)(2,1)S(1)} %get-tuple-element.39), channel_id=1, source_target_pairs={{0,4},{4,8},{8,12},{12,0},{1,5},{5,9},{9,13},{13,1},{2,6},{6,10},{... | collective-permute-start | bytes 393224 | tf_op jit(solution)/shard_map/ppermute | solution.py:445
  135.4 5.1 %collective-permute-start.9 = (bf16[2,256,128]{2,1,0:T(8,128)(2,1)S(1)}, bf16[2,256,128]{2,1,0:T(8,128)(2,1)S(1)}, u32[]{:S(2)}, u32[]{:S(2)}) collective-permute-start(bf16[2,256,128]{2,1,0:T(8,128)(2,1)S(1)} %get-tuple-element.40), channel_id=1, source_target_pairs={{0,12},{4,0},{8,4},{12,8},{1,13},{5,1},{9,5},{13,9},{2,14},{6,2},{... | collective-permute-start | bytes 393224 | tf_op jit(solution)/shard_map/ppermute | solution.py:447
  140.5 3.8 %collective-permute-done.8.before_ref = bf16[2,256,128]{2,1,0:T(8,128)(2,1)S(1)} collective-permute-done((bf16[2,256,128]{2,1,0:T(8,128)(2,1)S(1)}, bf16[2,256,128]{2,1,0:T(8,128)(2,1)S(1)}, u32[]{:S(2)}, u32[]{:S(2)}) %collective-permute-start.8) | collective-permute-done | bytes 131104 | tf_op jit(solution)/shard_map/ppermute | solution.py:445
  144.3 13.5 %collective-permute-done.9.after_ref = bf16[2,256,128]{2,1,0:T(8,128)(2,1)S(1)} collective-permute-done((bf16[2,256,128]{2,1,0:T(8,128)(2,1)S(1)}, bf16[2,256,128]{2,1,0:T(8,128)(2,1)S(1)}, u32[]{:S(2)}, u32[]{:S(2)}) %collective-permute-start.9) | collective-permute-done | bytes 131104 | tf_op jit(solution)/shard_map/ppermute | solution.py:447
  (25 shorter events, 3.7 us)
Async XLA Ops:
  2.7 31.4 %collective-permute-start = (bf16[560,128]{1,0:T(8,128)(2,1)}, bf16[560,128]{1,0:T(8,128)(2,1)S(1)}, u32[]{:S(2)}, u32[]{:S(2)}) collective-permute-start(bf16[560,128]{1,0:T(8,128)(2,1)} %get-tuple-element.24), channel_id=1, source_target_pairs={{0,4},{4,8},{8,12},{12,0},{1,5},{5,9},{9,13},{13,1},{2,6},{6,10},{... | collective-permute-start | bytes 430088 | tf_op jit(solution)/shard_map/ppermute | solution.py:412
  14.2 34.4 %collective-permute-start.1 = (bf16[560,128]{1,0:T(8,128)(2,1)}, bf16[560,128]{1,0:T(8,128)(2,1)S(1)}, u32[]{:S(2)}, u32[]{:S(2)}) collective-permute-start(bf16[560,128]{1,0:T(8,128)(2,1)} %get-tuple-element.25), channel_id=1, source_target_pairs={{0,8},{4,12},{8,0},{12,4},{1,9},{5,13},{9,1},{13,5},{2,10},{6,14},... | collective-permute-start | bytes 430088 | tf_op jit(solution)/shard_map/ppermute | solution.py:411
  28.4 25.0 %collective-permute-start.2 = (bf16[560,128]{1,0:T(8,128)(2,1)}, bf16[560,128]{1,0:T(8,128)(2,1)S(1)}, u32[]{:S(2)}, u32[]{:S(2)}) collective-permute-start(bf16[560,128]{1,0:T(8,128)(2,1)} %get-tuple-element.26), channel_id=1, source_target_pairs={{0,12},{4,0},{8,4},{12,8},{1,13},{5,1},{9,5},{13,9},{2,14},{6,2},{... | collective-permute-start | bytes 430088 | tf_op jit(solution)/shard_map/ppermute | solution.py:413
  31.8 1.2 copy-start
  33.0 0.8 copy-start.4
  33.9 19.6 %copy-start.1 = (bf16[560,128]{1,0:T(8,128)(2,1)S(1)}, bf16[560,128]{1,0:T(8,128)(2,1)}, u32[]{:S(2)}) copy-start(bf16[560,128]{1,0:T(8,128)(2,1)} %get-tuple-element.23.own_ref) | copy-start | bytes 430084
  33.9 19.6 %copy-start.2 = (bf16[2,32,128]{2,1,0:T(8,128)(2,1)S(1)}, bf16[2,32,128]{2,1,0:T(8,128)(2,1)}, u32[]{:S(2)}) copy-start(bf16[2,32,128]{2,1,0:T(8,128)(2,1)} %output_ref.1) | copy-start | bytes 49156
  34.0 19.4 %copy-start.3 = (f32[2,128]{1,0:T(2,128)S(1)}, f32[2,128]{1,0:T(2,128)}, u32[]{:S(2)}) copy-start(f32[2,128]{1,0:T(2,128)} %gain_ref.1) | copy-start | bytes 3076
  58.6 31.3 %all-to-all-start = ((bf16[64,5,8,128]{3,2,1,0:T(8,128)(2,1)}), bf16[64,5,8,128]{3,2,1,0:T(8,128)(2,1)S(1)}, u32[]{:S(2)}, u32[]{:S(2)}) async-start(bf16[64,5,8,128]{3,2,1,0:T(8,128)(2,1)} %layers.1), calls=%async_computation | async-start | bytes 1310720 | tf_op jit(solution)/shard_map/all_to_all | solution.py:417
  93.5 15.0 %collective-permute-start.3 = (bf16[2,2,2,256,128]{4,3,2,1,0:T(8,128)(2,1)S(1)}, bf16[2,2,2,256,128]{4,3,2,1,0:T(8,128)(2,1)S(1)}, u32[]{:S(2)}, u32[]{:S(2)}) collective-permute-start(bf16[2,2,2,256,128]{4,3,2,1,0:T(8,128)(2,1)S(1)} %get-tuple-element.30), channel_id=1, source_target_pairs={{0,1},{1,0},{2,3},{3,2},{4,5},{5,4},{6,7},{7,6},{8,9},{9,8},{10,11... | collective-permute-start | bytes 1572872 | tf_op jit(solution)/shard_map/ppermute | solution.py:431
  99.6 16.3 %collective-permute-start.4 = (bf16[2,2,2,256,128]{4,3,2,1,0:T(8,128)(2,1)S(1)}, bf16[2,2,2,256,128]{4,3,2,1,0:T(8,128)(2,1)S(1)}, u32[]{:S(2)}, u32[]{:S(2)}) collective-permute-start(bf16[2,2,2,256,128]{4,3,2,1,0:T(8,128)(2,1)S(1)} %b_sent.1), channel_id=1, source_target_pairs={{0,3},{1,2},{2,1},{3,0},{4,7},{5,6},{6,5},{7,4},{8,11},{9,10},{10,... | collective-permute-start | bytes 1572872 | tf_op jit(solution)/shard_map/ppermute | solution.py:433
  108.7 12.5 %collective-permute-start.6 = (bf16[2,2,256,128]{3,2,1,0:T(8,128)(2,1)S(1)}, bf16[2,2,256,128]{3,2,1,0:T(8,128)(2,1)S(1)}, u32[]{:S(2)}, u32[]{:S(2)}) collective-permute-start(bf16[2,2,256,128]{3,2,1,0:T(8,128)(2,1)S(1)} %get-tuple-element.37), channel_id=1, source_target_pairs={{0,3},{1,2},{2,1},{3,0},{4,7},{5,6},{6,5},{7,4},{8,11},{9,10},{10,... | collective-permute-start | bytes 786440 | tf_op jit(solution)/shard_map/ppermute | solution.py:437
  116.1 19.2 %collective-permute-start.5 = (bf16[2,2,256,128]{3,2,1,0:T(8,128)(2,1)S(1)}, bf16[2,2,256,128]{3,2,1,0:T(8,128)(2,1)S(1)}, u32[]{:S(2)}, u32[]{:S(2)}) collective-permute-start(bf16[2,2,256,128]{3,2,1,0:T(8,128)(2,1)S(1)} %get-tuple-element.34), channel_id=1, source_target_pairs={{0,1},{1,0},{2,3},{3,2},{4,5},{5,4},{6,7},{7,6},{8,9},{9,8},{10,11... | collective-permute-start | bytes 786440 | tf_op jit(solution)/shard_map/ppermute | solution.py:441
  121.2 19.2 %collective-permute-start.7 = (bf16[2,256,128]{2,1,0:T(8,128)(2,1)S(1)}, bf16[2,256,128]{2,1,0:T(8,128)(2,1)S(1)}, u32[]{:S(2)}, u32[]{:S(2)}) collective-permute-start(bf16[2,256,128]{2,1,0:T(8,128)(2,1)S(1)} %get-tuple-element.38), channel_id=1, source_target_pairs={{0,8},{4,12},{8,0},{12,4},{1,9},{5,13},{9,1},{13,5},{2,10},{6,14},... | collective-permute-start | bytes 393224 | tf_op jit(solution)/shard_map/ppermute | solution.py:444
  131.2 13.1 %collective-permute-start.8 = (bf16[2,256,128]{2,1,0:T(8,128)(2,1)S(1)}, bf16[2,256,128]{2,1,0:T(8,128)(2,1)S(1)}, u32[]{:S(2)}, u32[]{:S(2)}) collective-permute-start(bf16[2,256,128]{2,1,0:T(8,128)(2,1)S(1)} %get-tuple-element.39), channel_id=1, source_target_pairs={{0,4},{4,8},{8,12},{12,0},{1,5},{5,9},{9,13},{13,1},{2,6},{6,10},{... | collective-permute-start | bytes 393224 | tf_op jit(solution)/shard_map/ppermute | solution.py:445
  135.4 22.4 %collective-permute-start.9 = (bf16[2,256,128]{2,1,0:T(8,128)(2,1)S(1)}, bf16[2,256,128]{2,1,0:T(8,128)(2,1)S(1)}, u32[]{:S(2)}, u32[]{:S(2)}) collective-permute-start(bf16[2,256,128]{2,1,0:T(8,128)(2,1)S(1)} %get-tuple-element.40), channel_id=1, source_target_pairs={{0,12},{4,0},{8,4},{12,8},{1,13},{5,1},{9,5},{13,9},{2,14},{6,2},{... | collective-permute-start | bytes 393224 | tf_op jit(solution)/shard_map/ppermute | solution.py:447

commit v8 on v7

--- a/solution.py
+++ b/solution.py
@@ -56,7 +56,7 @@
     for part, source in enumerate((pooled_any, cotangent_any)):
         rows = pl.ds(part * POOLED_ROWS, POOLED_ROWS)
         for r in range(N_SLOT):
-            dest = lax.rem(place_ref[0] + r, N_SLOT)
+            dest = place_ref[0] ^ r
             fetches.append(pltpu.make_async_copy(source.at[dest], x_ref.at[r, rows], sems.at[part, r]))
             fetches[-1].start()
     slots = slot_ref[...]
@@ -74,7 +74,7 @@
     for copy in small:
         copy.wait()
     for r in range(N_SLOT):
-        dest = lax.rem(place_ref[0] + r, N_SLOT)
+        dest = place_ref[0] ^ r
         parts = []
         for b in range(PAIR):
             ids = ids_ref[dest * PAIR + b]
@@ -113,10 +113,10 @@
 
 
 def layers_kernel(
-    here_ref, own_ref, before_ref, far_ref, after_ref, compress_ref, basis_ref, output_ref, gain_ref, out_ref, x_ref
+    here_ref, own_ref, near_ref, mirror_ref, far_ref, compress_ref, basis_ref, output_ref, gain_ref, out_ref, x_ref
 ):
-    for r, ref in enumerate((own_ref, after_ref, far_ref, before_ref)):
-        x_ref[lax.rem(here_ref[0] + r, N_SLOT)] = ref[...]
+    for r, ref in enumerate((own_ref, near_ref, far_ref, mirror_ref)):
+        x_ref[here_ref[0] ^ r] = ref[...]
     gain = gain_ref[...]
     pair_rows = POOLED_ROWS
     current = []
@@ -355,18 +355,18 @@
     sent_ref[...] = wide_sum(kept_ref.at[1], got_ref.at[1]).astype(bf16)
 
 
-def sum_a_kernel(own_ref, got_ref, far_ref, after_ref):
-    far_ref[...] = wide_sum(own_ref.at[0], got_ref.at[0]).astype(bf16)
-    after_ref[...] = wide_sum(own_ref.at[1], got_ref.at[1]).astype(bf16)
-
-
-def sum_b_kernel(own_ref, got_ref, kept_ref, before_ref):
+def sum_a_kernel(own_ref, got_ref, near_ref, mirror_ref):
+    near_ref[...] = wide_sum(own_ref.at[0], got_ref.at[0]).astype(bf16)
+    mirror_ref[...] = wide_sum(own_ref.at[1], got_ref.at[1]).astype(bf16)
+
+
+def sum_b_kernel(own_ref, got_ref, kept_ref, far_ref):
     kept_ref[...] = wide_sum(own_ref.at[0], got_ref.at[0])
-    before_ref[...] = wide_sum(own_ref.at[1], got_ref.at[1]).astype(bf16)
-
-
-def final_kernel(kept_ref, far_ref, before_ref, after_ref, out_ref):
-    out_ref[...] = wide_sum(kept_ref, far_ref, before_ref, after_ref)
+    far_ref[...] = wide_sum(own_ref.at[1], got_ref.at[1]).astype(bf16)
+
+
+def final_kernel(kept_ref, near_ref, mirror_ref, far_ref, out_ref):
+    out_ref[...] = wide_sum(kept_ref, near_ref, mirror_ref, far_ref)
 
 
 def small_call(kernel, name, shapes, *args):
@@ -396,10 +396,8 @@
 ):
     here = lax.axis_index("slot").astype(jnp.int32)
     at_slot = here.reshape(1)
-    up_moves, far_moves, down_moves = (
-        [(i, (i + step) % N_SLOT) for i in range(N_SLOT)] for step in (1, 2, 3)
-    )
-    own, to_after, to_far, to_before = make_messages(
+    swaps = [[(i, i ^ r) for i in range(N_SLOT)] for r in range(N_SLOT)]
+    own, near, far, mirror = make_messages(
         at_slot,
         pooled.reshape(N_SLOT, POOLED_ROWS, D),
         cotangent.reshape(N_SLOT, POOLED_ROWS, D),
@@ -408,30 +406,29 @@
         slot_table.reshape(1, SLOT_DEV),
         table_home.reshape(1, -1),
     )
-    from_far = lax.ppermute(to_far, "slot", far_moves)
-    from_before = lax.ppermute(to_after, "slot", up_moves)
-    from_after = lax.ppermute(to_before, "slot", down_moves)
+    near = lax.ppermute(near, "slot", swaps[1])
+    mirror = lax.ppermute(mirror, "slot", swaps[3])
+    far = lax.ppermute(far, "slot", swaps[2])
     sent = run_layers(
-        at_slot, own, from_before, from_far, from_after, fetch(compress_weight), fm_basis, fm_output, norm_gain
+        at_slot, own, near, mirror, far, fetch(compress_weight), fm_basis, fm_output, norm_gain
     )
     got = lax.all_to_all(sent, "dp", split_axis=0, concat_axis=0, tiled=True)
     me = lax.axis_index("grp").astype(jnp.int32)
     side = me ^ 1
-    mirror = N_GRP - 1 - me
+    opposite = N_GRP - 1 - me
     across = side ^ 3
-    far, after, before = (here + 2) % N_SLOT, (here + 1) % N_SLOT, (here + 3) % N_SLOT
 
     def blocks(groups, chunks):
         return jnp.stack([chunk * N_GRP + group for group in groups for chunk in chunks])
 
-    half_a, half_b = (far, after), (here, before)
+    half_a, half_b = (here ^ 1, here ^ 3), (here, here ^ 2)
     side_moves = [(i, i ^ 1) for i in range(N_GRP)]
     mirror_moves = [(i, N_GRP - 1 - i) for i in range(N_GRP)]
     a_sent, *prepared = run_first_bags(blocks((side, across), half_a), got)
     a_got = lax.ppermute(a_sent, "grp", side_moves)
-    b_sent = run_later_bags(blocks((mirror, across), half_b), prepared, "b_sent")
+    b_sent = run_later_bags(blocks((opposite, across), half_b), prepared, "b_sent")
     b_got = lax.ppermute(b_sent, "grp", mirror_moves)
-    a_kept = run_later_bags(blocks((me, mirror), half_a), prepared, "a_kept")
+    a_kept = run_later_bags(blocks((me, opposite), half_a), prepared, "a_kept")
     part = ((2, *CHUNK), bf16)
     a_own, a_next = small_call(add_parts_kernel, "add_a", (part, part), a_kept, a_got)
     a_last = lax.ppermute(a_next, "grp", mirror_moves)
@@ -440,12 +437,12 @@
     b_own, b_next = small_call(add_parts_kernel, "add_b", (part, part), b_kept, b_got)
     b_last = lax.ppermute(b_next, "grp", side_moves)
     chunk = (CHUNK, bf16)
-    to_far, to_after = small_call(sum_a_kernel, "sum_a", (chunk, chunk), a_own, a_last)
-    from_far = lax.ppermute(to_far, "slot", far_moves)
-    from_before = lax.ppermute(to_after, "slot", up_moves)
-    kept, to_before = small_call(sum_b_kernel, "sum_b", ((CHUNK, f32), chunk), b_own, b_last)
-    from_after = lax.ppermute(to_before, "slot", down_moves)
-    return small_call(final_kernel, "final_sum", ((CHUNK, f32),), kept, from_far, from_before, from_after)[0]
+    near, mirror = small_call(sum_a_kernel, "sum_a", (chunk, chunk), a_own, a_last)
+    near = lax.ppermute(near, "slot", swaps[1])
+    mirror = lax.ppermute(mirror, "slot", swaps[3])
+    kept, far = small_call(sum_b_kernel, "sum_b", ((CHUNK, f32), chunk), b_own, b_last)
+    far = lax.ppermute(far, "slot", swaps[2])
+    return small_call(final_kernel, "final_sum", ((CHUNK, f32),), kept, near, mirror, far)[0]
 
 
 def solution(mesh):

time: 159 us -> 160 us (level)
  starting transfers between devices: 71.6 us -> 80.7 us
  waiting for transfers between devices: 62.9 us -> 54.5 us
    all_to_all x1, starting transfers between devices: 10.3 us -> 19.8 us  [per_device(): got = lax.all_to_all(sent, 'dp', split_axis=0, concat_axis=0, tiled=True)]
    ppermute x6, waiting for transfers between devices: 36.7 us -> 28.2 us  [the longest x2 25.9 us: per_device(): far = lax.ppermute(far, 'slot', swaps[2])]
  transfers between devices with their start and end apart: 11 -> 11, of which waited for: 7 -> 6; matrix products, arithmetic and copies ran while one was open for 0% -> 0% of each run, Pallas kernels for 6% -> 6%
where the time goes in v8:
time: 160 us; the launch traced here: 159 us
  starting transfers between devices  80.7 us (50%)
  waiting for transfers between devices  54.5 us (34%)
  Pallas kernels  21.2 us (13%)
  local copies, waits for them, and re-layouts  2.15 us (1%)
    ppermute x2, waiting for transfers between devices, per_device(): far = lax.ppermute(far, 'slot', swaps[2])  25.9 us
    ppermute x2, starting transfers between devices, per_device(): near = lax.ppermute(near, 'slot', swaps[1])  22.1 us
    all_to_all x1, waiting for transfers between devices, per_device(): got = lax.all_to_all(sent, 'dp', split_axis=0, concat_axis=0, tiled=True)  20.9 us
    all_to_all x1, starting transfers between devices, per_device(): got = lax.all_to_all(sent, 'dp', split_axis=0, concat_axis=0, tiled=True)  19.8 us
    ppermute x2, starting transfers between devices, per_device(): mirror = lax.ppermute(mirror, 'slot', swaps[3])  14.4 us
    ppermute x2, starting transfers between devices, per_device(): far = lax.ppermute(far, 'slot', swaps[2])  11.2 us
    pallas_call x3, Pallas kernels, run_later_bags(): pl.pallas_call(later_bags_kernel, out_shape=jax.ShapeDtypeStruct((2, 2, *...  8.63 us
    pallas_call x1, Pallas kernels, run_layers(): pl.pallas_call(layers_kernel, out_shape=jax.ShapeDtypeStruct((DP, N_SLOT...  5.14 us
  transfers between devices with their start and end apart: 11, of which 6 were waited for; matrix products, arithmetic and copies ran while one was open for 0% of the time, Pallas kernels for 6%

profile of v8, /device:TPU:1, one launch (start us, length us, event | category | flops | bytes accessed | tf_op | source)
XLA Modules:
  0.0 159.1 jit_solution(1384798944317194706)
XLA Ops:
  0.0 2.7 %messages.1 = (bf16[560,128]{1,0:T(8,128)(2,1)}, bf16[560,128]{1,0:T(8,128)(2,1)}, bf16[560,128]{1,0:T(8,128)(2,1)}, bf16[560,128]{1,0:T(8,128)(2,1)}) custom-call(s32[1]{0:T(128)} %bitcast.12.place_ref.here_ref, bf16[4,256,128]{2,1,0:T(8,128)(2,1)} %bitcast.22, bf16[4,256,128]{2,1,0:T(8,128)(2,1)} %bitcast.23, s32[8,8,128]{2,1,0:T(8,128)} %bitcast.24, ...), custom_call_target="tpu_custom_call" | custom-call | flops 1000000 | bytes 2097152 | tf_op jit(solution)/shard_map/messages/pallas_call | solution.py:97
  2.7 11.5 %collective-permute-start = (bf16[560,128]{1,0:T(8,128)(2,1)}, bf16[560,128]{1,0:T(8,128)(2,1)S(1)}, u32[]{:S(2)}, u32[]{:S(2)}) collective-permute-start(bf16[560,128]{1,0:T(8,128)(2,1)} %get-tuple-element.24), channel_id=1, source_target_pairs={{0,4},{4,0},{8,12},{12,8},{1,5},{5,1},{9,13},{13,9},{2,6},{6,2},{1... | collective-permute-start | bytes 430088 | tf_op jit(solution)/shard_map/ppermute | solution.py:409
  14.1 10.6 %collective-permute-start.1 = (bf16[560,128]{1,0:T(8,128)(2,1)}, bf16[560,128]{1,0:T(8,128)(2,1)S(1)}, u32[]{:S(2)}, u32[]{:S(2)}) collective-permute-start(bf16[560,128]{1,0:T(8,128)(2,1)} %get-tuple-element.25), channel_id=1, source_target_pairs={{0,12},{4,8},{8,4},{12,0},{1,13},{5,9},{9,5},{13,1},{2,14},{6,10},... | collective-permute-start | bytes 430088 | tf_op jit(solution)/shard_map/ppermute | solution.py:410
  24.8 5.6 %collective-permute-start.2 = (bf16[560,128]{1,0:T(8,128)(2,1)}, bf16[560,128]{1,0:T(8,128)(2,1)S(1)}, u32[]{:S(2)}, u32[]{:S(2)}) collective-permute-start(bf16[560,128]{1,0:T(8,128)(2,1)} %get-tuple-element.26), channel_id=1, source_target_pairs={{0,8},{4,12},{8,0},{12,4},{1,9},{5,13},{9,1},{13,5},{2,10},{6,14},... | collective-permute-start | bytes 430088 | tf_op jit(solution)/shard_map/ppermute | solution.py:411
  30.4 1.2 copy-done
  32.6 7.8 %collective-permute-done.2.far_ref = bf16[560,128]{1,0:T(8,128)(2,1)S(1)} collective-permute-done((bf16[560,128]{1,0:T(8,128)(2,1)}, bf16[560,128]{1,0:T(8,128)(2,1)S(1)}, u32[]{:S(2)}, u32[]{:S(2)}) %collective-permute-start.2) | collective-permute-done | bytes 143392 | tf_op jit(solution)/shard_map/ppermute | solution.py:411
  40.5 5.1 %layers.1 = bf16[64,5,8,128]{3,2,1,0:T(8,128)(2,1)} custom-call(s32[1]{0:T(128)} %bitcast.12.place_ref.here_ref, bf16[560,128]{1,0:T(8,128)(2,1)S(1)} %copy-done.1, bf16[560,128]{1,0:T(8,128)(2,1)S(1)} %collective-permute-done.near_ref, bf16[560,128]{1,0:T(8,128)(2,1)S(1)} %collective-permute-done.1.mirror_ref, ...), custom_call_target="tpu_custom_call" | custom-call | flops 2000000000 | bytes 4194304 | tf_op jit(solution)/shard_map/layers/pallas_call | solution.py:225
  45.6 19.8 %all-to-all-start = ((bf16[64,5,8,128]{3,2,1,0:T(8,128)(2,1)}), bf16[64,5,8,128]{3,2,1,0:T(8,128)(2,1)S(1)}, u32[]{:S(2)}, u32[]{:S(2)}) async-start(bf16[64,5,8,128]{3,2,1,0:T(8,128)(2,1)} %layers.1), calls=%async_computation | async-start | bytes 1310720 | tf_op jit(solution)/shard_map/all_to_all | solution.py:415
  65.6 20.9 %all-to-all-done.got_ref = bf16[64,5,8,128]{3,2,1,0:T(8,128)(2,1)S(1)} async-done(((bf16[64,5,8,128]{3,2,1,0:T(8,128)(2,1)}), bf16[64,5,8,128]{3,2,1,0:T(8,128)(2,1)S(1)}, u32[]{:S(2)}, u32[]{:S(2)}) %all-to-all-start) | async-done | bytes 655392 | tf_op jit(solution)/shard_map/all_to_all | solution.py:415
  86.5 3.6 %first_bags.1 = (bf16[2,2,2,256,128]{4,3,2,1,0:T(8,128)(2,1)S(1)}, bf16[8,256,256]{2,1,0:T(8,128)(2,1)S(1)}, f32[8,8,256]{2,1,0:T(8,128)S(1)}, f32[8,8,256]{2,1,0:T(8,128)S(1)}) custom-call(s32[4]{0:T(128)S(1)} %pad_add_fusion.2.blocks_ref, bf16[64,5,8,128]{3,2,1,0:T(8,128)(2,1)S(1)} %all-to-all-done.got_ref), custom_call_target="tpu_custom_call" | custom-call | flops 200000000 | bytes 1048576 | tf_op jit(solution)/shard_map/first_bags/pallas_call | solution.py:317
  90.1 3.1 %collective-permute-start.3 = (bf16[2,2,2,256,128]{4,3,2,1,0:T(8,128)(2,1)S(1)}, bf16[2,2,2,256,128]{4,3,2,1,0:T(8,128)(2,1)S(1)}, u32[]{:S(2)}, u32[]{:S(2)}) collective-permute-start(bf16[2,2,2,256,128]{4,3,2,1,0:T(8,128)(2,1)S(1)} %get-tuple-element.30), channel_id=1, source_target_pairs={{0,1},{1,0},{2,3},{3,2},{4,5},{5,4},{6,7},{7,6},{8,9},{9,8},{10,11... | collective-permute-start | bytes 1572872 | tf_op jit(solution)/shard_map/ppermute | solution.py:428
  93.3 2.9 %b_sent.1 = bf16[2,2,2,256,128]{4,3,2,1,0:T(8,128)(2,1)S(1)} custom-call(s32[4]{0:T(128)S(1)} %pad_add_fusion.3.blocks_ref, bf16[8,256,256]{2,1,0:T(8,128)(2,1)S(1)} %get-tuple-element.27.grads_ref, f32[8,8,256]{2,1,0:T(8,128)S(1)} %get-tuple-element.28.high_ref, f32[8,8,256]{2,1,0:T(8,128)S(1)} %get-tuple-element.29.low_ref), custom_call_target="tpu_custom_call" | custom-call | flops 200000000 | bytes 1048576 | tf_op jit(solution)/shard_map/b_sent/pallas_call | solution.py:335
  96.2 3.7 %collective-permute-start.4 = (bf16[2,2,2,256,128]{4,3,2,1,0:T(8,128)(2,1)S(1)}, bf16[2,2,2,256,128]{4,3,2,1,0:T(8,128)(2,1)S(1)}, u32[]{:S(2)}, u32[]{:S(2)}) collective-permute-start(bf16[2,2,2,256,128]{4,3,2,1,0:T(8,128)(2,1)S(1)} %b_sent.1), channel_id=1, source_target_pairs={{0,3},{1,2},{2,1},{3,0},{4,7},{5,6},{6,5},{7,4},{8,11},{9,10},{10,... | collective-permute-start | bytes 1572872 | tf_op jit(solution)/shard_map/ppermute | solution.py:430
  100.1 2.9 %a_kept.1.kept_ref = bf16[2,2,2,256,128]{4,3,2,1,0:T(8,128)(2,1)S(1)} custom-call(s32[4]{0:T(128)S(1)} %pad_add_fusion.1.blocks_ref, bf16[8,256,256]{2,1,0:T(8,128)(2,1)S(1)} %get-tuple-element.27.grads_ref, f32[8,8,256]{2,1,0:T(8,128)S(1)} %get-tuple-element.28.high_ref, f32[8,8,256]{2,1,0:T(8,128)S(1)} %get-tuple-element.29.low_ref), custom_call_target="tpu_custom_call" | custom-call | flops 200000000 | bytes 1048576 | tf_op jit(solution)/shard_map/a_kept/pallas_call | solution.py:335
  103.0 2.1 %collective-permute-done.3.got_ref = bf16[2,2,2,256,128]{4,3,2,1,0:T(8,128)(2,1)S(1)} collective-permute-done((bf16[2,2,2,256,128]{4,3,2,1,0:T(8,128)(2,1)S(1)}, bf16[2,2,2,256,128]{4,3,2,1,0:T(8,128)(2,1)S(1)}, u32[]{:S(2)}, u32[]{:S(2)}) %collective-permute-start.3) | collective-permute-done | bytes 524320 | tf_op jit(solution)/shard_map/ppermute | solution.py:428
  105.2 4.4 %collective-permute-start.6 = (bf16[2,2,256,128]{3,2,1,0:T(8,128)(2,1)S(1)}, bf16[2,2,256,128]{3,2,1,0:T(8,128)(2,1)S(1)}, u32[]{:S(2)}, u32[]{:S(2)}) collective-permute-start(bf16[2,2,256,128]{3,2,1,0:T(8,128)(2,1)S(1)} %get-tuple-element.37), channel_id=1, source_target_pairs={{0,3},{1,2},{2,1},{3,0},{4,7},{5,6},{6,5},{7,4},{8,11},{9,10},{10,... | collective-permute-start | bytes 786440 | tf_op jit(solution)/shard_map/ppermute | solution.py:434
  109.6 2.9 %b_kept.1.kept_ref = bf16[2,2,2,256,128]{4,3,2,1,0:T(8,128)(2,1)S(1)} custom-call(s32[4]{0:T(128)S(1)} %pad_add_fusion.blocks_ref, bf16[8,256,256]{2,1,0:T(8,128)(2,1)S(1)} %get-tuple-element.27.grads_ref, f32[8,8,256]{2,1,0:T(8,128)S(1)} %get-tuple-element.28.high_ref, f32[8,8,256]{2,1,0:T(8,128)S(1)} %get-tuple-element.29.low_ref), custom_call_target="tpu_custom_call" | custom-call | flops 200000000 | bytes 1048576 | tf_op jit(solution)/shard_map/b_kept/pallas_call | solution.py:335
  112.7 1.9 %collective-permute-start.5 = (bf16[2,2,256,128]{3,2,1,0:T(8,128)(2,1)S(1)}, bf16[2,2,256,128]{3,2,1,0:T(8,128)(2,1)S(1)}, u32[]{:S(2)}, u32[]{:S(2)}) collective-permute-start(bf16[2,2,256,128]{3,2,1,0:T(8,128)(2,1)S(1)} %get-tuple-element.34), channel_id=1, source_target_pairs={{0,1},{1,0},{2,3},{3,2},{4,5},{5,4},{6,7},{7,6},{8,9},{9,8},{10,11... | collective-permute-start | bytes 786440 | tf_op jit(solution)/shard_map/ppermute | solution.py:438
  114.6 3.1 %collective-permute-done.6.got_ref = bf16[2,2,256,128]{3,2,1,0:T(8,128)(2,1)S(1)} collective-permute-done((bf16[2,2,256,128]{3,2,1,0:T(8,128)(2,1)S(1)}, bf16[2,2,256,128]{3,2,1,0:T(8,128)(2,1)S(1)}, u32[]{:S(2)}, u32[]{:S(2)}) %collective-permute-start.6) | collective-permute-done | bytes 262176 | tf_op jit(solution)/shard_map/ppermute | solution.py:434
  117.8 10.6 %collective-permute-start.7 = (bf16[2,256,128]{2,1,0:T(8,128)(2,1)S(1)}, bf16[2,256,128]{2,1,0:T(8,128)(2,1)S(1)}, u32[]{:S(2)}, u32[]{:S(2)}) collective-permute-start(bf16[2,256,128]{2,1,0:T(8,128)(2,1)S(1)} %get-tuple-element.38), channel_id=1, source_target_pairs={{0,4},{4,0},{8,12},{12,8},{1,5},{5,1},{9,13},{13,9},{2,6},{6,2},{1... | collective-permute-start | bytes 393224 | tf_op jit(solution)/shard_map/ppermute | solution.py:441
  128.4 3.8 %collective-permute-start.8 = (bf16[2,256,128]{2,1,0:T(8,128)(2,1)S(1)}, bf16[2,256,128]{2,1,0:T(8,128)(2,1)S(1)}, u32[]{:S(2)}, u32[]{:S(2)}) collective-permute-start(bf16[2,256,128]{2,1,0:T(8,128)(2,1)S(1)} %get-tuple-element.39), channel_id=1, source_target_pairs={{0,12},{4,8},{8,4},{12,0},{1,13},{5,9},{9,5},{13,1},{2,14},{6,10},... | collective-permute-start | bytes 393224 | tf_op jit(solution)/shard_map/ppermute | solution.py:442
  132.3 5.6 %collective-permute-start.9 = (bf16[2,256,128]{2,1,0:T(8,128)(2,1)S(1)}, bf16[2,256,128]{2,1,0:T(8,128)(2,1)S(1)}, u32[]{:S(2)}, u32[]{:S(2)}) collective-permute-start(bf16[2,256,128]{2,1,0:T(8,128)(2,1)S(1)} %get-tuple-element.40), channel_id=1, source_target_pairs={{0,8},{4,12},{8,0},{12,4},{1,9},{5,13},{9,1},{13,5},{2,10},{6,14},... | collective-permute-start | bytes 393224 | tf_op jit(solution)/shard_map/ppermute | solution.py:444
  137.9 2.4 %collective-permute-done.7.near_ref = bf16[2,256,128]{2,1,0:T(8,128)(2,1)S(1)} collective-permute-done((bf16[2,256,128]{2,1,0:T(8,128)(2,1)S(1)}, bf16[2,256,128]{2,1,0:T(8,128)(2,1)S(1)}, u32[]{:S(2)}, u32[]{:S(2)}) %collective-permute-start.7) | collective-permute-done | bytes 131104 | tf_op jit(solution)/shard_map/ppermute | solution.py:441
  140.3 18.0 %collective-permute-done.9.far_ref = bf16[2,256,128]{2,1,0:T(8,128)(2,1)S(1)} collective-permute-done((bf16[2,256,128]{2,1,0:T(8,128)(2,1)S(1)}, bf16[2,256,128]{2,1,0:T(8,128)(2,1)S(1)}, u32[]{:S(2)}, u32[]{:S(2)}) %collective-permute-start.9) | collective-permute-done | bytes 131104 | tf_op jit(solution)/shard_map/ppermute | solution.py:444
  (25 shorter events, 2.5 us)
Async XLA Ops:
  2.7 29.9 %collective-permute-start = (bf16[560,128]{1,0:T(8,128)(2,1)}, bf16[560,128]{1,0:T(8,128)(2,1)S(1)}, u32[]{:S(2)}, u32[]{:S(2)}) collective-permute-start(bf16[560,128]{1,0:T(8,128)(2,1)} %get-tuple-element.24), channel_id=1, source_target_pairs={{0,4},{4,0},{8,12},{12,8},{1,5},{5,1},{9,13},{13,9},{2,6},{6,2},{1... | collective-permute-start | bytes 430088 | tf_op jit(solution)/shard_map/ppermute | solution.py:409
  14.1 18.5 %collective-permute-start.1 = (bf16[560,128]{1,0:T(8,128)(2,1)}, bf16[560,128]{1,0:T(8,128)(2,1)S(1)}, u32[]{:S(2)}, u32[]{:S(2)}) collective-permute-start(bf16[560,128]{1,0:T(8,128)(2,1)} %get-tuple-element.25), channel_id=1, source_target_pairs={{0,12},{4,8},{8,4},{12,0},{1,13},{5,9},{9,5},{13,1},{2,14},{6,10},... | collective-permute-start | bytes 430088 | tf_op jit(solution)/shard_map/ppermute | solution.py:410
  24.8 15.7 %collective-permute-start.2 = (bf16[560,128]{1,0:T(8,128)(2,1)}, bf16[560,128]{1,0:T(8,128)(2,1)S(1)}, u32[]{:S(2)}, u32[]{:S(2)}) collective-permute-start(bf16[560,128]{1,0:T(8,128)(2,1)} %get-tuple-element.26), channel_id=1, source_target_pairs={{0,8},{4,12},{8,0},{12,4},{1,9},{5,13},{9,1},{13,5},{2,10},{6,14},... | collective-permute-start | bytes 430088 | tf_op jit(solution)/shard_map/ppermute | solution.py:411
  30.4 1.2 copy-start
  31.6 0.8 copy-start.4
  32.4 8.0 %copy-start.1 = (bf16[560,128]{1,0:T(8,128)(2,1)S(1)}, bf16[560,128]{1,0:T(8,128)(2,1)}, u32[]{:S(2)}) copy-start(bf16[560,128]{1,0:T(8,128)(2,1)} %get-tuple-element.23.own_ref) | copy-start | bytes 430084
  32.4 8.0 %copy-start.2 = (bf16[2,32,128]{2,1,0:T(8,128)(2,1)S(1)}, bf16[2,32,128]{2,1,0:T(8,128)(2,1)}, u32[]{:S(2)}) copy-start(bf16[2,32,128]{2,1,0:T(8,128)(2,1)} %output_ref.1) | copy-start | bytes 49156
  32.6 7.9 %copy-start.3 = (f32[2,128]{1,0:T(2,128)S(1)}, f32[2,128]{1,0:T(2,128)}, u32[]{:S(2)}) copy-start(f32[2,128]{1,0:T(2,128)} %gain_ref.1) | copy-start | bytes 3076
  45.6 40.9 %all-to-all-start = ((bf16[64,5,8,128]{3,2,1,0:T(8,128)(2,1)}), bf16[64,5,8,128]{3,2,1,0:T(8,128)(2,1)S(1)}, u32[]{:S(2)}, u32[]{:S(2)}) async-start(bf16[64,5,8,128]{3,2,1,0:T(8,128)(2,1)} %layers.1), calls=%async_computation | async-start | bytes 1310720 | tf_op jit(solution)/shard_map/all_to_all | solution.py:415
  90.1 15.0 %collective-permute-start.3 = (bf16[2,2,2,256,128]{4,3,2,1,0:T(8,128)(2,1)S(1)}, bf16[2,2,2,256,128]{4,3,2,1,0:T(8,128)(2,1)S(1)}, u32[]{:S(2)}, u32[]{:S(2)}) collective-permute-start(bf16[2,2,2,256,128]{4,3,2,1,0:T(8,128)(2,1)S(1)} %get-tuple-element.30), channel_id=1, source_target_pairs={{0,1},{1,0},{2,3},{3,2},{4,5},{5,4},{6,7},{7,6},{8,9},{9,8},{10,11... | collective-permute-start | bytes 1572872 | tf_op jit(solution)/shard_map/ppermute | solution.py:428
  96.2 16.3 %collective-permute-start.4 = (bf16[2,2,2,256,128]{4,3,2,1,0:T(8,128)(2,1)S(1)}, bf16[2,2,2,256,128]{4,3,2,1,0:T(8,128)(2,1)S(1)}, u32[]{:S(2)}, u32[]{:S(2)}) collective-permute-start(bf16[2,2,2,256,128]{4,3,2,1,0:T(8,128)(2,1)S(1)} %b_sent.1), channel_id=1, source_target_pairs={{0,3},{1,2},{2,1},{3,0},{4,7},{5,6},{6,5},{7,4},{8,11},{9,10},{10,... | collective-permute-start | bytes 1572872 | tf_op jit(solution)/shard_map/ppermute | solution.py:430
  105.2 12.5 %collective-permute-start.6 = (bf16[2,2,256,128]{3,2,1,0:T(8,128)(2,1)S(1)}, bf16[2,2,256,128]{3,2,1,0:T(8,128)(2,1)S(1)}, u32[]{:S(2)}, u32[]{:S(2)}) collective-permute-start(bf16[2,2,256,128]{3,2,1,0:T(8,128)(2,1)S(1)} %get-tuple-element.37), channel_id=1, source_target_pairs={{0,3},{1,2},{2,1},{3,0},{4,7},{5,6},{6,5},{7,4},{8,11},{9,10},{10,... | collective-permute-start | bytes 786440 | tf_op jit(solution)/shard_map/ppermute | solution.py:434
  112.7 19.5 %collective-permute-start.5 = (bf16[2,2,256,128]{3,2,1,0:T(8,128)(2,1)S(1)}, bf16[2,2,256,128]{3,2,1,0:T(8,128)(2,1)S(1)}, u32[]{:S(2)}, u32[]{:S(2)}) collective-permute-start(bf16[2,2,256,128]{3,2,1,0:T(8,128)(2,1)S(1)} %get-tuple-element.34), channel_id=1, source_target_pairs={{0,1},{1,0},{2,3},{3,2},{4,5},{5,4},{6,7},{7,6},{8,9},{9,8},{10,11... | collective-permute-start | bytes 786440 | tf_op jit(solution)/shard_map/ppermute | solution.py:438
  117.8 22.5 %collective-permute-start.7 = (bf16[2,256,128]{2,1,0:T(8,128)(2,1)S(1)}, bf16[2,256,128]{2,1,0:T(8,128)(2,1)S(1)}, u32[]{:S(2)}, u32[]{:S(2)}) collective-permute-start(bf16[2,256,128]{2,1,0:T(8,128)(2,1)S(1)} %get-tuple-element.38), channel_id=1, source_target_pairs={{0,4},{4,0},{8,12},{12,8},{1,5},{5,1},{9,13},{13,9},{2,6},{6,2},{1... | collective-permute-start | bytes 393224 | tf_op jit(solution)/shard_map/ppermute | solution.py:441
  128.4 11.8 %collective-permute-start.8 = (bf16[2,256,128]{2,1,0:T(8,128)(2,1)S(1)}, bf16[2,256,128]{2,1,0:T(8,128)(2,1)S(1)}, u32[]{:S(2)}, u32[]{:S(2)}) collective-permute-start(bf16[2,256,128]{2,1,0:T(8,128)(2,1)S(1)} %get-tuple-element.39), channel_id=1, source_target_pairs={{0,12},{4,8},{8,4},{12,0},{1,13},{5,9},{9,5},{13,1},{2,14},{6,10},... | collective-permute-start | bytes 393224 | tf_op jit(solution)/shard_map/ppermute | solution.py:442
  132.3 26.0 %collective-permute-start.9 = (bf16[2,256,128]{2,1,0:T(8,128)(2,1)S(1)}, bf16[2,256,128]{2,1,0:T(8,128)(2,1)S(1)}, u32[]{:S(2)}, u32[]{:S(2)}) collective-permute-start(bf16[2,256,128]{2,1,0:T(8,128)(2,1)S(1)} %get-tuple-element.40), channel_id=1, source_target_pairs={{0,8},{4,12},{8,0},{12,4},{1,9},{5,13},{9,1},{13,5},{2,10},{6,14},... | collective-permute-start | bytes 393224 | tf_op jit(solution)/shard_map/ppermute | solution.py:444

commit v9 on v8

--- a/solution.py
+++ b/solution.py
@@ -83,11 +83,12 @@
             parts.append((ids % ROW_BLOCK).astype(f32))
         x_ref[r, 2 * POOLED_ROWS : 2 * POOLED_ROWS + ID_ROWS] = jnp.concatenate(parts, axis=0).astype(bf16)
         x_ref[r, 2 * POOLED_ROWS + ID_ROWS :] = marks
-    for copy in fetches:
-        copy.wait()
-    stores = [pltpu.make_async_copy(x_ref.at[r], out_refs[r], sems.at[2, r]) for r in range(N_SLOT)]
-    for copy in stores:
-        copy.start()
+    stores = []
+    for r in (1, 3, 2, 0):
+        fetches[r].wait()
+        fetches[N_SLOT + r].wait()
+        stores.append(pltpu.make_async_copy(x_ref.at[r], out_refs[r], sems.at[2, r]))
+        stores[-1].start()
     for copy in stores:
         copy.wait()
 
@@ -113,7 +114,7 @@
 
 
 def layers_kernel(
-    here_ref, own_ref, near_ref, mirror_ref, far_ref, compress_ref, basis_ref, output_ref, gain_ref, out_ref, x_ref
+    here_ref, own_ref, near_ref, mirror_ref, far_ref, compress_ref, turned_ref, basis_ref, output_ref, gain_ref, out_ref, x_ref
 ):
     for r, ref in enumerate((own_ref, near_ref, far_ref, mirror_ref)):
         x_ref[here_ref[0] ^ r] = ref[...]
@@ -164,7 +165,7 @@
             local.append(grad_sum + dot(grad_feat, coeff))
             lows.append(low)
             grad_feats.append(grad_feat)
-        linear = dot(compress_ref[layer], jnp.concatenate(lows, axis=1), 0, 0)
+        linear = dot(turned_ref[layer], jnp.concatenate(lows, axis=1))
         basis_twice = jnp.concatenate([basis_ref[layer], basis_ref[layer]], axis=1)
         for b in range(PAIR):
             grad_coeff = dot(grad_feats[b], saved[layer][b][0], 0, 0)
@@ -188,36 +189,35 @@
         out_ref[:, k] = dot(placing, values).astype(bf16).reshape(DP, PAIR * CAPACITY, D)
     shape = (DP * 8, SLOTS)
     row = iota(shape, 0)
-    row_key = row // 8 * CAPACITY + row % 8 * 1024
-    column_key = jnp.concatenate([targets[k] + k * 1024 for k in range(N_SLOT)], axis=1)
+    row_key = row // 8 + row % 8 * 1024
+    targets = jnp.concatenate(targets, axis=1)
+    column_key = targets // CAPACITY + iota((1, SLOTS), 1) // SLOT_DEV * 1024
     unpacked = jnp.concatenate(
         [x_ref[k, 2 * pair_rows : 2 * pair_rows + ID_ROWS, :] for k in range(N_SLOT)], axis=1
     )
-    unpacked = jnp.concatenate([unpacked] * CAPACITY, axis=0)
-    rank_lane = iota((1, D), 1) // 32
-    ids = jnp.zeros((DP * 8, D), f32)
-    for rank in range(CAPACITY):
-        placing = jnp.where(row_key + rank == column_key, 1.0, 0.0).astype(bf16)
-        ids = ids + jnp.where(rank_lane == rank, dot(placing, unpacked, 1, 1), 0.0)
+    unpacked = jnp.concatenate([unpacked.astype(f32)] * CAPACITY, axis=0)
+    picked = iota((D, SLOTS), 0) // ID_ROWS == targets % CAPACITY
+    unpacked = jnp.where(picked, unpacked, 0.0).astype(bf16)
+    ids = dot(jnp.where(row_key == column_key, 1.0, 0.0).astype(bf16), unpacked, 1, 1)
     out_ref[:, N_SLOT] = ids.astype(bf16).reshape(DP, 8, D)
 
 
-def fetch_kernel(source_any, out_ref, sem):
-    copy = pltpu.make_async_copy(source_any, out_ref, sem)
-    copy.start()
-    copy.wait()
-
-
-def fetch(source):
-    return pl.pallas_call(
-        fetch_kernel,
-        out_shape=jax.ShapeDtypeStruct(source.shape, source.dtype),
-        in_specs=[ANY_SPEC],
-        out_specs=VMEM_SPEC,
-        scratch_shapes=[pltpu.SemaphoreType.DMA],
-        compiler_params=pltpu.CompilerParams(vmem_limit_bytes=8 << 20),
-        cost_estimate=pl.CostEstimate(flops=0, bytes_accessed=2 << 20, transcendentals=0),
-        name="fetch_weights",
+def weights_kernel(source_ref, out_ref, turned_ref):
+    for layer in range(LAYERS):
+        out_ref[layer] = source_ref[layer]
+        turned_ref[layer] = source_ref[layer].T
+
+
+def prepare_weights(source):
+    shape = jax.ShapeDtypeStruct(source.shape, source.dtype)
+    return pl.pallas_call(
+        weights_kernel,
+        out_shape=(shape, shape),
+        in_specs=[VMEM_SPEC],
+        out_specs=(VMEM_SPEC, VMEM_SPEC),
+        compiler_params=pltpu.CompilerParams(vmem_limit_bytes=12 << 20),
+        cost_estimate=pl.CostEstimate(flops=0, bytes_accessed=3 << 20, transcendentals=0),
+        name="prepare_weights",
     )(source)
 
 
@@ -410,7 +410,7 @@
     mirror = lax.ppermute(mirror, "slot", swaps[3])
     far = lax.ppermute(far, "slot", swaps[2])
     sent = run_layers(
-        at_slot, own, near, mirror, far, fetch(compress_weight), fm_basis, fm_output, norm_gain
+        at_slot, own, near, mirror, far, *prepare_weights(compress_weight), fm_basis, fm_output, norm_gain
     )
     got = lax.all_to_all(sent, "dp", split_axis=0, concat_axis=0, tiled=True)
     me = lax.axis_index("grp").astype(jnp.int32)
@@ -438,6 +438,7 @@
     b_last = lax.ppermute(b_next, "grp", side_moves)
     chunk = (CHUNK, bf16)
     near, mirror = small_call(sum_a_kernel, "sum_a", (chunk, chunk), a_own, a_last)
+    b_own, near, mirror = lax.optimization_barrier((b_own, near, mirror))
     near = lax.ppermute(near, "slot", swaps[1])
     mirror = lax.ppermute(mirror, "slot", swaps[3])
     kept, far = small_call(sum_b_kernel, "sum_b", ((CHUNK, f32), chunk), b_own, b_last)

time: 160 us -> 159 us (level)
    ppermute x2, waiting for transfers between devices: 25.9 us -> 8.33 us  [per_device(): far = lax.ppermute(far, 'slot', swaps[2])]
    ppermute x2, waiting for transfers between devices: 2.36 us -> 17.3 us  [per_device(): near = lax.ppermute(near, 'slot', swaps[1])]
    ppermute x2, starting transfers between devices: 11.2 us -> 17.7 us  [per_device(): far = lax.ppermute(far, 'slot', swaps[2])]
    ppermute x2, starting transfers between devices: 22.1 us -> 17.3 us  [per_device(): near = lax.ppermute(near, 'slot', swaps[1])]
    ppermute x1, waiting for transfers between devices: 0.01 us -> 2.37 us  [per_device(): b_last = lax.ppermute(b_next, 'grp', side_moves)]
    ppermute x2, starting transfers between devices: 14.4 us -> 12.6 us  [per_device(): mirror = lax.ppermute(mirror, 'slot', swaps[3])]
where the time goes in v9:
time: 159 us
  starting transfers between devices  80.6 us (51%)
  waiting for transfers between devices  54.3 us (34%)
  Pallas kernels  21 us (13%)
  local copies, waits for them, and re-layouts  2.08 us (1%)
    all_to_all x1, waiting for transfers between devices, per_device(): got = lax.all_to_all(sent, 'dp', split_axis=0, concat_axis=0, tiled=True)  20.9 us
    all_to_all x1, starting transfers between devices, per_device(): got = lax.all_to_all(sent, 'dp', split_axis=0, concat_axis=0, tiled=True)  19.8 us
    ppermute x2, starting transfers between devices, per_device(): far = lax.ppermute(far, 'slot', swaps[2])  17.7 us
    ppermute x2, waiting for transfers between devices, per_device(): near = lax.ppermute(near, 'slot', swaps[1])  17.3 us
    ppermute x2, starting transfers between devices, per_device(): near = lax.ppermute(near, 'slot', swaps[1])  17.3 us
    ppermute x2, starting transfers between devices, per_device(): mirror = lax.ppermute(mirror, 'slot', swaps[3])  12.6 us
    pallas_call x3, Pallas kernels, run_later_bags(): pl.pallas_call(later_bags_kernel, out_shape=jax.ShapeDtypeStruct((2, 2, *...  8.63 us
    ppermute x2, waiting for transfers between devices, per_device(): far = lax.ppermute(far, 'slot', swaps[2])  8.33 us
  transfers between devices with their start and end apart: 11, of which 6 were waited for; matrix products, arithmetic and copies ran while one was open for 0% of the time, Pallas kernels for 6%

profile of v9, /device:TPU:1, one launch (start us, length us, event | category | flops | bytes accessed | tf_op | source)
XLA Modules:
  0.0 158.6 jit_solution(17469758635093999567)
XLA Ops:
  0.0 2.7 %messages.1 = (bf16[560,128]{1,0:T(8,128)(2,1)}, bf16[560,128]{1,0:T(8,128)(2,1)}, bf16[560,128]{1,0:T(8,128)(2,1)}, bf16[560,128]{1,0:T(8,128)(2,1)}) custom-call(s32[1]{0:T(128)} %bitcast.12.place_ref.here_ref, bf16[4,256,128]{2,1,0:T(8,128)(2,1)} %bitcast.22, bf16[4,256,128]{2,1,0:T(8,128)(2,1)} %bitcast.23, s32[8,8,128]{2,1,0:T(8,128)} %bitcast.24, ...), custom_call_target="tpu_custom_call" | custom-call | flops 1000000 | bytes 2097152 | tf_op jit(solution)/shard_map/messages/pallas_call | solution.py:98
  2.7 11.5 %collective-permute-start = (bf16[560,128]{1,0:T(8,128)(2,1)}, bf16[560,128]{1,0:T(8,128)(2,1)S(1)}, u32[]{:S(2)}, u32[]{:S(2)}) collective-permute-start(bf16[560,128]{1,0:T(8,128)(2,1)} %get-tuple-element.29), channel_id=1, source_target_pairs={{0,4},{4,0},{8,12},{12,8},{1,5},{5,1},{9,13},{13,9},{2,6},{6,2},{1... | collective-permute-start | bytes 430088 | tf_op jit(solution)/shard_map/ppermute | solution.py:409
  14.1 10.6 %collective-permute-start.1 = (bf16[560,128]{1,0:T(8,128)(2,1)}, bf16[560,128]{1,0:T(8,128)(2,1)S(1)}, u32[]{:S(2)}, u32[]{:S(2)}) collective-permute-start(bf16[560,128]{1,0:T(8,128)(2,1)} %get-tuple-element.30), channel_id=1, source_target_pairs={{0,12},{4,8},{8,4},{12,0},{1,13},{5,9},{9,5},{13,1},{2,14},{6,10},... | collective-permute-start | bytes 430088 | tf_op jit(solution)/shard_map/ppermute | solution.py:410
  24.8 5.6 %collective-permute-start.2 = (bf16[560,128]{1,0:T(8,128)(2,1)}, bf16[560,128]{1,0:T(8,128)(2,1)S(1)}, u32[]{:S(2)}, u32[]{:S(2)}) collective-permute-start(bf16[560,128]{1,0:T(8,128)(2,1)} %get-tuple-element.31), channel_id=1, source_target_pairs={{0,8},{4,12},{8,0},{12,4},{1,9},{5,13},{9,1},{13,5},{2,10},{6,14},... | collective-permute-start | bytes 430088 | tf_op jit(solution)/shard_map/ppermute | solution.py:411
  30.5 1.2 copy-done
  32.1 8.3 %collective-permute-done.2.far_ref = bf16[560,128]{1,0:T(8,128)(2,1)S(1)} collective-permute-done((bf16[560,128]{1,0:T(8,128)(2,1)}, bf16[560,128]{1,0:T(8,128)(2,1)S(1)}, u32[]{:S(2)}, u32[]{:S(2)}) %collective-permute-start.2) | collective-permute-done | bytes 143392 | tf_op jit(solution)/shard_map/ppermute | solution.py:411
  41.1 4.7 %layers.1 = bf16[64,5,8,128]{3,2,1,0:T(8,128)(2,1)} custom-call(s32[1]{0:T(128)} %bitcast.12.place_ref.here_ref, bf16[560,128]{1,0:T(8,128)(2,1)S(1)} %copy-done.1, bf16[560,128]{1,0:T(8,128)(2,1)S(1)} %collective-permute-done.near_ref, bf16[560,128]{1,0:T(8,128)(2,1)S(1)} %collective-permute-done.1.mirror_ref, ...), custom_call_target="tpu_custom_call" | custom-call | flops 2000000000 | bytes 4194304 | tf_op jit(solution)/shard_map/layers/pallas_call | solution.py:225
  45.9 19.8 %all-to-all-start = ((bf16[64,5,8,128]{3,2,1,0:T(8,128)(2,1)}), bf16[64,5,8,128]{3,2,1,0:T(8,128)(2,1)S(1)}, u32[]{:S(2)}, u32[]{:S(2)}) async-start(bf16[64,5,8,128]{3,2,1,0:T(8,128)(2,1)} %layers.1), calls=%async_computation | async-start | bytes 1310720 | tf_op jit(solution)/shard_map/all_to_all | solution.py:415
  65.8 20.9 %all-to-all-done.got_ref = bf16[64,5,8,128]{3,2,1,0:T(8,128)(2,1)S(1)} async-done(((bf16[64,5,8,128]{3,2,1,0:T(8,128)(2,1)}), bf16[64,5,8,128]{3,2,1,0:T(8,128)(2,1)S(1)}, u32[]{:S(2)}, u32[]{:S(2)}) %all-to-all-start) | async-done | bytes 655392 | tf_op jit(solution)/shard_map/all_to_all | solution.py:415
  86.7 3.6 %first_bags.1 = (bf16[2,2,2,256,128]{4,3,2,1,0:T(8,128)(2,1)S(1)}, bf16[8,256,256]{2,1,0:T(8,128)(2,1)S(1)}, f32[8,8,256]{2,1,0:T(8,128)S(1)}, f32[8,8,256]{2,1,0:T(8,128)S(1)}) custom-call(s32[4]{0:T(128)S(1)} %pad_add_fusion.2.blocks_ref, bf16[64,5,8,128]{3,2,1,0:T(8,128)(2,1)S(1)} %all-to-all-done.got_ref), custom_call_target="tpu_custom_call" | custom-call | flops 200000000 | bytes 1048576 | tf_op jit(solution)/shard_map/first_bags/pallas_call | solution.py:317
  90.3 3.1 %collective-permute-start.3 = (bf16[2,2,2,256,128]{4,3,2,1,0:T(8,128)(2,1)S(1)}, bf16[2,2,2,256,128]{4,3,2,1,0:T(8,128)(2,1)S(1)}, u32[]{:S(2)}, u32[]{:S(2)}) collective-permute-start(bf16[2,2,2,256,128]{4,3,2,1,0:T(8,128)(2,1)S(1)} %get-tuple-element.37), channel_id=1, source_target_pairs={{0,1},{1,0},{2,3},{3,2},{4,5},{5,4},{6,7},{7,6},{8,9},{9,8},{10,11... | collective-permute-start | bytes 1572872 | tf_op jit(solution)/shard_map/ppermute | solution.py:428
  93.5 2.9 %b_sent.1 = bf16[2,2,2,256,128]{4,3,2,1,0:T(8,128)(2,1)S(1)} custom-call(s32[4]{0:T(128)S(1)} %pad_add_fusion.3.blocks_ref, bf16[8,256,256]{2,1,0:T(8,128)(2,1)S(1)} %get-tuple-element.34.grads_ref, f32[8,8,256]{2,1,0:T(8,128)S(1)} %get-tuple-element.35.high_ref, f32[8,8,256]{2,1,0:T(8,128)S(1)} %get-tuple-element.36.low_ref), custom_call_target="tpu_custom_call" | custom-call | flops 200000000 | bytes 1048576 | tf_op jit(solution)/shard_map/b_sent/pallas_call | solution.py:335
  96.4 3.7 %collective-permute-start.4 = (bf16[2,2,2,256,128]{4,3,2,1,0:T(8,128)(2,1)S(1)}, bf16[2,2,2,256,128]{4,3,2,1,0:T(8,128)(2,1)S(1)}, u32[]{:S(2)}, u32[]{:S(2)}) collective-permute-start(bf16[2,2,2,256,128]{4,3,2,1,0:T(8,128)(2,1)S(1)} %b_sent.1), channel_id=1, source_target_pairs={{0,3},{1,2},{2,1},{3,0},{4,7},{5,6},{6,5},{7,4},{8,11},{9,10},{10,... | collective-permute-start | bytes 1572872 | tf_op jit(solution)/shard_map/ppermute | solution.py:430
  100.3 2.9 %a_kept.1.kept_ref = bf16[2,2,2,256,128]{4,3,2,1,0:T(8,128)(2,1)S(1)} custom-call(s32[4]{0:T(128)S(1)} %pad_add_fusion.1.blocks_ref, bf16[8,256,256]{2,1,0:T(8,128)(2,1)S(1)} %get-tuple-element.34.grads_ref, f32[8,8,256]{2,1,0:T(8,128)S(1)} %get-tuple-element.35.high_ref, f32[8,8,256]{2,1,0:T(8,128)S(1)} %get-tuple-element.36.low_ref), custom_call_target="tpu_custom_call" | custom-call | flops 200000000 | bytes 1048576 | tf_op jit(solution)/shard_map/a_kept/pallas_call | solution.py:335
  103.2 2.2 %collective-permute-done.3.got_ref = bf16[2,2,2,256,128]{4,3,2,1,0:T(8,128)(2,1)S(1)} collective-permute-done((bf16[2,2,2,256,128]{4,3,2,1,0:T(8,128)(2,1)S(1)}, bf16[2,2,2,256,128]{4,3,2,1,0:T(8,128)(2,1)S(1)}, u32[]{:S(2)}, u32[]{:S(2)}) %collective-permute-start.3) | collective-permute-done | bytes 524320 | tf_op jit(solution)/shard_map/ppermute | solution.py:428
  105.5 4.4 %collective-permute-start.5 = (bf16[2,2,256,128]{3,2,1,0:T(8,128)(2,1)S(1)}, bf16[2,2,256,128]{3,2,1,0:T(8,128)(2,1)S(1)}, u32[]{:S(2)}, u32[]{:S(2)}) collective-permute-start(bf16[2,2,256,128]{3,2,1,0:T(8,128)(2,1)S(1)} %get-tuple-element.42), channel_id=1, source_target_pairs={{0,3},{1,2},{2,1},{3,0},{4,7},{5,6},{6,5},{7,4},{8,11},{9,10},{10,... | collective-permute-start | bytes 786440 | tf_op jit(solution)/shard_map/ppermute | solution.py:434
  109.9 2.9 %b_kept.1.kept_ref = bf16[2,2,2,256,128]{4,3,2,1,0:T(8,128)(2,1)S(1)} custom-call(s32[4]{0:T(128)S(1)} %pad_add_fusion.blocks_ref, bf16[8,256,256]{2,1,0:T(8,128)(2,1)S(1)} %get-tuple-element.34.grads_ref, f32[8,8,256]{2,1,0:T(8,128)S(1)} %get-tuple-element.35.high_ref, f32[8,8,256]{2,1,0:T(8,128)S(1)} %get-tuple-element.36.low_ref), custom_call_target="tpu_custom_call" | custom-call | flops 200000000 | bytes 1048576 | tf_op jit(solution)/shard_map/b_kept/pallas_call | solution.py:335
  112.9 1.9 %collective-permute-start.6 = (bf16[2,2,256,128]{3,2,1,0:T(8,128)(2,1)S(1)}, bf16[2,2,256,128]{3,2,1,0:T(8,128)(2,1)S(1)}, u32[]{:S(2)}, u32[]{:S(2)}) collective-permute-start(bf16[2,2,256,128]{3,2,1,0:T(8,128)(2,1)S(1)} %get-tuple-element.46), channel_id=1, source_target_pairs={{0,1},{1,0},{2,3},{3,2},{4,5},{5,4},{6,7},{7,6},{8,9},{9,8},{10,11... | collective-permute-start | bytes 786440 | tf_op jit(solution)/shard_map/ppermute | solution.py:438
  114.8 3.1 %collective-permute-done.5.got_ref = bf16[2,2,256,128]{3,2,1,0:T(8,128)(2,1)S(1)} collective-permute-done((bf16[2,2,256,128]{3,2,1,0:T(8,128)(2,1)S(1)}, bf16[2,2,256,128]{3,2,1,0:T(8,128)(2,1)S(1)}, u32[]{:S(2)}, u32[]{:S(2)}) %collective-permute-start.5) | collective-permute-done | bytes 262176 | tf_op jit(solution)/shard_map/ppermute | solution.py:434
  118.0 2.4 %collective-permute-done.6.got_ref = bf16[2,2,256,128]{3,2,1,0:T(8,128)(2,1)S(1)} collective-permute-done((bf16[2,2,256,128]{3,2,1,0:T(8,128)(2,1)S(1)}, bf16[2,2,256,128]{3,2,1,0:T(8,128)(2,1)S(1)}, u32[]{:S(2)}, u32[]{:S(2)}) %collective-permute-start.6) | collective-permute-done | bytes 262176 | tf_op jit(solution)/shard_map/ppermute | solution.py:438
  120.5 12.2 %collective-permute-start.9 = (bf16[2,256,128]{2,1,0:T(8,128)(2,1)S(1)}, bf16[2,256,128]{2,1,0:T(8,128)(2,1)S(1)}, u32[]{:S(2)}, u32[]{:S(2)}) collective-permute-start(bf16[2,256,128]{2,1,0:T(8,128)(2,1)S(1)} %get-tuple-element.50), channel_id=1, source_target_pairs={{0,8},{4,12},{8,0},{12,4},{1,9},{5,13},{9,1},{13,5},{2,10},{6,14},... | collective-permute-start | bytes 393224 | tf_op jit(solution)/shard_map/ppermute | solution.py:445
  132.6 5.9 %collective-permute-start.7 = (bf16[2,256,128]{2,1,0:T(8,128)(2,1)S(1)}, bf16[2,256,128]{2,1,0:T(8,128)(2,1)S(1)}, u32[]{:S(2)}, u32[]{:S(2)}) collective-permute-start(bf16[2,256,128]{2,1,0:T(8,128)(2,1)S(1)} %get-tuple-element.48), channel_id=1, source_target_pairs={{0,4},{4,0},{8,12},{12,8},{1,5},{5,1},{9,13},{13,9},{2,6},{6,2},{1... | collective-permute-start | bytes 393224 | tf_op jit(solution)/shard_map/ppermute | solution.py:442
  138.5 1.9 %collective-permute-start.8 = (bf16[2,256,128]{2,1,0:T(8,128)(2,1)S(1)}, bf16[2,256,128]{2,1,0:T(8,128)(2,1)S(1)}, u32[]{:S(2)}, u32[]{:S(2)}) collective-permute-start(bf16[2,256,128]{2,1,0:T(8,128)(2,1)S(1)} %get-tuple-element.49), channel_id=1, source_target_pairs={{0,12},{4,8},{8,4},{12,0},{1,13},{5,9},{9,5},{13,1},{2,14},{6,10},... | collective-permute-start | bytes 393224 | tf_op jit(solution)/shard_map/ppermute | solution.py:443
  140.5 17.3 %collective-permute-done.7.near_ref = bf16[2,256,128]{2,1,0:T(8,128)(2,1)S(1)} collective-permute-done((bf16[2,256,128]{2,1,0:T(8,128)(2,1)S(1)}, bf16[2,256,128]{2,1,0:T(8,128)(2,1)S(1)}, u32[]{:S(2)}, u32[]{:S(2)}) %collective-permute-start.7) | collective-permute-done | bytes 131104 | tf_op jit(solution)/shard_map/ppermute | solution.py:442
  (25 shorter events, 2.6 us)
Async XLA Ops:
  0.0 30.4 %copy-start.4 = (bf16[2,512,32]{1,2,0:T(8,128)(2,1)S(1)}, bf16[2,512,32]{1,2,0:T(8,128)(2,1)}, u32[]{:S(2)}) copy-start(bf16[2,512,32]{1,2,0:T(8,128)(2,1)} %param.13) | copy-start | bytes 196612
  2.7 29.4 %collective-permute-start = (bf16[560,128]{1,0:T(8,128)(2,1)}, bf16[560,128]{1,0:T(8,128)(2,1)S(1)}, u32[]{:S(2)}, u32[]{:S(2)}) collective-permute-start(bf16[560,128]{1,0:T(8,128)(2,1)} %get-tuple-element.29), channel_id=1, source_target_pairs={{0,4},{4,0},{8,12},{12,8},{1,5},{5,1},{9,13},{13,9},{2,6},{6,2},{1... | collective-permute-start | bytes 430088 | tf_op jit(solution)/shard_map/ppermute | solution.py:409
  14.1 18.0 %collective-permute-start.1 = (bf16[560,128]{1,0:T(8,128)(2,1)}, bf16[560,128]{1,0:T(8,128)(2,1)S(1)}, u32[]{:S(2)}, u32[]{:S(2)}) collective-permute-start(bf16[560,128]{1,0:T(8,128)(2,1)} %get-tuple-element.30), channel_id=1, source_target_pairs={{0,12},{4,8},{8,4},{12,0},{1,13},{5,9},{9,5},{13,1},{2,14},{6,10},... | collective-permute-start | bytes 430088 | tf_op jit(solution)/shard_map/ppermute | solution.py:410
  24.8 15.7 %collective-permute-start.2 = (bf16[560,128]{1,0:T(8,128)(2,1)}, bf16[560,128]{1,0:T(8,128)(2,1)S(1)}, u32[]{:S(2)}, u32[]{:S(2)}) collective-permute-start(bf16[560,128]{1,0:T(8,128)(2,1)} %get-tuple-element.31), channel_id=1, source_target_pairs={{0,8},{4,12},{8,0},{12,4},{1,9},{5,13},{9,1},{13,5},{2,10},{6,14},... | collective-permute-start | bytes 430088 | tf_op jit(solution)/shard_map/ppermute | solution.py:411
  30.5 1.2 copy-start
  31.8 8.7 %copy-start.1 = (bf16[560,128]{1,0:T(8,128)(2,1)S(1)}, bf16[560,128]{1,0:T(8,128)(2,1)}, u32[]{:S(2)}) copy-start(bf16[560,128]{1,0:T(8,128)(2,1)} %get-tuple-element.28.own_ref) | copy-start | bytes 430084
  31.8 8.7 %copy-start.2 = (bf16[2,32,128]{2,1,0:T(8,128)(2,1)S(1)}, bf16[2,32,128]{2,1,0:T(8,128)(2,1)}, u32[]{:S(2)}) copy-start(bf16[2,32,128]{2,1,0:T(8,128)(2,1)} %output_ref.1) | copy-start | bytes 49156
  40.5 0.7 copy-start.3
  45.9 40.9 %all-to-all-start = ((bf16[64,5,8,128]{3,2,1,0:T(8,128)(2,1)}), bf16[64,5,8,128]{3,2,1,0:T(8,128)(2,1)S(1)}, u32[]{:S(2)}, u32[]{:S(2)}) async-start(bf16[64,5,8,128]{3,2,1,0:T(8,128)(2,1)} %layers.1), calls=%async_computation | async-start | bytes 1310720 | tf_op jit(solution)/shard_map/all_to_all | solution.py:415
  90.3 15.0 %collective-permute-start.3 = (bf16[2,2,2,256,128]{4,3,2,1,0:T(8,128)(2,1)S(1)}, bf16[2,2,2,256,128]{4,3,2,1,0:T(8,128)(2,1)S(1)}, u32[]{:S(2)}, u32[]{:S(2)}) collective-permute-start(bf16[2,2,2,256,128]{4,3,2,1,0:T(8,128)(2,1)S(1)} %get-tuple-element.37), channel_id=1, source_target_pairs={{0,1},{1,0},{2,3},{3,2},{4,5},{5,4},{6,7},{7,6},{8,9},{9,8},{10,11... | collective-permute-start | bytes 1572872 | tf_op jit(solution)/shard_map/ppermute | solution.py:428
  96.4 16.3 %collective-permute-start.4 = (bf16[2,2,2,256,128]{4,3,2,1,0:T(8,128)(2,1)S(1)}, bf16[2,2,2,256,128]{4,3,2,1,0:T(8,128)(2,1)S(1)}, u32[]{:S(2)}, u32[]{:S(2)}) collective-permute-start(bf16[2,2,2,256,128]{4,3,2,1,0:T(8,128)(2,1)S(1)} %b_sent.1), channel_id=1, source_target_pairs={{0,3},{1,2},{2,1},{3,0},{4,7},{5,6},{6,5},{7,4},{8,11},{9,10},{10,... | collective-permute-start | bytes 1572872 | tf_op jit(solution)/shard_map/ppermute | solution.py:430
  105.5 12.5 %collective-permute-start.5 = (bf16[2,2,256,128]{3,2,1,0:T(8,128)(2,1)S(1)}, bf16[2,2,256,128]{3,2,1,0:T(8,128)(2,1)S(1)}, u32[]{:S(2)}, u32[]{:S(2)}) collective-permute-start(bf16[2,2,256,128]{3,2,1,0:T(8,128)(2,1)S(1)} %get-tuple-element.42), channel_id=1, source_target_pairs={{0,3},{1,2},{2,1},{3,0},{4,7},{5,6},{6,5},{7,4},{8,11},{9,10},{10,... | collective-permute-start | bytes 786440 | tf_op jit(solution)/shard_map/ppermute | solution.py:434
  112.9 7.5 %collective-permute-start.6 = (bf16[2,2,256,128]{3,2,1,0:T(8,128)(2,1)S(1)}, bf16[2,2,256,128]{3,2,1,0:T(8,128)(2,1)S(1)}, u32[]{:S(2)}, u32[]{:S(2)}) collective-permute-start(bf16[2,2,256,128]{3,2,1,0:T(8,128)(2,1)S(1)} %get-tuple-element.46), channel_id=1, source_target_pairs={{0,1},{1,0},{2,3},{3,2},{4,5},{5,4},{6,7},{7,6},{8,9},{9,8},{10,11... | collective-permute-start | bytes 786440 | tf_op jit(solution)/shard_map/ppermute | solution.py:438
  120.5 20.0 %collective-permute-start.9 = (bf16[2,256,128]{2,1,0:T(8,128)(2,1)S(1)}, bf16[2,256,128]{2,1,0:T(8,128)(2,1)S(1)}, u32[]{:S(2)}, u32[]{:S(2)}) collective-permute-start(bf16[2,256,128]{2,1,0:T(8,128)(2,1)S(1)} %get-tuple-element.50), channel_id=1, source_target_pairs={{0,8},{4,12},{8,0},{12,4},{1,9},{5,13},{9,1},{13,5},{2,10},{6,14},... | collective-permute-start | bytes 393224 | tf_op jit(solution)/shard_map/ppermute | solution.py:445
  132.6 25.2 %collective-permute-start.7 = (bf16[2,256,128]{2,1,0:T(8,128)(2,1)S(1)}, bf16[2,256,128]{2,1,0:T(8,128)(2,1)S(1)}, u32[]{:S(2)}, u32[]{:S(2)}) collective-permute-start(bf16[2,256,128]{2,1,0:T(8,128)(2,1)S(1)} %get-tuple-element.48), channel_id=1, source_target_pairs={{0,4},{4,0},{8,12},{12,8},{1,5},{5,1},{9,13},{13,9},{2,6},{6,2},{1... | collective-permute-start | bytes 393224 | tf_op jit(solution)/shard_map/ppermute | solution.py:442
  138.5 19.3 %collective-permute-start.8 = (bf16[2,256,128]{2,1,0:T(8,128)(2,1)S(1)}, bf16[2,256,128]{2,1,0:T(8,128)(2,1)S(1)}, u32[]{:S(2)}, u32[]{:S(2)}) collective-permute-start(bf16[2,256,128]{2,1,0:T(8,128)(2,1)S(1)} %get-tuple-element.49), channel_id=1, source_target_pairs={{0,12},{4,8},{8,4},{12,0},{1,13},{5,9},{9,5},{13,1},{2,14},{6,10},... | collective-permute-start | bytes 393224 | tf_op jit(solution)/shard_map/ppermute | solution.py:443
